TPU v7x, 32 devices: a whole 2x2x4 slice. The times are simulated.
32 devices in a mesh: parts: 2 (over y), space: 4 (over z), dp: 2 (over x), chan: 2 (over core).
Axes of the slice: x: 2, y: 2, z: 4, core: 2. Of those that a mesh axis runs over, the one named last changes fastest.
Arguments:
- grad_out: bfloat16 [4, 4, 16, 16, 1024], P(('parts', 'dp'), 'space', None, None, 'chan'), parts along dimension 0, may hold values from -6 to 6
- saved_spectrum: bfloat16 [2, 4, 4, 16, 16, 1024], P(None, ('parts', 'dp'), None, 'space', None, 'chan'), parts along dimension 1, may hold values from -6 to 6
- w_first: bfloat16 [8, 2, 128, 128], P('chan'), may hold values from -0.375 to 0.375
- bias_first: bfloat16 [2, 1024], P(None, 'chan'), may hold values from -3 to 3
- w_second: bfloat16 [8, 2, 128, 128], P('chan'), may hold values from -0.375 to 0.375
Outputs:
- grad_in: bfloat16 [4, 4, 16, 16, 1024], P(('parts', 'dp'), 'space', None, None, 'chan'), parts along dimension 0
- grad_first: float32 [16, 2, 128, 128], P(('parts', 'chan'), None, ('space', 'dp')), parts along dimension 0
- grad_second: float32 [16, 2, 128, 128], P(('parts', 'chan'), None, ('space', 'dp')), parts along dimension 0
There are 2 independent parts, one for each index of `parts`. A program takes and returns all parts, laid end to end along the dimension named above; an argument that names none is the same for every part. Nothing has to cross between parts.
All inputs are finite; a program needn't handle non-finite values.
Results may differ from a plain program's by a relative error of at most 0.013.
Values may be sent and summed in bfloat16 or wider, within the bound.
No kernel may reach another device: no remote copies, remote signals or barrier semaphores. Data moves between devices by JAX's collectives and lax.ppermute only.
A program may use at most 64 MiB of HBM per device.

v0:
```python
import math

import jax
import jax.numpy as jnp
from jax import lax
from jax.sharding import PartitionSpec as P

inv_root_two = 1.0 / math.sqrt(2.0)
inv_root_tau = 1.0 / math.sqrt(2.0 * math.pi)
highest = lax.Precision.HIGHEST


def gelu_value(values):
    return values * 0.5 * (1.0 + lax.erf(values * inv_root_two))


def gelu_slope(values):
    return (
        0.5 * (1.0 + lax.erf(values * inv_root_two))
        + values * jnp.exp(-0.5 * values * values) * inv_root_tau
    )


def tables(length, orient):
    position = jnp.arange(length, dtype=jnp.int32)
    phases = position[:, None] * position[None, :] % length
    angles = phases.astype(jnp.float32) * (2.0 * math.pi / length)
    return (jnp.cos(angles), orient * jnp.sin(angles))


def complex_table(length, orient):
    cosine, sine = tables(length, orient)
    return jnp.stack([jnp.stack([cosine, -sine]), jnp.stack([sine, cosine])])


def apply_table(pattern, table, values):
    return jnp.einsum(pattern, table, values, precision=highest, preferred_element_type=jnp.float32)


def forward_product(left, right):
    return jnp.einsum("rbc,bcd->rbd", left, right, preferred_element_type=jnp.float32)


def adjoint_product(left, right):
    return jnp.einsum("rbd,bcd->rbc", left, right, preferred_element_type=jnp.float32)


def weight_product(left, right):
    return jnp.einsum("rbc,rbd->bcd", left, right, preferred_element_type=jnp.float32)


def body(grad_out, saved_spectrum, w_first, bias_first, w_second):
    planes = grad_out.shape[1]
    length_y = grad_out.shape[2]
    length_z = grad_out.shape[3]
    count_local = w_first.shape[0]
    block = w_first.shape[2]
    length_x = planes * lax.axis_size("space")
    cells = length_x * length_y * length_z
    norm_scale = 1.0 / math.sqrt(cells)
    grad_scale = 1.0 / math.sqrt(cells * grad_out.shape[0] * lax.axis_size("dp"))
    source = grad_out.astype(jnp.float32)
    forward_z = jnp.stack(tables(length_z, -1.0))
    partial_spec = apply_table("pkz,sxyzw->psxykw", forward_z, source)
    partial_spec = apply_table("pqky,qsxyzw->psxkzw", complex_table(length_y, -1.0), partial_spec)
    packed = partial_spec.astype(jnp.bfloat16)
    pencil = lax.all_to_all(packed, "space", split_axis=3, concat_axis=2, tiled=True).astype(
        jnp.float32
    )
    spectrum = apply_table("pqkx,qsxyzw->pskyzw", complex_table(length_x, -1.0), pencil)
    grad_pair = (spectrum * norm_scale).astype(jnp.bfloat16)
    pencil_shape = grad_pair.shape[1:]

    def blocks(values):
        return values.reshape(-1, count_local, block)

    grad_real = blocks(grad_pair[0])
    grad_imag = blocks(grad_pair[1])
    saved_real = blocks(saved_spectrum[0])
    saved_imag = blocks(saved_spectrum[1])
    first_real = w_first[:, 0]
    first_imag = w_first[:, 1]
    second_real = w_second[:, 0]
    second_imag = w_second[:, 1]
    bias_real = bias_first[0].astype(jnp.float32).reshape(count_local, block)
    bias_imag = bias_first[1].astype(jnp.float32).reshape(count_local, block)
    pre_real = (
        forward_product(saved_real, first_real)
        - forward_product(saved_imag, first_imag)
        + bias_real
    )
    pre_imag = (
        forward_product(saved_real, first_imag)
        + forward_product(saved_imag, first_real)
        + bias_imag
    )
    act_real = gelu_value(pre_real).astype(jnp.bfloat16)
    act_imag = gelu_value(pre_imag).astype(jnp.bfloat16)
    back_real = adjoint_product(grad_real, second_real) + adjoint_product(grad_imag, second_imag)
    back_imag = adjoint_product(grad_imag, second_real) - adjoint_product(grad_real, second_imag)
    slope_real = (back_real * gelu_slope(pre_real)).astype(jnp.bfloat16)
    slope_imag = (back_imag * gelu_slope(pre_imag)).astype(jnp.bfloat16)
    input_real = adjoint_product(slope_real, first_real) + adjoint_product(slope_imag, first_imag)
    input_imag = adjoint_product(slope_imag, first_real) - adjoint_product(slope_real, first_imag)
    second_term = (
        jnp.stack(
            [
                weight_product(act_real, grad_real) + weight_product(act_imag, grad_imag),
                weight_product(act_real, grad_imag) - weight_product(act_imag, grad_real),
            ],
            axis=1,
        )
        * grad_scale
    )
    first_term = (
        jnp.stack(
            [
                weight_product(saved_real, slope_real) + weight_product(saved_imag, slope_imag),
                weight_product(saved_real, slope_imag) - weight_product(saved_imag, slope_real),
            ],
            axis=1,
        )
        * grad_scale
    )
    input_pair = jnp.stack([input_real.reshape(pencil_shape), input_imag.reshape(pencil_shape)])
    returned = apply_table("pqkx,qsxyzw->pskyzw", complex_table(length_x, 1.0), input_pair).astype(
        jnp.bfloat16
    )
    planes_back = lax.all_to_all(returned, "space", split_axis=2, concat_axis=3, tiled=True).astype(
        jnp.float32
    )
    planes_back = apply_table("pqky,qsxyzw->psxkzw", complex_table(length_y, 1.0), planes_back)
    inverse_cos, inverse_sin = tables(length_z, 1.0)
    inverse_z = jnp.stack([inverse_cos, -inverse_sin])
    field = apply_table("qkz,qsxyzw->sxykw", inverse_z, planes_back)
    grad_in = (field * norm_scale).astype(jnp.bfloat16)
    space_first, space_second = (
        lax.psum_scatter(
            first_term.astype(jnp.bfloat16), "space", scatter_dimension=2, tiled=True
        ).astype(jnp.float32),
        lax.psum_scatter(
            second_term.astype(jnp.bfloat16), "space", scatter_dimension=2, tiled=True
        ).astype(jnp.float32),
    )
    grad_first, grad_second = (
        lax.psum_scatter(
            space_first.astype(jnp.bfloat16), "dp", scatter_dimension=2, tiled=True
        ).astype(jnp.float32),
        lax.psum_scatter(
            space_second.astype(jnp.bfloat16), "dp", scatter_dimension=2, tiled=True
        ).astype(jnp.float32),
    )
    return (grad_in, grad_first, grad_second)


def solution(mesh):
    in_specs = (
        P(("parts", "dp"), "space", None, None, "chan"),
        P(None, ("parts", "dp"), None, "space", None, "chan"),
        P("chan", None, None, None),
        P(None, "chan"),
        P("chan", None, None, None),
    )
    out_specs = (
        P(("parts", "dp"), "space", None, None, "chan"),
        P(("parts", "chan"), None, ("space", "dp"), None),
        P(("parts", "chan"), None, ("space", "dp"), None),
    )
    return jax.shard_map(body, mesh=mesh, in_specs=in_specs, out_specs=out_specs, check_vma=False)
```

profile of v0, /device:TPU:0, one launch (start us, length us, event | category | flops | bytes accessed | tf_op | source)
XLA Modules:
  0.0 124.7 jit_solution(18170415602737115705)
XLA Ops:
  7.4 0.7 copy-done
  8.7 1.7 %fusion.6 = bf16[2,1,1,16,16,512]{5,3,0,4,2,1:T(8,128)(2,1)S(1)} fusion(f32[2,16,16,512,1]{3,2,1,0,4:T(8,128)S(1)} %convolution_bitcast_fusion.4, f32[1,2,16,16]{3,2,1,0:T(8,128)S(1)} %get-tuple-element.26, f32[1,2,16,16]{3,2,1,0:T(8,128)S(1)} %get-tuple-element.25), kind=kOutput, calls=%fused_computation.11 | convolution fusion | flops 100926464 | bytes 1576960 | tf_op jit(solution)/shard_map/pqky,qsxyzw->psxkzw/dot_general | solution.py:37
  10.4 1.4 %copy.147 = bf16[2,1,1,16,16,512]{5,0,4,2,1,3:T(2,128)(2,1)} copy(bf16[2,1,1,16,16,512]{5,3,0,4,2,1:T(8,128)(2,1)S(1)} %fusion.6) | data formatting | bytes 1048576 | tf_op jit(solution)/shard_map/convert_element_type | solution.py:66
  11.7 6.5 %all-to-all-start = ((bf16[2,1,1,16,16,512]{5,0,4,2,1,3:T(2,128)(2,1)}), bf16[2,1,1,16,16,512]{5,0,4,2,1,3:T(2,128)(2,1)S(1)}, u32[]{:S(2)}, u32[]{:S(2)}) async-start(bf16[2,1,1,16,16,512]{5,0,4,2,1,3:T(2,128)(2,1)} %copy.147), calls=%async_computation | async-start | bytes 1048576 | tf_op jit(solution)/shard_map/all_to_all | solution.py:67
  19.9 1.1 multiply_convert_fusion.1
  21.0 1.1 multiply_convert_fusion
  22.1 10.6 %all-to-all-done = bf16[2,1,1,16,16,512]{5,0,4,2,1,3:T(2,128)(2,1)S(1)} async-done(((bf16[2,1,1,16,16,512]{5,0,4,2,1,3:T(2,128)(2,1)}), bf16[2,1,1,16,16,512]{5,0,4,2,1,3:T(2,128)(2,1)S(1)}, u32[]{:S(2)}, u32[]{:S(2)}) %all-to-all-start) | async-done | bytes 524320 | tf_op jit(solution)/shard_map/all_to_all | solution.py:67
  32.7 1.4 %fusion.4 = bf16[2,1,4,4,16,512]{5,2,0,4,3,1:T(4,128)(2,1)S(1)} fusion(bf16[2,4,4,16,512,1]{4,0,3,2,1,5:T(2,128)(2,1)S(1)} %bitcast.225, f32[1,2,4,4]{3,2,1,0:T(4,128)S(1)} %get-tuple-element.29, f32[1,2,4,4]{3,2,1,0:T(4,128)S(1)} %get-tuple-element.30), kind=kOutput, calls=%fused_computation.9 | convolution fusion | flops 25690176 | bytes 1048832 | tf_op jit(solution)/shard_map/pqkx,qsxyzw->pskyzw/dot_general | solution.py:37
  35.0 0.7 copy-done.4
  36.2 0.8 copy-done.3
  38.5 0.9 copy.201
  39.4 1.4 %fusion.19 = bf16[256,4,128]{2,0,1:T(8,128)(2,1)S(1)} fusion(f32[4,256,128]{2,1,0:T(8,128)S(1)} %fusion.58, f32[256,4,128]{2,0,1:T(8,128)} %get-tuple-element.36, bf16[256,4,128]{2,1,0:T(4,128)(2,1)S(1)} %reshape_squeeze.12, bf16[4,2,128,128]{3,2,1,0:T(8,128)(2,1)S(1)} %copy-done.5), kind=kOutput, calls=%fused_computation.31 | convolution fusion | flops 34996224 | bytes 1703936 | tf_op jit(solution)/shard_map/rbd,bcd->rbc/dot_general | solution.py:45
  41.7 0.9 copy.188
  45.2 2.0 %fusion.5 = bf16[2,1,4,4,16,512]{5,2,0,4,3,1:T(4,128)(2,1)S(1)} fusion(f32[1,1,4,4,16,512]{5,2,0,4,3,1:T(4,128)S(1)} %copy.175, f32[1,1,4,4,16,512]{5,2,0,4,3,1:T(4,128)S(1)} %copy.174, f32[1,2,4,4]{3,2,1,0:T(4,128)S(1)} %get-tuple-element.28, f32[1,2,4,4]{3,2,1,0:T(4,128)S(1)} %get-tuple-element.27), kind=kOutput, calls=%fused_computation.10 | convolution fusion | flops 25690176 | bytes 1573120 | tf_op jit(solution)/shard_map/pqkx,qsxyzw->pskyzw/dot_general | solution.py:37
  47.2 1.3 %copy.176 = bf16[2,1,4,4,16,512]{5,0,4,3,1,2:T(2,128)(2,1)} copy(bf16[2,1,4,4,16,512]{5,2,0,4,3,1:T(4,128)(2,1)S(1)} %fusion.5) | data formatting | bytes 1048576 | tf_op jit(solution)/shard_map/convert_element_type | solution.py:126
  48.4 3.5 %all-to-all-start.1 = ((bf16[2,1,4,4,16,512]{5,0,4,3,1,2:T(2,128)(2,1)}), bf16[2,1,4,4,16,512]{5,0,4,3,1,2:T(2,128)(2,1)S(1)}, u32[]{:S(2)}, u32[]{:S(2)}) async-start(bf16[2,1,4,4,16,512]{5,0,4,3,1,2:T(2,128)(2,1)} %copy.176), calls=%async_computation.1 | async-start | bytes 1048576 | tf_op jit(solution)/shard_map/all_to_all | solution.py:129
  52.2 0.6 copy-done.9
  54.1 34.0 %all-reduce.9.cloned.1.call-done = (bf16[4,2,128,128]{3,0,1,2:T(4,128)(2,1)}, bf16[4,2,128,128]{3,0,1,2:T(4,128)(2,1)}) async-done(((bf16[4,2,128,128]{3,0,1,2:T(4,128)(2,1)}, bf16[4,2,128,128]{3,0,1,2:T(4,128)(2,1)}), (bf16[4,2,128,128]{3,0,1,2:T(4,128)(2,1)}, bf16[4,2,128,128]{3,0,1,2:T(4,128)(2,1)})) %all-reduce.9.cloned.1.call-update) | async-done | bytes 524304
  88.1 1.5 %constant_dynamic-slice_fusion = bf16[4,2,32,128]{3,0,1,2:T(4,128)(2,1)} fusion(bf16[4,2,128,128]{3,0,1,2:T(4,128)(2,1)} %get-tuple-element.16, u32[]{:T(128)S(6)} %multiply.1), kind=kLoop, calls=%fused_computation.174 | loop fusion | bytes 131076
  89.6 1.5 %constant_dynamic-slice_fusion.1 = bf16[4,2,32,128]{3,0,1,2:T(4,128)(2,1)} fusion(bf16[4,2,128,128]{3,0,1,2:T(4,128)(2,1)} %get-tuple-element.15, u32[]{:T(128)S(6)} %multiply.1), kind=kLoop, calls=%fused_computation.175 | loop fusion | bytes 131076
  93.0 19.8 %all-reduce.11.cloned.1.call-done = (bf16[4,2,32,128]{3,0,1,2:T(4,128)(2,1)}, bf16[4,2,32,128]{3,0,1,2:T(4,128)(2,1)}) async-done(((bf16[4,2,32,128]{3,0,1,2:T(4,128)(2,1)}, bf16[4,2,32,128]{3,0,1,2:T(4,128)(2,1)}), (bf16[4,2,32,128]{3,0,1,2:T(4,128)(2,1)}, bf16[4,2,32,128]{3,0,1,2:T(4,128)(2,1)})) %all-reduce.11.cloned.1.call-update) | async-done | bytes 131088
  112.8 0.8 dynamic-slice_convert_fusion
  115.0 0.8 convolution_bitcast_fusion
  115.8 2.0 %fusion.25 = bf16[1,1,16,16,512]{4,3,2,1,0:T(8,128)(2,1)} fusion(f32[2,16,16,512]{3,1,0,2:T(8,128)S(1)} %convolution_bitcast_fusion, f32[1,16,16]{2,1,0:T(8,128)S(1)} %get-tuple-element.38, f32[1,16,16]{2,1,0:T(8,128)S(1)} %get-tuple-element.40), kind=kOutput, calls=%fused_computation.41 | convolution fusion | flops 50594304 | bytes 1312768 | tf_op jit(solution)/shard_map/qkz,qsxyzw->sxykw/dot_general | solution.py:37
  (69 shorter events, 12.3 us)
Async XLA Ops:
  7.2 1.0 copy-start
  11.7 6.6 %copy-start.2 = (bf16[2,1,4,4,16,512]{5,4,3,2,1,0:T(8,128)(2,1)S(1)}, bf16[2,1,4,4,16,512]{5,4,3,2,1,0:T(8,128)(2,1)}, u32[]{:S(2)}) copy-start(bf16[2,1,4,4,16,512]{5,4,3,2,1,0:T(8,128)(2,1)} %param.6) | copy-start | bytes 1572868
  11.7 20.9 %all-to-all-start = ((bf16[2,1,1,16,16,512]{5,0,4,2,1,3:T(2,128)(2,1)}), bf16[2,1,1,16,16,512]{5,0,4,2,1,3:T(2,128)(2,1)S(1)}, u32[]{:S(2)}, u32[]{:S(2)}) async-start(bf16[2,1,1,16,16,512]{5,0,4,2,1,3:T(2,128)(2,1)} %copy.147), calls=%async_computation | async-start | bytes 1048576 | tf_op jit(solution)/shard_map/all_to_all | solution.py:67
  18.2 69.9 %all-reduce.9.cloned.1.call-start = ((), (), s32[]{:S(2)}) async-start(), calls=%async_computation.2 | async-start | bytes 1048576
  18.4 0.7 copy-start.7
  18.4 1.0 copy-start.1
  34.8 1.0 copy-start.4
  36.0 1.0 copy-start.3
  38.5 1.0 copy-start.5
  48.4 66.6 %all-to-all-start.1 = ((bf16[2,1,4,4,16,512]{5,0,4,3,1,2:T(2,128)(2,1)}), bf16[2,1,4,4,16,512]{5,0,4,3,1,2:T(2,128)(2,1)S(1)}, u32[]{:S(2)}, u32[]{:S(2)}) async-start(bf16[2,1,4,4,16,512]{5,0,4,3,1,2:T(2,128)(2,1)} %copy.176), calls=%async_computation.1 | async-start | bytes 1048576 | tf_op jit(solution)/shard_map/all_to_all | solution.py:129
  51.9 60.9 %all-reduce.11.cloned.1.call-start = ((), (), s32[]{:S(2)}) async-start(), calls=%async_computation.3 | async-start | bytes 262144
  52.2 0.7 copy-start.9
  91.1 0.7 copy-start.8
  113.6 0.8 copy-start.6
Sparse Core Ops, SparseCore 0:
  43.0 45.0 all-reduce.8
  91.2 21.5 all-reduce.10
where the time goes:
time: 125 us
  waiting for transfers between devices  64.5 us (52%)
  local copies, waits for them, and re-layouts  16.8 us (13%)
  matrix products  16.2 us (13%)
  between operations  15.7 us (13%)
  starting transfers between devices  10.2 us (8%)
  other arithmetic  1.26 us (1%)
    unnamed x4, waiting for transfers between devices  53.9 us
    all_to_all x1, waiting for transfers between devices, body(): lax.all_to_all(packed, 'space', split_axis=3, concat_axis=2, tiled=True)  10.6 us
    unnamed x26, local copies, waits for them, and re-layouts  10.1 us
    dot_general x6, matrix products, apply_table(): jnp.einsum(pattern, table, values, precision=highest, preferred_element_t...  8.34 us
    all_to_all x1, starting transfers between devices, body(): lax.all_to_all(packed, 'space', split_axis=3, concat_axis=2, tiled=True)  6.45 us
    all_to_all x1, starting transfers between devices, body(): lax.all_to_all(returned, 'space', split_axis=2, concat_axis=3, tiled=True)  3.47 us
    dot_general x8, matrix products, adjoint_product(): jnp.einsum('rbd,bcd->rbc', left, right, preferred_element_type=jnp.float32)  3.08 us
    dot_general x4, matrix products, forward_product(): jnp.einsum('rbc,bcd->rbd', left, right, preferred_element_type=jnp.float32)  2.59 us
  transfers between devices with their start and end apart: 4, of which 3 were waited for; matrix products, arithmetic and copies ran while one was open for 12% of the time, Pallas kernels for 0%

commit v1 on v0

v1 whole, which is shorter than its diff:
```python
import functools
import math

import jax
import jax.numpy as jnp
import numpy as np
from jax import lax
from jax.experimental import pallas as pl
from jax.experimental.pallas import tpu as pltpu
from jax.sharding import PartitionSpec as P

inv_root_two = 1.0 / math.sqrt(2.0)
inv_root_tau = 1.0 / math.sqrt(2.0 * math.pi)
f32 = jnp.float32
bf16 = jnp.bfloat16
vmem_bytes = 24 * 1024 * 1024


def phase_table(length_y, length_z):
    whole = math.lcm(length_y, length_z)
    y = np.arange(length_y)
    z = np.arange(length_z)
    turns = (
        (y[:, None, None, None] * y[None, None, :, None]) * (whole // length_y)
        + (z[None, :, None, None] * z[None, None, None, :]) * (whole // length_z)
    ) % whole
    cells = length_y * length_z
    return turns.reshape(cells, cells) * (2.0 * math.pi / whole)


def round_scaled(table):
    levels = np.unique(np.abs(table).round(12))
    factors = np.linspace(1.0, 2.0, 2049)[:-1]
    scaled = factors[:, None] * levels
    error = np.abs(scaled.astype(bf16).astype(np.float64) / factors[:, None] - levels).max(axis=1)
    factor = float(factors[np.argmin(error)])
    return (table * factor).astype(bf16), factor


def transform_tables(length_y, length_z, count):
    angles = phase_table(length_y, length_z)
    cells = length_y * length_z
    rows = cells // count
    both = np.stack([np.cos(angles), -np.sin(angles)]).reshape(2, count, rows, cells)
    forward, factor = round_scaled(both.transpose(1, 0, 2, 3).reshape(count, 2 * rows, cells))
    inverse = np.ascontiguousarray(forward.transpose(0, 2, 1))
    return forward, inverse, factor


def turn(real, imag, step, length, orient):
    step %= length
    if step == 0:
        return real, imag
    if 2 * step == length:
        return -real, -imag
    if 4 * step == length or 4 * step == 3 * length:
        sign = orient if 4 * step == length else -orient
        return (-imag, real) if sign > 0 else (imag, -real)
    cosine = math.cos(2.0 * math.pi * step / length)
    sine = orient * math.sin(2.0 * math.pi * step / length)
    return cosine * real - sine * imag, sine * real + cosine * imag


def short_transform(pairs, orient):
    length = len(pairs)
    if length == 1:
        return pairs
    if length % 2 == 0:
        even = short_transform(pairs[0::2], orient)
        odd = short_transform(pairs[1::2], orient)
        half = length // 2
        out = [None] * length
        for k in range(half):
            real, imag = turn(*odd[k], k, length, orient)
            out[k] = (even[k][0] + real, even[k][1] + imag)
            out[k + half] = (even[k][0] - real, even[k][1] - imag)
        return out
    out = []
    for k in range(length):
        terms = [turn(*pairs[x], k * x, length, orient) for x in range(length)]
        out.append((sum(t[0] for t in terms), sum(t[1] for t in terms)))
    return out


def paired(weight_ref, at):
    real = weight_ref[at, 0]
    imag = weight_ref[at, 1]
    return jnp.concatenate(
        [jnp.concatenate([real, imag], axis=1), jnp.concatenate([-imag, real], axis=1)], axis=0
    )


def dot_transposed(left, right):
    return lax.dot_general(left, right, (((1,), (1,)), ((), ())), preferred_element_type=f32)


def forward_kernel(count, scale, cell_ref, table_ref, *out_refs):
    me = lax.axis_index("space")
    for step, out_ref in enumerate(out_refs):
        table = table_ref[lax.rem(me + step, count)]
        for plane in range(cell_ref.shape[0]):
            product = jnp.dot(table, cell_ref[plane], preferred_element_type=f32)
            out_ref[plane] = (product * scale).astype(bf16)


def activation_kernel(saved_ref, first_ref, bias_ref, act_ref, flip_ref, slope_ref):
    count, _, block, _ = first_ref.shape
    for at in range(count):
        lanes = slice(at * block, (at + 1) * block)
        saved = jnp.concatenate([saved_ref[0, :, lanes], saved_ref[1, :, lanes]], axis=1)
        bias = jnp.concatenate([bias_ref[0:1, lanes], bias_ref[1:2, lanes]], axis=1).astype(f32)
        pre = jnp.dot(saved, paired(first_ref, at), preferred_element_type=f32) + bias
        share = 0.5 * (1.0 + lax.erf(pre * inv_root_two))
        act_ref[at] = (pre * share).astype(bf16).T
        flip_ref[at] = saved.T
        slope_ref[at] = share + pre * jnp.exp(-0.5 * pre * pre) * inv_root_tau


def filter_kernel(
    count, samples, norm_scale, grad_scale, exchange, part_refs, act_ref, flip_ref, slope_ref,
    first_ref, second_ref, back_refs, term_refs, pencil, grad, inner, returned,
):
    me = lax.axis_index("space")
    blocks, _, block, _ = first_ref.shape
    planes = part_refs[0].shape[0] // samples
    rows = part_refs[0].shape[1] // 2
    length_x = count * planes
    tile = 16 if rows % 16 == 0 else rows
    for step, part_ref in enumerate(part_refs):
        home = lax.rem(me + count - step, count)
        for sample in range(samples):
            for plane in range(planes):
                pencil[sample, home * planes + plane] = part_ref[sample * planes + plane]
    for at in range(blocks):
        lanes = slice(at * block, (at + 1) * block)
        for sample in range(samples):
            for start in range(0, rows, tile):
                pairs = [
                    (
                        pencil[sample, x, start : start + tile, lanes].astype(f32),
                        pencil[sample, x, rows + start : rows + start + tile, lanes].astype(f32),
                    )
                    for x in range(length_x)
                ]
                for x, (real, imag) in enumerate(short_transform(pairs, -1)):
                    base = (sample * length_x + x) * rows + start
                    grad[base : base + tile, :block] = (real * norm_scale).astype(bf16)
                    grad[base : base + tile, block:] = (imag * norm_scale).astype(bf16)
        value = grad[...]
        back = dot_transposed(value, paired(second_ref, at))
        slope = (back * slope_ref[at]).astype(bf16)
        inner[...] = dot_transposed(slope, paired(first_ref, at))
        for sample in range(samples):
            for start in range(0, rows, tile):
                pairs = []
                for x in range(length_x):
                    base = (sample * length_x + x) * rows + start
                    pairs.append((inner[base : base + tile, :block], inner[base : base + tile, block:]))
                for x, (real, imag) in enumerate(short_transform(pairs, 1)):
                    returned[sample, x, start : start + tile, lanes] = real.astype(bf16)
                    returned[sample, x, rows + start : rows + start + tile, lanes] = imag.astype(bf16)
        for which, left, right in ((0, flip_ref[at], slope), (1, act_ref[at], value)):
            square = jnp.dot(left, right, preferred_element_type=f32) * grad_scale
            real = square[:block, :block] + square[block:, block:]
            imag = square[:block, block:] - square[block:, :block]
            for part, term in ((0, real), (1, imag)):
                if exchange:
                    keep_ref, send_ref = term_refs
                    split = term.reshape(count, 2, block // (2 * count), block)
                    mine = lax.axis_index("dp") == 0
                    keep_ref[:, which, at, part] = jnp.where(mine, split[:, 0], split[:, 1])
                    send_ref[:, which, at, part] = jnp.where(mine, split[:, 1], split[:, 0]).astype(bf16)
                else:
                    term_refs[0][which, at, part] = term.astype(bf16)
    for step, back_ref in enumerate(back_refs):
        home = lax.rem(me + step, count)
        for sample in range(samples):
            for plane in range(planes):
                back_ref[sample * planes + plane] = returned[sample, home * planes + plane]


def inverse_kernel(count, scale, table_ref, *refs):
    me = lax.axis_index("space")
    back_refs, out_ref = refs[:-1], refs[-1]
    for plane in range(out_ref.shape[0]):
        total = None
        for step, back_ref in enumerate(back_refs):
            table = table_ref[lax.rem(me + count - step, count)]
            product = jnp.dot(table, back_ref[plane], preferred_element_type=f32)
            total = product if total is None else total + product
        out_ref[plane] = (total * scale).astype(bf16)


def pair_sum_kernel(count, keep_ref, got_ref, own_ref, *send_refs):
    me = lax.axis_index("space")
    own_ref[...] = keep_ref[me] + got_ref[me].astype(f32)
    for step, send_ref in enumerate(send_refs):
        home = lax.rem(me + step + 1, count)
        send_ref[...] = (keep_ref[home] + got_ref[home].astype(f32)).astype(bf16)


def last_sum_kernel(own_ref, *refs):
    got_refs, out_refs = refs[:-2], refs[-2:]
    for which, out_ref in enumerate(out_refs):
        total = own_ref[which]
        for got_ref in got_refs:
            total = total + got_ref[which].astype(f32)
        out_ref[...] = total


def call(kernel, outs, args, scratch=(), flops=0, transcendentals=0, name=None):
    moved = sum(a.size * a.dtype.itemsize for a in args) + sum(
        math.prod(o.shape) * o.dtype.itemsize for o in outs
    )
    return pl.pallas_call(
        kernel,
        out_shape=tuple(outs),
        in_specs=[pl.BlockSpec(memory_space=pltpu.VMEM)] * len(args),
        out_specs=tuple(pl.BlockSpec(memory_space=pltpu.VMEM) for _ in outs),
        scratch_shapes=list(scratch),
        compiler_params=pltpu.CompilerParams(vmem_limit_bytes=vmem_bytes),
        cost_estimate=pl.CostEstimate(flops=flops, bytes_accessed=moved, transcendentals=transcendentals),
        name=name,
    )(*args)


def shifted(values, step, count, axis):
    return lax.ppermute(values, axis, [(at, (at + step) % count) for at in range(count)])


def body(grad_out, saved_spectrum, w_first, bias_first, w_second):
    samples, planes, length_y, length_z, width = grad_out.shape
    blocks, _, block, _ = w_first.shape
    count = lax.axis_size("space")
    pair = lax.axis_size("dp")
    length_x = planes * count
    cells = length_y * length_z
    rows = cells // count
    lines = samples * length_x * rows
    norm_scale = 1.0 / math.sqrt(length_x * cells)
    grad_scale = 1.0 / math.sqrt(length_x * cells * samples * pair)
    piece = block // (pair * count)
    exchange = pair == 2 and piece * pair * count == block and piece % 16 == 0
    forward, inverse, factor = transform_tables(length_y, length_z, count)
    shape = jax.ShapeDtypeStruct

    slab = shape((samples * planes, 2 * rows, width), bf16)
    parts = call(
        functools.partial(forward_kernel, count, 1.0 / factor),
        [slab] * count,
        [grad_out.reshape(samples * planes, cells, width), jnp.asarray(forward)],
        flops=4 * samples * planes * cells * cells * width,
        name="forward",
    )
    parts = [parts[0]] + [shifted(parts[s], s, count, "space") for s in range(1, count)]

    act, flip, slope = call(
        activation_kernel,
        [
            shape((blocks, 2 * block, lines), bf16),
            shape((blocks, 2 * block, lines), bf16),
            shape((blocks, lines, 2 * block), f32),
        ],
        [saved_spectrum.reshape(2, lines, width), w_first, bias_first],
        flops=8 * lines * block * block * blocks,
        transcendentals=4 * lines * width,
        name="activation",
    )

    if exchange:
        terms = [shape((count, 2, blocks, 2, piece, block), kind) for kind in (f32, bf16)]
    else:
        terms = [shape((2, blocks, 2, block, block), bf16)]

    def filter_body(*refs):
        part_refs = refs[:count]
        inputs = refs[count : count + 5]
        back_refs = refs[count + 5 : 2 * count + 5]
        term_refs = refs[2 * count + 5 : 2 * count + 5 + len(terms)]
        filter_kernel(
            count, samples, norm_scale, grad_scale, exchange, part_refs, *inputs, back_refs, term_refs,
            *refs[2 * count + 5 + len(terms) :],
        )

    results = call(
        filter_body,
        [slab] * count + terms,
        [*parts, act, flip, slope, w_first, w_second],
        scratch=[
            pltpu.VMEM((samples, length_x, 2 * rows, width), bf16),
            pltpu.VMEM((lines, 2 * block), bf16),
            pltpu.VMEM((lines, 2 * block), f32),
            pltpu.VMEM((samples, length_x, 2 * rows, width), bf16),
        ],
        flops=32 * lines * block * block * blocks,
        name="filter",
    )
    backs = results[:count]
    if exchange:
        keep, send = results[count:]
        got = shifted(send, 1, pair, "dp")
        backs = [backs[0]] + [shifted(backs[s], s, count, "space") for s in range(1, count)]
        piece_shape = (2, blocks, 2, piece, block)
        sums = call(
            functools.partial(pair_sum_kernel, count),
            [shape(piece_shape, f32)] + [shape(piece_shape, bf16)] * (count - 1),
            [keep, got],
            name="pair_sum",
        )
        others = [shifted(sums[s], s, count, "space") for s in range(1, count)]
        grad_first, grad_second = call(
            last_sum_kernel, [shape(piece_shape[1:], f32)] * 2, [sums[0], *others], name="last_sum"
        )
    else:
        backs = [backs[0]] + [shifted(backs[s], s, count, "space") for s in range(1, count)]
        term = lax.psum_scatter(results[count], "space", scatter_dimension=3, tiled=True)
        term = lax.psum_scatter(term, "dp", scatter_dimension=3, tiled=True).astype(f32)
        grad_first, grad_second = term[0], term[1]
    (grad_in,) = call(
        functools.partial(inverse_kernel, count, norm_scale / factor),
        [shape((samples * planes, cells, width), bf16)],
        [jnp.asarray(inverse), *backs],
        flops=4 * samples * planes * cells * cells * width,
        name="inverse",
    )
    return grad_in.reshape(grad_out.shape), grad_first, grad_second


def solution(mesh):
    in_specs = (
        P(("parts", "dp"), "space", None, None, "chan"),
        P(None, ("parts", "dp"), None, "space", None, "chan"),
        P("chan", None, None, None),
        P(None, "chan"),
        P("chan", None, None, None),
    )
    out_specs = (
        P(("parts", "dp"), "space", None, None, "chan"),
        P(("parts", "chan"), None, ("space", "dp"), None),
        P(("parts", "chan"), None, ("space", "dp"), None),
    )
    return jax.shard_map(body, mesh=mesh, in_specs=in_specs, out_specs=out_specs, check_vma=False)
```

time: 125 us -> 41.1 us (0.33)
  waiting for transfers between devices: 64.5 us -> 12.8 us
  matrix products: 16.2 us -> 0 us
  between operations: 15.7 us -> 0.68 us
  local copies, waits for them, and re-layouts: 16.8 us -> 2.95 us
  starting transfers between devices: 10.2 us -> 20.1 us
  Pallas kernels: 0 us -> 4.33 us
  other arithmetic: 1.26 us -> 0 us
    unnamed x4 -> x0, waiting for transfers between devices: 53.9 us -> none
    ppermute x0 -> x10, starting transfers between devices: none -> 20.1 us  [shifted(): lax.ppermute(values, axis, [(at, (at + step) % count) for at in range(cou...]
    dot_general x26 -> x0, matrix products: 16.2 us -> none  [the longest x6 8.34 us: apply_table(): jnp.einsum(pattern, table, values, precision=highest, preferred_element_t...]
    ppermute x0 -> x10, waiting for transfers between devices: none -> 12.8 us  [shifted(): lax.ppermute(values, axis, [(at, (at + step) % count) for at in range(cou...]
    all_to_all x2 -> x0, waiting for transfers between devices: 10.6 us -> none  [the longest x1 10.6 us: body(): lax.all_to_all(packed, 'space', split_axis=3, concat_axis=2, tiled=True)]
    all_to_all x2 -> x0, starting transfers between devices: 9.92 us -> none  [the longest x1 6.45 us: body(): lax.all_to_all(packed, 'space', split_axis=3, concat_axis=2, tiled=True)]
    unnamed x26 -> x14, local copies, waits for them, and re-layouts: 10.1 us -> 2.95 us
    convert_element_type x4 -> x0, local copies, waits for them, and re-layouts: 4.41 us -> none  [the longest x1 1.36 us: body(): packed = partial_spec.astype(jnp.bfloat16)]
  transfers between devices with their start and end apart: 4 -> 10, of which waited for: 3 -> 5; matrix products, arithmetic and copies ran while one was open for 12% -> 0% of each run, Pallas kernels for 0% -> 5%
where the time goes in v1:
time: 41.1 us; the launch traced here: 40.9 us
  starting transfers between devices  20.1 us (49%)
  waiting for transfers between devices  12.8 us (31%)
  Pallas kernels  4.33 us (11%)
  local copies, waits for them, and re-layouts  2.95 us (7%)
  between operations  0.68 us (2%)
    ppermute x10, starting transfers between devices, shifted(): lax.ppermute(values, axis, [(at, (at + step) % count) for at in range(cou...  20.1 us
    ppermute x10, waiting for transfers between devices, shifted(): lax.ppermute(values, axis, [(at, (at + step) % count) for at in range(cou...  12.8 us
    pallas_call x6, Pallas kernels, call(): pl.pallas_call(kernel, out_shape=tuple(outs), in_specs=[pl.BlockSpec(memo...  4.33 us
    unnamed x14, local copies, waits for them, and re-layouts  2.95 us
  transfers between devices with their start and end apart: 10, of which 5 were waited for; matrix products, arithmetic and copies ran while one was open for 0% of the time, Pallas kernels for 5%

profile of v1, /device:TPU:0, one launch (start us, length us, event | category | flops | bytes accessed | tf_op | source)
XLA Modules:
  0.0 40.9 jit_solution(1302496166554863252)
XLA Ops:
  0.6 0.9 %copy-done.2 = bf16[1,1,16,16,512]{4,3,2,1,0:T(8,128)(2,1)S(1)} copy-done((bf16[1,1,16,16,512]{4,3,2,1,0:T(8,128)(2,1)S(1)}, bf16[1,1,16,16,512]{4,3,2,1,0:T(8,128)(2,1)}, u32[]{:S(2)}) %copy-start.2) | copy-done | bytes 262168
  1.6 0.9 %copy-done.3 = bf16[4,128,256]{2,1,0:T(8,128)(2,1)S(1)} copy-done((bf16[4,128,256]{2,1,0:T(8,128)(2,1)S(1)}, bf16[4,128,256]{2,1,0:T(8,128)(2,1)}, u32[]{:S(2)}) %copy-start.3) | copy-done | bytes 262168
  2.5 0.3 forward.1
  2.8 3.1 %collective-permute-start = (bf16[1,128,512]{2,1,0:T(8,128)(2,1)S(1)}, bf16[1,128,512]{2,1,0:T(8,128)(2,1)S(1)}, u32[]{:S(2)}, u32[]{:S(2)}) collective-permute-start(bf16[1,128,512]{2,1,0:T(8,128)(2,1)S(1)} %get-tuple-element.23), channel_id=1, source_target_pairs={{0,4},{4,8},{8,12},{12,0},{1,5},{5,9},{9,13},{13,1},{2,6},{6,10},{... | collective-permute-start | bytes 393224 | tf_op jit(solution)/shard_map/ppermute | solution.py:228
  5.9 2.6 %collective-permute-start.1 = (bf16[1,128,512]{2,1,0:T(8,128)(2,1)S(1)}, bf16[1,128,512]{2,1,0:T(8,128)(2,1)S(1)}, u32[]{:S(2)}, u32[]{:S(2)}) collective-permute-start(bf16[1,128,512]{2,1,0:T(8,128)(2,1)S(1)} %get-tuple-element.24), channel_id=1, source_target_pairs={{0,8},{4,12},{8,0},{12,4},{1,9},{5,13},{9,1},{13,5},{2,10},{6,14},... | collective-permute-start | bytes 393224 | tf_op jit(solution)/shard_map/ppermute | solution.py:228
  8.5 1.3 %collective-permute-start.2 = (bf16[1,128,512]{2,1,0:T(8,128)(2,1)S(1)}, bf16[1,128,512]{2,1,0:T(8,128)(2,1)S(1)}, u32[]{:S(2)}, u32[]{:S(2)}) collective-permute-start(bf16[1,128,512]{2,1,0:T(8,128)(2,1)S(1)} %get-tuple-element.25), channel_id=1, source_target_pairs={{0,12},{4,0},{8,4},{12,8},{1,13},{5,1},{9,5},{13,9},{2,14},{6,2},{... | collective-permute-start | bytes 393224 | tf_op jit(solution)/shard_map/ppermute | solution.py:228
  9.9 1.0 %copy-done.5 = bf16[2,1,4,4,16,512]{5,4,3,2,1,0:T(8,128)(2,1)S(1)} copy-done((bf16[2,1,4,4,16,512]{5,4,3,2,1,0:T(8,128)(2,1)S(1)}, bf16[2,1,4,4,16,512]{5,4,3,2,1,0:T(8,128)(2,1)}, u32[]{:S(2)}) %copy-start.5) | copy-done | bytes 524312
  10.9 0.7 %activation.1 = (bf16[4,256,256]{2,1,0:T(8,128)(2,1)S(1)}, bf16[4,256,256]{2,1,0:T(8,128)(2,1)S(1)}, f32[4,256,256]{2,1,0:T(8,128)S(1)}) custom-call(bf16[2,256,512]{2,1,0:T(8,128)(2,1)S(1)} %bitcast.4, bf16[4,2,128,128]{3,2,1,0:T(8,128)(2,1)S(1)} %copy-done, bf16[2,512]{1,0:T(2,128)(2,1)S(1)} %copy-done.6), custom_call_target="tpu_custom_call" | custom-call | flops 134217728 | bytes 2885632 | tf_op jit(solution)/shard_map/activation/pallas_call | solution.py:215
  11.7 0.7 %collective-permute-done.refs_1_ = bf16[1,128,512]{2,1,0:T(8,128)(2,1)S(1)} collective-permute-done((bf16[1,128,512]{2,1,0:T(8,128)(2,1)S(1)}, bf16[1,128,512]{2,1,0:T(8,128)(2,1)S(1)}, u32[]{:S(2)}, u32[]{:S(2)}) %collective-permute-start) | collective-permute-done | bytes 131104 | tf_op jit(solution)/shard_map/ppermute | solution.py:228
  12.4 4.8 %collective-permute-done.1.refs_2_ = bf16[1,128,512]{2,1,0:T(8,128)(2,1)S(1)} collective-permute-done((bf16[1,128,512]{2,1,0:T(8,128)(2,1)S(1)}, bf16[1,128,512]{2,1,0:T(8,128)(2,1)S(1)}, u32[]{:S(2)}, u32[]{:S(2)}) %collective-permute-start.1) | collective-permute-done | bytes 131104 | tf_op jit(solution)/shard_map/ppermute | solution.py:228
  17.2 1.4 %filter.1 = (bf16[1,128,512]{2,1,0:T(8,128)(2,1)S(1)}, bf16[1,128,512]{2,1,0:T(8,128)(2,1)S(1)}, bf16[1,128,512]{2,1,0:T(8,128)(2,1)S(1)}, bf16[1,128,512]{2,1,0...) custom-call(bf16[1,128,512]{2,1,0:T(8,128)(2,1)S(1)} %get-tuple-element.22.refs_0_, ...), custom_call_target="tpu_custom_call" | custom-call | flops 536870912 | bytes 4456448 | tf_op jit(solution)/shard_map/filter/pallas_call | solution.py:215
  18.6 1.6 %collective-permute-start.6 = (bf16[4,2,4,2,16,128]{5,4,3,2,1,0:T(8,128)(2,1)S(1)}, bf16[4,2,4,2,16,128]{5,4,3,2,1,0:T(8,128)(2,1)S(1)}, u32[]{:S(2)}, u32[]{:S(2)}) collective-permute-start(bf16[4,2,4,2,16,128]{5,4,3,2,1,0:T(8,128)(2,1)S(1)} %get-tuple-element.34), channel_id=1, source_target_pairs={{0,2},{2,0},{1,3},{3,1},{4,6},{6,4},{5,7},{7,5},{8,10},{10,8},{9,1... | collective-permute-start | bytes 786440 | tf_op jit(solution)/shard_map/ppermute | solution.py:228
  20.2 3.3 %collective-permute-start.3 = (bf16[1,128,512]{2,1,0:T(8,128)(2,1)S(1)}, bf16[1,128,512]{2,1,0:T(8,128)(2,1)S(1)}, u32[]{:S(2)}, u32[]{:S(2)}) collective-permute-start(bf16[1,128,512]{2,1,0:T(8,128)(2,1)S(1)} %get-tuple-element.30), channel_id=1, source_target_pairs={{0,4},{4,8},{8,12},{12,0},{1,5},{5,9},{9,13},{13,1},{2,6},{6,10},{... | collective-permute-start | bytes 393224 | tf_op jit(solution)/shard_map/ppermute | solution.py:228
  23.4 1.6 %collective-permute-start.4 = (bf16[1,128,512]{2,1,0:T(8,128)(2,1)S(1)}, bf16[1,128,512]{2,1,0:T(8,128)(2,1)S(1)}, u32[]{:S(2)}, u32[]{:S(2)}) collective-permute-start(bf16[1,128,512]{2,1,0:T(8,128)(2,1)S(1)} %get-tuple-element.31), channel_id=1, source_target_pairs={{0,8},{4,12},{8,0},{12,4},{1,9},{5,13},{9,1},{13,5},{2,10},{6,14},... | collective-permute-start | bytes 393224 | tf_op jit(solution)/shard_map/ppermute | solution.py:228
  25.1 0.7 %collective-permute-start.5 = (bf16[1,128,512]{2,1,0:T(8,128)(2,1)S(1)}, bf16[1,128,512]{2,1,0:T(8,128)(2,1)S(1)}, u32[]{:S(2)}, u32[]{:S(2)}) collective-permute-start(bf16[1,128,512]{2,1,0:T(8,128)(2,1)S(1)} %get-tuple-element.32), channel_id=1, source_target_pairs={{0,12},{4,0},{8,4},{12,8},{1,13},{5,1},{9,5},{13,9},{2,14},{6,2},{... | collective-permute-start | bytes 393224 | tf_op jit(solution)/shard_map/ppermute | solution.py:228
  25.8 1.0 %collective-permute-done.6.got_ref = bf16[4,2,4,2,16,128]{5,4,3,2,1,0:T(8,128)(2,1)S(1)} collective-permute-done((bf16[4,2,4,2,16,128]{5,4,3,2,1,0:T(8,128)(2,1)S(1)}, bf16[4,2,4,2,16,128]{5,4,3,2,1,0:T(8,128)(2,1)S(1)}, u32[]{:S(2)}, u32[]{:S(2)}) %collective-permute-start.6) | collective-permute-done | bytes 262176 | tf_op jit(solution)/shard_map/ppermute | solution.py:228
  26.9 3.4 %collective-permute-start.7 = (bf16[2,4,2,16,128]{4,3,2,1,0:T(8,128)(2,1)S(1)}, bf16[2,4,2,16,128]{4,3,2,1,0:T(8,128)(2,1)S(1)}, u32[]{:S(2)}, u32[]{:S(2)}) collective-permute-start(bf16[2,4,2,16,128]{4,3,2,1,0:T(8,128)(2,1)S(1)} %get-tuple-element.36), channel_id=1, source_target_pairs={{0,4},{4,8},{8,12},{12,0},{1,5},{5,9},{9,13},{13,1},{2,6},{6,10},{... | collective-permute-start | bytes 196616 | tf_op jit(solution)/shard_map/ppermute | solution.py:228
  30.3 0.6 %collective-permute-start.8 = (bf16[2,4,2,16,128]{4,3,2,1,0:T(8,128)(2,1)S(1)}, bf16[2,4,2,16,128]{4,3,2,1,0:T(8,128)(2,1)S(1)}, u32[]{:S(2)}, u32[]{:S(2)}) collective-permute-start(bf16[2,4,2,16,128]{4,3,2,1,0:T(8,128)(2,1)S(1)} %get-tuple-element.37), channel_id=1, source_target_pairs={{0,8},{4,12},{8,0},{12,4},{1,9},{5,13},{9,1},{13,5},{2,10},{6,14},... | collective-permute-start | bytes 196616 | tf_op jit(solution)/shard_map/ppermute | solution.py:228
  30.9 1.9 %collective-permute-start.9 = (bf16[2,4,2,16,128]{4,3,2,1,0:T(8,128)(2,1)S(1)}, bf16[2,4,2,16,128]{4,3,2,1,0:T(8,128)(2,1)S(1)}, u32[]{:S(2)}, u32[]{:S(2)}) collective-permute-start(bf16[2,4,2,16,128]{4,3,2,1,0:T(8,128)(2,1)S(1)} %get-tuple-element.38), channel_id=1, source_target_pairs={{0,12},{4,0},{8,4},{12,8},{1,13},{5,1},{9,5},{13,9},{2,14},{6,2},{... | collective-permute-start | bytes 196616 | tf_op jit(solution)/shard_map/ppermute | solution.py:228
  32.7 2.0 %collective-permute-done.4.refs_2_ = bf16[1,128,512]{2,1,0:T(8,128)(2,1)S(1)} collective-permute-done((bf16[1,128,512]{2,1,0:T(8,128)(2,1)S(1)}, bf16[1,128,512]{2,1,0:T(8,128)(2,1)S(1)}, u32[]{:S(2)}, u32[]{:S(2)}) %collective-permute-start.4) | collective-permute-done | bytes 131104 | tf_op jit(solution)/shard_map/ppermute | solution.py:228
  34.7 1.1 %inverse.1 = bf16[1,256,512]{2,1,0:T(8,128)(2,1)} custom-call(bf16[4,256,128]{2,1,0:T(8,128)(2,1)S(1)} %copy-done.4, bf16[1,128,512]{2,1,0:T(8,128)(2,1)S(1)} %get-tuple-element.29.refs_0_, bf16[1,128,512]{2,1,0:T(8,128)(2,1)S(1)} %collective-permute-done.3.refs_1_, bf16[1,128,512]{2,1,0:T(8,128)(2,1)S(1)} %collective-permute-done.4.refs_2_, ...), custom_call_target="tpu_custom_call" | custom-call | flops 134217728 | bytes 1048576 | tf_op jit(solution)/shard_map/inverse/pallas_call | solution.py:215
  35.8 0.0 collective-permute-done.7.refs_0_
  35.9 4.3 %collective-permute-done.8.refs_1_ = bf16[2,4,2,16,128]{4,3,2,1,0:T(8,128)(2,1)S(1)} collective-permute-done((bf16[2,4,2,16,128]{4,3,2,1,0:T(8,128)(2,1)S(1)}, bf16[2,4,2,16,128]{4,3,2,1,0:T(8,128)(2,1)S(1)}, u32[]{:S(2)}, u32[]{:S(2)}) %collective-permute-start.8) | collective-permute-done | bytes 65568 | tf_op jit(solution)/shard_map/ppermute | solution.py:228
  40.2 0.7 %last_sum.1 = (f32[4,2,16,128]{3,2,1,0:T(8,128)}, f32[4,2,16,128]{3,2,1,0:T(8,128)}) custom-call(f32[2,4,2,16,128]{4,3,2,1,0:T(8,128)S(1)} %get-tuple-element.35.own_ref, bf16[2,4,2,16,128]{4,3,2,1,0:T(8,128)(2,1)S(1)} %collective-permute-done.7.refs_0_, bf16[2,4,2,16,128]{4,3,2,1,0:T(8,128)(2,1)S(1)} %collective-permute-done.8.refs_1_, ...), custom_call_target="tpu_custom_call" | custom-call | bytes 458752 | tf_op jit(solution)/shard_map/last_sum/pallas_call | solution.py:215
  (16 shorter events, 0.1 us)
Async XLA Ops:
  0.6 1.0 %copy-start.2 = (bf16[1,1,16,16,512]{4,3,2,1,0:T(8,128)(2,1)S(1)}, bf16[1,1,16,16,512]{4,3,2,1,0:T(8,128)(2,1)}, u32[]{:S(2)}) copy-start(bf16[1,1,16,16,512]{4,3,2,1,0:T(8,128)(2,1)} %param.7) | copy-start | bytes 786436
  1.6 0.9 %copy-start.3 = (bf16[4,128,256]{2,1,0:T(8,128)(2,1)S(1)}, bf16[4,128,256]{2,1,0:T(8,128)(2,1)}, u32[]{:S(2)}) copy-start(bf16[4,128,256]{2,1,0:T(8,128)(2,1)} %constant.4.clone.table_ref) | copy-start | bytes 786436
  2.5 7.3 %copy-start = (bf16[4,2,128,128]{3,2,1,0:T(8,128)(2,1)S(1)}, bf16[4,2,128,128]{3,2,1,0:T(8,128)(2,1)}, u32[]{:S(2)}) copy-start(bf16[4,2,128,128]{3,2,1,0:T(8,128)(2,1)} %refs_7_.1) | copy-start | bytes 786436
  2.8 9.5 %collective-permute-start = (bf16[1,128,512]{2,1,0:T(8,128)(2,1)S(1)}, bf16[1,128,512]{2,1,0:T(8,128)(2,1)S(1)}, u32[]{:S(2)}, u32[]{:S(2)}) collective-permute-start(bf16[1,128,512]{2,1,0:T(8,128)(2,1)S(1)} %get-tuple-element.23), channel_id=1, source_target_pairs={{0,4},{4,8},{8,12},{12,0},{1,5},{5,9},{9,13},{13,1},{2,6},{6,10},{... | collective-permute-start | bytes 393224 | tf_op jit(solution)/shard_map/ppermute | solution.py:228
  5.9 3.9 %copy-start.6 = (bf16[2,512]{1,0:T(2,128)(2,1)S(1)}, bf16[2,512]{1,0:T(2,128)(2,1)}, u32[]{:S(2)}) copy-start(bf16[2,512]{1,0:T(2,128)(2,1)} %bias_ref.1) | copy-start | bytes 6148
  5.9 11.2 %collective-permute-start.1 = (bf16[1,128,512]{2,1,0:T(8,128)(2,1)S(1)}, bf16[1,128,512]{2,1,0:T(8,128)(2,1)S(1)}, u32[]{:S(2)}, u32[]{:S(2)}) collective-permute-start(bf16[1,128,512]{2,1,0:T(8,128)(2,1)S(1)} %get-tuple-element.24), channel_id=1, source_target_pairs={{0,8},{4,12},{8,0},{12,4},{1,9},{5,13},{9,1},{13,5},{2,10},{6,14},... | collective-permute-start | bytes 393224 | tf_op jit(solution)/shard_map/ppermute | solution.py:228
  8.5 8.6 %collective-permute-start.2 = (bf16[1,128,512]{2,1,0:T(8,128)(2,1)S(1)}, bf16[1,128,512]{2,1,0:T(8,128)(2,1)S(1)}, u32[]{:S(2)}, u32[]{:S(2)}) collective-permute-start(bf16[1,128,512]{2,1,0:T(8,128)(2,1)S(1)} %get-tuple-element.25), channel_id=1, source_target_pairs={{0,12},{4,0},{8,4},{12,8},{1,13},{5,1},{9,5},{13,9},{2,14},{6,2},{... | collective-permute-start | bytes 393224 | tf_op jit(solution)/shard_map/ppermute | solution.py:228
  9.9 1.0 %copy-start.5 = (bf16[2,1,4,4,16,512]{5,4,3,2,1,0:T(8,128)(2,1)S(1)}, bf16[2,1,4,4,16,512]{5,4,3,2,1,0:T(8,128)(2,1)}, u32[]{:S(2)}) copy-start(bf16[2,1,4,4,16,512]{5,4,3,2,1,0:T(8,128)(2,1)} %param.8) | copy-start | bytes 1572868
  10.9 6.2 %copy-start.1 = (bf16[4,2,128,128]{3,2,1,0:T(8,128)(2,1)S(1)}, bf16[4,2,128,128]{3,2,1,0:T(8,128)(2,1)}, u32[]{:S(2)}) copy-start(bf16[4,2,128,128]{3,2,1,0:T(8,128)(2,1)} %refs_8_.1) | copy-start | bytes 786436
  18.6 8.2 %collective-permute-start.6 = (bf16[4,2,4,2,16,128]{5,4,3,2,1,0:T(8,128)(2,1)S(1)}, bf16[4,2,4,2,16,128]{5,4,3,2,1,0:T(8,128)(2,1)S(1)}, u32[]{:S(2)}, u32[]{:S(2)}) collective-permute-start(bf16[4,2,4,2,16,128]{5,4,3,2,1,0:T(8,128)(2,1)S(1)} %get-tuple-element.34), channel_id=1, source_target_pairs={{0,2},{2,0},{1,3},{3,1},{4,6},{6,4},{5,7},{7,5},{8,10},{10,8},{9,1... | collective-permute-start | bytes 786440 | tf_op jit(solution)/shard_map/ppermute | solution.py:228
  20.2 10.7 %collective-permute-start.3 = (bf16[1,128,512]{2,1,0:T(8,128)(2,1)S(1)}, bf16[1,128,512]{2,1,0:T(8,128)(2,1)S(1)}, u32[]{:S(2)}, u32[]{:S(2)}) collective-permute-start(bf16[1,128,512]{2,1,0:T(8,128)(2,1)S(1)} %get-tuple-element.30), channel_id=1, source_target_pairs={{0,4},{4,8},{8,12},{12,0},{1,5},{5,9},{9,13},{13,1},{2,6},{6,10},{... | collective-permute-start | bytes 393224 | tf_op jit(solution)/shard_map/ppermute | solution.py:228
  23.4 11.2 %collective-permute-start.4 = (bf16[1,128,512]{2,1,0:T(8,128)(2,1)S(1)}, bf16[1,128,512]{2,1,0:T(8,128)(2,1)S(1)}, u32[]{:S(2)}, u32[]{:S(2)}) collective-permute-start(bf16[1,128,512]{2,1,0:T(8,128)(2,1)S(1)} %get-tuple-element.31), channel_id=1, source_target_pairs={{0,8},{4,12},{8,0},{12,4},{1,9},{5,13},{9,1},{13,5},{2,10},{6,14},... | collective-permute-start | bytes 393224 | tf_op jit(solution)/shard_map/ppermute | solution.py:228
  25.1 9.6 %collective-permute-start.5 = (bf16[1,128,512]{2,1,0:T(8,128)(2,1)S(1)}, bf16[1,128,512]{2,1,0:T(8,128)(2,1)S(1)}, u32[]{:S(2)}, u32[]{:S(2)}) collective-permute-start(bf16[1,128,512]{2,1,0:T(8,128)(2,1)S(1)} %get-tuple-element.32), channel_id=1, source_target_pairs={{0,12},{4,0},{8,4},{12,8},{1,13},{5,1},{9,5},{13,9},{2,14},{6,2},{... | collective-permute-start | bytes 393224 | tf_op jit(solution)/shard_map/ppermute | solution.py:228
  26.8 7.9 %copy-start.4 = (bf16[4,256,128]{2,1,0:T(8,128)(2,1)S(1)}, bf16[4,256,128]{2,1,0:T(8,128)(2,1)}, u32[]{:S(2)}) copy-start(bf16[4,256,128]{2,1,0:T(8,128)(2,1)} %constant.5.clone.table_ref) | copy-start | bytes 786436
  26.9 9.0 %collective-permute-start.7 = (bf16[2,4,2,16,128]{4,3,2,1,0:T(8,128)(2,1)S(1)}, bf16[2,4,2,16,128]{4,3,2,1,0:T(8,128)(2,1)S(1)}, u32[]{:S(2)}, u32[]{:S(2)}) collective-permute-start(bf16[2,4,2,16,128]{4,3,2,1,0:T(8,128)(2,1)S(1)} %get-tuple-element.36), channel_id=1, source_target_pairs={{0,4},{4,8},{8,12},{12,0},{1,5},{5,9},{9,13},{13,1},{2,6},{6,10},{... | collective-permute-start | bytes 196616 | tf_op jit(solution)/shard_map/ppermute | solution.py:228
  30.3 9.9 %collective-permute-start.8 = (bf16[2,4,2,16,128]{4,3,2,1,0:T(8,128)(2,1)S(1)}, bf16[2,4,2,16,128]{4,3,2,1,0:T(8,128)(2,1)S(1)}, u32[]{:S(2)}, u32[]{:S(2)}) collective-permute-start(bf16[2,4,2,16,128]{4,3,2,1,0:T(8,128)(2,1)S(1)} %get-tuple-element.37), channel_id=1, source_target_pairs={{0,8},{4,12},{8,0},{12,4},{1,9},{5,13},{9,1},{13,5},{2,10},{6,14},... | collective-permute-start | bytes 196616 | tf_op jit(solution)/shard_map/ppermute | solution.py:228
  30.9 9.3 %collective-permute-start.9 = (bf16[2,4,2,16,128]{4,3,2,1,0:T(8,128)(2,1)S(1)}, bf16[2,4,2,16,128]{4,3,2,1,0:T(8,128)(2,1)S(1)}, u32[]{:S(2)}, u32[]{:S(2)}) collective-permute-start(bf16[2,4,2,16,128]{4,3,2,1,0:T(8,128)(2,1)S(1)} %get-tuple-element.38), channel_id=1, source_target_pairs={{0,12},{4,0},{8,4},{12,8},{1,13},{5,1},{9,5},{13,9},{2,14},{6,2},{... | collective-permute-start | bytes 196616 | tf_op jit(solution)/shard_map/ppermute | solution.py:228

commit v2 on v1

v2 whole, which is shorter than its diff:
```python
import functools
import math

import jax
import jax.numpy as jnp
import numpy as np
from jax import lax
from jax.experimental import pallas as pl
from jax.experimental.pallas import tpu as pltpu
from jax.sharding import PartitionSpec as P

inv_root_two = 1.0 / math.sqrt(2.0)
inv_root_tau = 1.0 / math.sqrt(2.0 * math.pi)
f32 = jnp.float32
bf16 = jnp.bfloat16
vmem_bytes = 24 * 1024 * 1024


def phase_table(length_y, length_z):
    whole = math.lcm(length_y, length_z)
    y = np.arange(length_y)
    z = np.arange(length_z)
    turns = (
        (y[:, None, None, None] * y[None, None, :, None]) * (whole // length_y)
        + (z[None, :, None, None] * z[None, None, None, :]) * (whole // length_z)
    ) % whole
    cells = length_y * length_z
    return turns.reshape(cells, cells) * (2.0 * math.pi / whole)


def round_scaled(table):
    levels = np.unique(np.abs(table).round(12))
    factors = np.linspace(1.0, 2.0, 2049)[:-1]
    scaled = factors[:, None] * levels
    error = np.abs(scaled.astype(bf16).astype(np.float64) / factors[:, None] - levels).max(axis=1)
    factor = float(factors[np.argmin(error)])
    return (table * factor).astype(bf16), factor


def inverse_table(length_y, length_z, count):
    angles = phase_table(length_y, length_z)
    cells = length_y * length_z
    rows = cells // count
    both = np.stack([np.cos(angles), -np.sin(angles)]).reshape(2, count, rows, cells)
    table, factor = round_scaled(both.transpose(1, 3, 0, 2).reshape(count, cells, 2 * rows))
    return table, factor


def turn(real, imag, step, length, orient):
    step %= length
    if step == 0:
        return real, imag
    if 2 * step == length:
        return -real, -imag
    if 4 * step == length or 4 * step == 3 * length:
        sign = orient if 4 * step == length else -orient
        return (-imag, real) if sign > 0 else (imag, -real)
    cosine = math.cos(2.0 * math.pi * step / length)
    sine = orient * math.sin(2.0 * math.pi * step / length)
    return cosine * real - sine * imag, sine * real + cosine * imag


def short_transform(pairs, orient):
    length = len(pairs)
    if length == 1:
        return pairs
    if length % 2 == 0:
        even = short_transform(pairs[0::2], orient)
        odd = short_transform(pairs[1::2], orient)
        half = length // 2
        out = [None] * length
        for k in range(half):
            real, imag = turn(*odd[k], k, length, orient)
            out[k] = (even[k][0] + real, even[k][1] + imag)
            out[k + half] = (even[k][0] - real, even[k][1] - imag)
        return out
    out = []
    for k in range(length):
        terms = [turn(*pairs[x], k * x, length, orient) for x in range(length)]
        out.append((sum(t[0] for t in terms), sum(t[1] for t in terms)))
    return out


def paired(weight_ref, at):
    real = weight_ref[at, 0]
    imag = weight_ref[at, 1]
    return jnp.concatenate(
        [jnp.concatenate([real, imag], axis=1), jnp.concatenate([-imag, real], axis=1)], axis=0
    )


def dot_transposed(left, right):
    return lax.dot_general(left, right, (((1,), (1,)), ((), ())), preferred_element_type=f32)


def wave_rows(length, cells, inner, outer):
    row = lax.broadcasted_iota(jnp.int32, (length, cells), 0)
    cell = lax.broadcasted_iota(jnp.int32, (length, cells), 1)
    angle = lax.rem(row * lax.rem(cell // inner, outer), length).astype(f32) * (2.0 * math.pi / length)
    return jnp.cos(angle), jnp.sin(angle)


def forward_kernel(count, factor, length_y, length_z, spans, cell_ref, *refs):
    out_refs, (table_ref,) = refs[:-1], refs[-1:]
    me = lax.axis_index("space")
    planes, cells, _ = cell_ref.shape
    rows = cells // count
    cos_y, sin_y = wave_rows(length_y, cells, length_z, length_y)
    cos_z, sin_z = wave_rows(length_z, cells, 1, length_z)
    cos_z, sin_z = cos_z * factor, sin_z * factor
    each = length_y // count
    for ky in range(length_y):
        cos_k, sin_k = cos_y[ky : ky + 1], sin_y[ky : ky + 1]
        start = ky % each * length_z
        table_ref[ky // each, start : start + length_z] = (cos_z * cos_k - sin_z * sin_k).astype(bf16)
        table_ref[ky // each, rows + start : rows + start + length_z] = (
            -(cos_z * sin_k) - sin_z * cos_k
        ).astype(bf16)
    for step in range(count):
        table = table_ref[lax.rem(me + step, count)]
        for plane in range(planes):
            product = jnp.dot(table, cell_ref[plane], preferred_element_type=f32) * (1.0 / factor)
            for chunk, (low, high) in enumerate(spans):
                out_refs[chunk * count + step][plane] = product[:, low:high].astype(bf16)


def activation_kernel(spans, saved_ref, first_ref, bias_ref, *out_refs):
    count, _, block, _ = first_ref.shape
    for at in range(count):
        chunk = [low <= at * block < high for low, high in spans].index(True)
        here = at - spans[chunk][0] // block
        lanes = slice(at * block, (at + 1) * block)
        saved = jnp.concatenate([saved_ref[0, :, lanes], saved_ref[1, :, lanes]], axis=1)
        bias = jnp.concatenate([bias_ref[0:1, lanes], bias_ref[1:2, lanes]], axis=1).astype(f32)
        pre = jnp.dot(saved, paired(first_ref, at), preferred_element_type=f32) + bias
        share = 0.5 * (1.0 + lax.erf(pre * inv_root_two))
        act_ref, flip_ref, slope_ref = out_refs[chunk * 3 : chunk * 3 + 3]
        act_ref[here] = (pre * share).astype(bf16).T
        flip_ref[here] = saved.T
        slope_ref[here] = share + pre * jnp.exp(-0.5 * pre * pre) * inv_root_tau


def filter_kernel(
    count, samples, norm_scale, first_block, part_refs, slope_ref, first_ref, second_ref, back_refs,
    value_ref, delta_ref, pencil, inner, returned,
):
    me = lax.axis_index("space")
    blocks = slope_ref.shape[0]
    block = first_ref.shape[2]
    planes = part_refs[0].shape[0] // samples
    rows = part_refs[0].shape[1] // 2
    length_x = count * planes
    tile = 16 if rows % 16 == 0 else rows
    for step, part_ref in enumerate(part_refs):
        home = lax.rem(me + count - step, count)
        for sample in range(samples):
            for plane in range(planes):
                pencil[sample, home * planes + plane] = part_ref[sample * planes + plane]
    for at in range(blocks):
        lanes = slice(at * block, (at + 1) * block)
        for sample in range(samples):
            for start in range(0, rows, tile):
                pairs = [
                    (
                        pencil[sample, x, start : start + tile, lanes].astype(f32),
                        pencil[sample, x, rows + start : rows + start + tile, lanes].astype(f32),
                    )
                    for x in range(length_x)
                ]
                for x, (real, imag) in enumerate(short_transform(pairs, -1)):
                    base = (sample * length_x + x) * rows + start
                    value_ref[at, base : base + tile, :block] = (real * norm_scale).astype(bf16)
                    value_ref[at, base : base + tile, block:] = (imag * norm_scale).astype(bf16)
        back = dot_transposed(value_ref[at], paired(second_ref, first_block + at))
        delta = (back * slope_ref[at]).astype(bf16)
        delta_ref[at] = delta
        inner[...] = dot_transposed(delta, paired(first_ref, first_block + at))
        for sample in range(samples):
            for start in range(0, rows, tile):
                pairs = []
                for x in range(length_x):
                    base = (sample * length_x + x) * rows + start
                    pairs.append((inner[base : base + tile, :block], inner[base : base + tile, block:]))
                for x, (real, imag) in enumerate(short_transform(pairs, 1)):
                    returned[sample, x, start : start + tile, lanes] = real.astype(bf16)
                    returned[sample, x, rows + start : rows + start + tile, lanes] = imag.astype(bf16)
    for step, back_ref in enumerate(back_refs):
        home = lax.rem(me + step, count)
        for sample in range(samples):
            for plane in range(planes):
                back_ref[sample * planes + plane] = returned[sample, home * planes + plane]


def weight_kernel(count, scale, exchange, chunks, *refs):
    groups = [refs[4 * c : 4 * c + 4] for c in range(chunks)]
    term_refs = refs[4 * chunks :]
    at = 0
    for act_ref, flip_ref, value_ref, delta_ref in groups:
        block = act_ref.shape[1] // 2
        for here in range(act_ref.shape[0]):
            lanes = slice(at * block, (at + 1) * block)
            for which, left, right in ((0, flip_ref, delta_ref), (1, act_ref, value_ref)):
                square = jnp.dot(left[here], right[here], preferred_element_type=f32) * scale
                real = square[:block, :block] + square[block:, block:]
                imag = square[:block, block:] - square[block:, :block]
                for part, term in ((0, real), (1, imag)):
                    if exchange:
                        keep_ref, send_refs = term_refs[0], term_refs[1:]
                        piece = block // (2 * count)
                        split = term.reshape(count, 2, piece, block)
                        mine = lax.axis_index("dp") == 0
                        place = slice((2 * which + part) * piece, (2 * which + part + 1) * piece)
                        keep_ref[:, place, lanes] = jnp.where(mine, split[:, 0], split[:, 1])
                        short = slice(part * piece, (part + 1) * piece)
                        send_refs[which][:, short, lanes] = jnp.where(mine, split[:, 1], split[:, 0]).astype(bf16)
                    else:
                        term_refs[0][which, at, part] = term.astype(bf16)
            at += 1


def inverse_kernel(count, scale, low, high, table_ref, *refs):
    me = lax.axis_index("space")
    back_refs, (out_ref, held, sem) = refs[:count], refs[-3:]
    for plane in range(held.shape[0]):
        total = None
        for step, back_ref in enumerate(back_refs):
            table = table_ref[lax.rem(me + count - step, count)]
            product = jnp.dot(table, back_ref[plane], preferred_element_type=f32)
            total = product if total is None else total + product
        held[plane] = (total * scale).astype(bf16)
    copy = pltpu.make_async_copy(held, out_ref.at[:, :, low:high], sem)
    copy.start()
    copy.wait()


def pair_sum_kernel(count, extra, keep_ref, low_ref, high_ref, *refs):
    me = lax.axis_index("space")
    for step, out_ref in enumerate(refs[extra:]):
        home = lax.rem(me + step, count)
        half = low_ref.shape[1]
        out_ref[:half] = (keep_ref[home, :half] + low_ref[home].astype(f32)).astype(out_ref.dtype)
        out_ref[half:] = (keep_ref[home, half:] + high_ref[home].astype(f32)).astype(out_ref.dtype)


def last_sum_kernel(*refs):
    got_refs, out_refs = refs[:-2], refs[-2:]
    blocks, _, piece, block = out_refs[0].shape
    total = got_refs[0][...]
    for got_ref in got_refs[1:]:
        total = total + got_ref[...].astype(f32)
    for at in range(blocks):
        for which in range(2):
            for part in range(2):
                place = (2 * which + part) * piece
                out_refs[which][at, part] = total[place : place + piece, at * block : (at + 1) * block]


def call(kernel, outs, args, scratch=(), flops=0, transcendentals=0, name=None, **extra):
    whole = pl.BlockSpec(memory_space=pltpu.VMEM)
    return pl.pallas_call(
        kernel,
        out_shape=tuple(outs),
        in_specs=extra.pop("in_specs", [whole] * len(args)),
        out_specs=extra.pop("out_specs", (whole,) * len(outs)),
        scratch_shapes=list(scratch),
        compiler_params=pltpu.CompilerParams(vmem_limit_bytes=vmem_bytes),
        cost_estimate=pl.CostEstimate(flops=0, bytes_accessed=0, transcendentals=0),
        name=name,
        **extra,
    )(*args)


def shifted(values, step, count, axis):
    return lax.ppermute(values, axis, [(at, (at + step) % count) for at in range(count)])


def body(grad_out, saved_spectrum, w_first, bias_first, w_second):
    samples, planes, length_y, length_z, width = grad_out.shape
    blocks, _, block, _ = w_first.shape
    count = lax.axis_size("space")
    pair = lax.axis_size("dp")
    length_x = planes * count
    cells = length_y * length_z
    rows = cells // count
    lines = samples * length_x * rows
    norm_scale = 1.0 / math.sqrt(length_x * cells)
    grad_scale = 1.0 / math.sqrt(length_x * cells * samples * pair)
    piece = block // (pair * count)
    exchange = pair == 2 and piece * pair * count == block and piece % 16 == 0
    sizes = (blocks,)
    chunks = len(sizes)
    spans = [(sum(sizes[:c]) * block, sum(sizes[: c + 1]) * block) for c in range(chunks)]
    slabs = samples * planes
    inverse, factor = inverse_table(length_y, length_z, count)
    shape = jax.ShapeDtypeStruct
    far_first = sorted(range(1, count), key=lambda s: -min(s, count - s))

    def spread(values):
        moved = {s: shifted(values[s], s, count, "space") for s in far_first}
        return [values[0]] + [moved[s] for s in range(1, count)]

    outs = call(
        functools.partial(forward_kernel, count, factor, length_y, length_z, spans),
        [shape((slabs, 2 * rows, high - low), bf16) for low, high in spans for _ in range(count)],
        [grad_out.reshape(slabs, cells, width)],
        scratch=[pltpu.VMEM((count, 2 * rows, cells), bf16)],
        flops=4 * slabs * cells * cells * width,
        name="forward",
    )
    parts = [spread(outs[c * count : (c + 1) * count]) for c in range(chunks)]

    active = call(
        functools.partial(activation_kernel, spans),
        [
            shape((each,) + dims, kind)
            for each in sizes
            for dims, kind in (
                ((2 * block, lines), bf16),
                ((2 * block, lines), bf16),
                ((lines, 2 * block), f32),
            )
        ],
        [saved_spectrum.reshape(2, lines, width), w_first, bias_first],
        flops=8 * lines * block * block * blocks,
        transcendentals=4 * lines * width,
        name="activation",
    )

    inverses = []
    groups = []
    for chunk, (low, high) in enumerate(spans):
        each = sizes[chunk]
        lanes = high - low
        act, flip, slope = active[3 * chunk : 3 * chunk + 3]

        def filter_body(*refs, low=low):
            filter_kernel(
                count, samples, norm_scale, low // block, refs[:count], *refs[count : count + 3],
                refs[count + 3 : 2 * count + 3], *refs[2 * count + 3 :],
            )

        results = call(
            filter_body,
            [shape((slabs, 2 * rows, lanes), bf16)] * count + [shape((each, lines, 2 * block), bf16)] * 2,
            [*parts[chunk], slope, w_first, w_second],
            scratch=[
                pltpu.VMEM((samples, length_x, 2 * rows, lanes), bf16),
                pltpu.VMEM((lines, 2 * block), f32),
                pltpu.VMEM((samples, length_x, 2 * rows, lanes), bf16),
            ],
            flops=16 * lines * block * block * each,
            name="filter" + str(chunk),
        )
        groups += [act, flip, *results[count:]]
        inverses.append(([jnp.asarray(inverse), *spread(results[:count])], low, high))

    if exchange:
        terms = [shape((count, 4 * piece, width), f32)] + [shape((count, 2 * piece, width), bf16)] * 2
    else:
        terms = [shape((2, blocks, 2, block, block), bf16)]
    terms = call(
        functools.partial(weight_kernel, count, grad_scale, exchange, chunks), terms, groups,
        flops=16 * lines * block * block * blocks, name="weight",
    )
    grad_in = None

    def invert(out, args, low, high):
        aliases = {}
        if out is not None:
            aliases = {len(args): 0}
            args = args + [out]

        return call(
            functools.partial(inverse_kernel, count, norm_scale / factor, low, high),
            [shape((slabs, cells, width), bf16)],
            args,
            in_specs=[pl.BlockSpec(memory_space=pltpu.VMEM)] * (count + 1)
            + [pl.BlockSpec(memory_space=pl.ANY)] * len(aliases),
            out_specs=(pl.BlockSpec(memory_space=pl.ANY),),
            scratch=[pltpu.VMEM((slabs, cells, high - low), bf16), pltpu.SemaphoreType.DMA],
            input_output_aliases=aliases,
            flops=4 * slabs * cells * cells * (high - low),
            name="inverse" + str(low // block),
        )[0]

    if exchange:
        keep = terms[0]
        got = [shifted(send, 1, pair, "dp") for send in terms[1:]]
        ties = [inverses[0][0][1 + far_first[0]]]
        sums = call(
            functools.partial(pair_sum_kernel, count, len(ties)),
            [shape((4 * piece, width), f32)] + [shape((4 * piece, width), bf16)] * (count - 1),
            [keep, *got, *ties],
            in_specs=[pl.BlockSpec(memory_space=pltpu.VMEM)] * 3
            + [pl.BlockSpec(memory_space=pl.ANY)] * len(ties),
            name="pair_sum",
        )
        grad_first, grad_second = call(
            last_sum_kernel,
            [shape((blocks, 2, piece, block), f32)] * 2,
            spread(sums),
            name="last_sum",
        )
    else:
        term = lax.psum_scatter(terms[0], "space", scatter_dimension=3, tiled=True)
        term = lax.psum_scatter(term, "dp", scatter_dimension=3, tiled=True).astype(f32)
        grad_first, grad_second = term[0], term[1]
    for piece_args in inverses:
        grad_in = invert(grad_in, *piece_args)
    return grad_in.reshape(grad_out.shape), grad_first, grad_second


def solution(mesh):
    in_specs = (
        P(("parts", "dp"), "space", None, None, "chan"),
        P(None, ("parts", "dp"), None, "space", None, "chan"),
        P("chan", None, None, None),
        P(None, "chan"),
        P("chan", None, None, None),
    )
    out_specs = (
        P(("parts", "dp"), "space", None, None, "chan"),
        P(("parts", "chan"), None, ("space", "dp"), None),
        P(("parts", "chan"), None, ("space", "dp"), None),
    )
    return jax.shard_map(body, mesh=mesh, in_specs=in_specs, out_specs=out_specs, check_vma=False)
```

time: 41.1 us -> 37.8 us (0.920)
  waiting for transfers between devices: 12.8 us -> 11.2 us
  local copies, waits for them, and re-layouts: 2.95 us -> 2.04 us
  starting transfers between devices: 20.1 us -> 19.4 us
    ppermute x10 -> x11, waiting for transfers between devices: 12.8 us -> 11.2 us  [shifted(): lax.ppermute(values, axis, [(at, (at + step) % count) for at in range(cou...]
    unnamed x14 -> x12, local copies, waits for them, and re-layouts: 2.95 us -> 2.04 us
    ppermute x10 -> x11, starting transfers between devices: 20.1 us -> 19.4 us  [shifted(): lax.ppermute(values, axis, [(at, (at + step) % count) for at in range(cou...]
    pallas_call x6 -> x7, Pallas kernels: 4.33 us -> 4.31 us  [call(): pl.pallas_call(kernel, out_shape=tuple(outs), in_specs=extra.pop('in_spec...]
  transfers between devices with their start and end apart: 10 -> 11, of which waited for: 5 -> 7; matrix products, arithmetic and copies ran while one was open for 0% -> 0% of each run, Pallas kernels for 5% -> 6%
where the time goes in v2:
time: 37.8 us; the launch traced here: 37.6 us
  starting transfers between devices  19.4 us (51%)
  waiting for transfers between devices  11.2 us (30%)
  Pallas kernels  4.31 us (11%)
  local copies, waits for them, and re-layouts  2.04 us (5%)
  between operations  0.71 us (2%)
    ppermute x11, starting transfers between devices, shifted(): lax.ppermute(values, axis, [(at, (at + step) % count) for at in range(cou...  19.4 us
    ppermute x11, waiting for transfers between devices, shifted(): lax.ppermute(values, axis, [(at, (at + step) % count) for at in range(cou...  11.2 us
    pallas_call x7, Pallas kernels, call(): pl.pallas_call(kernel, out_shape=tuple(outs), in_specs=extra.pop('in_spec...  4.31 us
    unnamed x12, local copies, waits for them, and re-layouts  2.04 us
  transfers between devices with their start and end apart: 11, of which 7 were waited for; matrix products, arithmetic and copies ran while one was open for 0% of the time, Pallas kernels for 6%

profile of v2, /device:TPU:0, one launch (start us, length us, event | category | flops | bytes accessed | tf_op | source)
XLA Modules:
  0.0 37.6 jit_solution(2401239365793861042)
XLA Ops:
  0.6 1.0 %copy-done.2 = bf16[1,1,16,16,512]{4,3,2,1,0:T(8,128)(2,1)S(1)} copy-done((bf16[1,1,16,16,512]{4,3,2,1,0:T(8,128)(2,1)S(1)}, bf16[1,1,16,16,512]{4,3,2,1,0:T(8,128)(2,1)}, u32[]{:S(2)}) %copy-start.2) | copy-done | bytes 262168
  1.6 0.5 %forward.1 = (bf16[1,128,512]{2,1,0:T(8,128)(2,1)S(1)}, bf16[1,128,512]{2,1,0:T(8,128)(2,1)S(1)}, bf16[1,128,512]{2,1,0:T(8,128)(2,1)S(1)}, bf16[1,128,512]{2,1,0:T(8,128)(2,1)S(1)}) custom-call(bf16[1,256,512]{2,1,0:T(8,128)(2,1)S(1)} %bitcast.4), custom_call_target="tpu_custom_call" | custom-call | tf_op jit(solution)/shard_map/forward/pallas_call | solution.py:260
  2.1 3.1 %collective-permute-start = (bf16[1,128,512]{2,1,0:T(8,128)(2,1)S(1)}, bf16[1,128,512]{2,1,0:T(8,128)(2,1)S(1)}, u32[]{:S(2)}, u32[]{:S(2)}) collective-permute-start(bf16[1,128,512]{2,1,0:T(8,128)(2,1)S(1)} %get-tuple-element.26), channel_id=1, source_target_pairs={{0,4},{4,8},{8,12},{12,0},{1,5},{5,9},{9,13},{13,1},{2,6},{6,10},{... | collective-permute-start | bytes 393224 | tf_op jit(solution)/shard_map/ppermute | solution.py:274
  5.2 2.6 %collective-permute-start.1 = (bf16[1,128,512]{2,1,0:T(8,128)(2,1)S(1)}, bf16[1,128,512]{2,1,0:T(8,128)(2,1)S(1)}, u32[]{:S(2)}, u32[]{:S(2)}) collective-permute-start(bf16[1,128,512]{2,1,0:T(8,128)(2,1)S(1)} %get-tuple-element.27), channel_id=1, source_target_pairs={{0,8},{4,12},{8,0},{12,4},{1,9},{5,13},{9,1},{13,5},{2,10},{6,14},... | collective-permute-start | bytes 393224 | tf_op jit(solution)/shard_map/ppermute | solution.py:274
  7.8 1.3 %collective-permute-start.2 = (bf16[1,128,512]{2,1,0:T(8,128)(2,1)S(1)}, bf16[1,128,512]{2,1,0:T(8,128)(2,1)S(1)}, u32[]{:S(2)}, u32[]{:S(2)}) collective-permute-start(bf16[1,128,512]{2,1,0:T(8,128)(2,1)S(1)} %get-tuple-element.28), channel_id=1, source_target_pairs={{0,12},{4,0},{8,4},{12,8},{1,13},{5,1},{9,5},{13,9},{2,14},{6,2},{... | collective-permute-start | bytes 393224 | tf_op jit(solution)/shard_map/ppermute | solution.py:274
  9.2 1.0 %copy-done.1 = bf16[2,1,4,4,16,512]{5,4,3,2,1,0:T(8,128)(2,1)S(1)} copy-done((bf16[2,1,4,4,16,512]{5,4,3,2,1,0:T(8,128)(2,1)S(1)}, bf16[2,1,4,4,16,512]{5,4,3,2,1,0:T(8,128)(2,1)}, u32[]{:S(2)}) %copy-start.1) | copy-done | bytes 524312
  10.2 0.7 %activation.1 = (bf16[4,256,256]{2,1,0:T(8,128)(2,1)S(1)}, bf16[4,256,256]{2,1,0:T(8,128)(2,1)S(1)}, f32[4,256,256]{2,1,0:T(8,128)S(1)}) custom-call(bf16[2,256,512]{2,1,0:T(8,128)(2,1)S(1)} %bitcast.3, bf16[4,2,128,128]{3,2,1,0:T(8,128)(2,1)S(1)} %copy-done, bf16[2,512]{1,0:T(2,128)(2,1)S(1)} %copy-done.5), custom_call_target="tpu_custom_call" | custom-call | tf_op jit(solution)/shard_map/activation/pallas_call | solution.py:260
  10.9 0.7 %collective-permute-done.refs_1_ = bf16[1,128,512]{2,1,0:T(8,128)(2,1)S(1)} collective-permute-done((bf16[1,128,512]{2,1,0:T(8,128)(2,1)S(1)}, bf16[1,128,512]{2,1,0:T(8,128)(2,1)S(1)}, u32[]{:S(2)}, u32[]{:S(2)}) %collective-permute-start) | collective-permute-done | bytes 131104 | tf_op jit(solution)/shard_map/ppermute | solution.py:274
  11.7 4.8 %collective-permute-done.1.refs_2_ = bf16[1,128,512]{2,1,0:T(8,128)(2,1)S(1)} collective-permute-done((bf16[1,128,512]{2,1,0:T(8,128)(2,1)S(1)}, bf16[1,128,512]{2,1,0:T(8,128)(2,1)S(1)}, u32[]{:S(2)}, u32[]{:S(2)}) %collective-permute-start.1) | collective-permute-done | bytes 131104 | tf_op jit(solution)/shard_map/ppermute | solution.py:274
  16.5 0.8 %filter0.1 = (bf16[1,128,512]{2,1,0:T(8,128)(2,1)S(1)}, bf16[1,128,512]{2,1,0:T(8,128)(2,1)S(1)}, bf16[1,128,512]{2,1,0:T(8,128)(2,1)S(1)}, bf16[1,128,512]{2,1,...) custom-call(bf16[1,128,512]{2,1,0:T(8,128)(2,1)S(1)} %get-tuple-element.25.refs_0_, ...), custom_call_target="tpu_custom_call" | custom-call | tf_op jit(solution)/shard_map/filter0/pallas_call | solution.py:260
  17.2 2.3 %collective-permute-start.4 = (bf16[1,128,512]{2,1,0:T(8,128)(2,1)S(1)}, bf16[1,128,512]{2,1,0:T(8,128)(2,1)S(1)}, u32[]{:S(2)}, u32[]{:S(2)}) collective-permute-start(bf16[1,128,512]{2,1,0:T(8,128)(2,1)S(1)} %get-tuple-element.32), channel_id=1, source_target_pairs={{0,8},{4,12},{8,0},{12,4},{1,9},{5,13},{9,1},{13,5},{2,10},{6,14},... | collective-permute-start | bytes 393224 | tf_op jit(solution)/shard_map/ppermute | solution.py:274
  19.6 0.5 %weight.1 = (f32[4,64,512]{2,1,0:T(8,128)S(1)}, bf16[4,32,512]{2,1,0:T(8,128)(2,1)S(1)}, bf16[4,32,512]{2,1,0:T(8,128)(2,1)S(1)}) custom-call(bf16[4,256,256]{2,1,0:T(8,128)(2,1)S(1)} %get-tuple-element.34.refs_0_, bf16[4,256,256]{2,1,0:T(8,128)(2,1)S(1)} %get-tuple-element.35.refs_1_, bf16[4,256,256]{2,1,0:T(8,128)(2,1)S(1)} %get-tuple-element.36.refs_2_, ...), custom_call_target="tpu_custom_call" | custom-call | tf_op jit(solution)/shard_map/weight/pallas_call | solution.py:260
  20.0 1.6 %collective-permute-start.6 = (bf16[4,32,512]{2,1,0:T(8,128)(2,1)S(1)}, bf16[4,32,512]{2,1,0:T(8,128)(2,1)S(1)}, u32[]{:S(2)}, u32[]{:S(2)}) collective-permute-start(bf16[4,32,512]{2,1,0:T(8,128)(2,1)S(1)} %get-tuple-element.39), channel_id=1, source_target_pairs={{0,2},{2,0},{1,3},{3,1},{4,6},{6,4},{5,7},{7,5},{8,10},{10,8},{9,1... | collective-permute-start | bytes 393224 | tf_op jit(solution)/shard_map/ppermute | solution.py:274
  21.6 0.5 %collective-permute-start.7 = (bf16[4,32,512]{2,1,0:T(8,128)(2,1)S(1)}, bf16[4,32,512]{2,1,0:T(8,128)(2,1)S(1)}, u32[]{:S(2)}, u32[]{:S(2)}) collective-permute-start(bf16[4,32,512]{2,1,0:T(8,128)(2,1)S(1)} %get-tuple-element.40), channel_id=1, source_target_pairs={{0,2},{2,0},{1,3},{3,1},{4,6},{6,4},{5,7},{7,5},{8,10},{10,8},{9,1... | collective-permute-start | bytes 393224 | tf_op jit(solution)/shard_map/ppermute | solution.py:274
  22.1 2.7 %collective-permute-start.3 = (bf16[1,128,512]{2,1,0:T(8,128)(2,1)S(1)}, bf16[1,128,512]{2,1,0:T(8,128)(2,1)S(1)}, u32[]{:S(2)}, u32[]{:S(2)}) collective-permute-start(bf16[1,128,512]{2,1,0:T(8,128)(2,1)S(1)} %get-tuple-element.31), channel_id=1, source_target_pairs={{0,4},{4,8},{8,12},{12,0},{1,5},{5,9},{9,13},{13,1},{2,6},{6,10},{... | collective-permute-start | bytes 393224 | tf_op jit(solution)/shard_map/ppermute | solution.py:274
  24.8 1.2 %collective-permute-start.5 = (bf16[1,128,512]{2,1,0:T(8,128)(2,1)S(1)}, bf16[1,128,512]{2,1,0:T(8,128)(2,1)S(1)}, u32[]{:S(2)}, u32[]{:S(2)}) collective-permute-start(bf16[1,128,512]{2,1,0:T(8,128)(2,1)S(1)} %get-tuple-element.33), channel_id=1, source_target_pairs={{0,12},{4,0},{8,4},{12,8},{1,13},{5,1},{9,5},{13,9},{2,14},{6,2},{... | collective-permute-start | bytes 393224 | tf_op jit(solution)/shard_map/ppermute | solution.py:274
  25.9 0.5 %collective-permute-done.6.low_ref = bf16[4,32,512]{2,1,0:T(8,128)(2,1)S(1)} collective-permute-done((bf16[4,32,512]{2,1,0:T(8,128)(2,1)S(1)}, bf16[4,32,512]{2,1,0:T(8,128)(2,1)S(1)}, u32[]{:S(2)}, u32[]{:S(2)}) %collective-permute-start.6) | collective-permute-done | bytes 131104 | tf_op jit(solution)/shard_map/ppermute | solution.py:274
  26.5 1.5 %collective-permute-done.7.high_ref = bf16[4,32,512]{2,1,0:T(8,128)(2,1)S(1)} collective-permute-done((bf16[4,32,512]{2,1,0:T(8,128)(2,1)S(1)}, bf16[4,32,512]{2,1,0:T(8,128)(2,1)S(1)}, u32[]{:S(2)}, u32[]{:S(2)}) %collective-permute-start.7) | collective-permute-done | bytes 131104 | tf_op jit(solution)/shard_map/ppermute | solution.py:274
  28.1 1.7 %collective-permute-start.8 = (bf16[64,512]{1,0:T(8,128)(2,1)S(1)}, bf16[64,512]{1,0:T(8,128)(2,1)S(1)}, u32[]{:S(2)}, u32[]{:S(2)}) collective-permute-start(bf16[64,512]{1,0:T(8,128)(2,1)S(1)} %get-tuple-element.42), channel_id=1, source_target_pairs={{0,4},{4,8},{8,12},{12,0},{1,5},{5,9},{9,13},{13,1},{2,6},{6,10},{... | collective-permute-start | bytes 196616 | tf_op jit(solution)/shard_map/ppermute | solution.py:274
  29.8 2.3 %collective-permute-start.9 = (bf16[64,512]{1,0:T(8,128)(2,1)S(1)}, bf16[64,512]{1,0:T(8,128)(2,1)S(1)}, u32[]{:S(2)}, u32[]{:S(2)}) collective-permute-start(bf16[64,512]{1,0:T(8,128)(2,1)S(1)} %get-tuple-element.43), channel_id=1, source_target_pairs={{0,8},{4,12},{8,0},{12,4},{1,9},{5,13},{9,1},{13,5},{2,10},{6,14},... | collective-permute-start | bytes 196616 | tf_op jit(solution)/shard_map/ppermute | solution.py:274
  32.2 1.1 %inverse0.1 = bf16[1,256,512]{2,1,0:T(8,128)(2,1)} custom-call(bf16[4,256,128]{2,1,0:T(8,128)(2,1)S(1)} %copy-done.3, bf16[1,128,512]{2,1,0:T(8,128)(2,1)S(1)} %get-tuple-element.30.refs_0_, bf16[1,128,512]{2,1,0:T(8,128)(2,1)S(1)} %collective-permute-done.3.refs_1_, bf16[1,128,512]{2,1,0:T(8,128)(2,1)S(1)} %collective-permute-done.4.refs_2_.refs_0_, ...), custom_call_target="tpu_custom_call" | custom-call | tf_op jit(solution)/shard_map/inverse0/pallas_call | solution.py:260
  33.3 1.6 %collective-permute-done.8.refs_1_ = bf16[64,512]{1,0:T(8,128)(2,1)S(1)} collective-permute-done((bf16[64,512]{1,0:T(8,128)(2,1)S(1)}, bf16[64,512]{1,0:T(8,128)(2,1)S(1)}, u32[]{:S(2)}, u32[]{:S(2)}) %collective-permute-start.8) | collective-permute-done | bytes 65568 | tf_op jit(solution)/shard_map/ppermute | solution.py:274
  34.9 1.8 %collective-permute-done.9.refs_2_ = bf16[64,512]{1,0:T(8,128)(2,1)S(1)} collective-permute-done((bf16[64,512]{1,0:T(8,128)(2,1)S(1)}, bf16[64,512]{1,0:T(8,128)(2,1)S(1)}, u32[]{:S(2)}, u32[]{:S(2)}) %collective-permute-start.9) | collective-permute-done | bytes 65568 | tf_op jit(solution)/shard_map/ppermute | solution.py:274
  36.9 0.7 %last_sum.1 = (f32[4,2,16,128]{3,2,1,0:T(8,128)}, f32[4,2,16,128]{3,2,1,0:T(8,128)}) custom-call(f32[64,512]{1,0:T(8,128)S(1)} %get-tuple-element.41.refs_0_, bf16[64,512]{1,0:T(8,128)(2,1)S(1)} %collective-permute-done.8.refs_1_, bf16[64,512]{1,0:T(8,128)(2,1)S(1)} %collective-permute-done.9.refs_2_, bf16[64,512]{1,0:T(8,128)(2,1)S(1)} %collective-permute-done.10.refs_3_), custom_call_target="tpu_custom_call" | custom-call | tf_op jit(solution)/shard_map/last_sum/pallas_call | solution.py:260
  (17 shorter events, 0.3 us)
Async XLA Ops:
  0.6 8.5 %copy-start = (bf16[4,2,128,128]{3,2,1,0:T(8,128)(2,1)S(1)}, bf16[4,2,128,128]{3,2,1,0:T(8,128)(2,1)}, u32[]{:S(2)}) copy-start(bf16[4,2,128,128]{3,2,1,0:T(8,128)(2,1)} %refs_5_.1) | copy-start | bytes 786436
  0.6 1.0 %copy-start.2 = (bf16[1,1,16,16,512]{4,3,2,1,0:T(8,128)(2,1)S(1)}, bf16[1,1,16,16,512]{4,3,2,1,0:T(8,128)(2,1)}, u32[]{:S(2)}) copy-start(bf16[1,1,16,16,512]{4,3,2,1,0:T(8,128)(2,1)} %param.6) | copy-start | bytes 786436
  2.1 9.5 %collective-permute-start = (bf16[1,128,512]{2,1,0:T(8,128)(2,1)S(1)}, bf16[1,128,512]{2,1,0:T(8,128)(2,1)S(1)}, u32[]{:S(2)}, u32[]{:S(2)}) collective-permute-start(bf16[1,128,512]{2,1,0:T(8,128)(2,1)S(1)} %get-tuple-element.26), channel_id=1, source_target_pairs={{0,4},{4,8},{8,12},{12,0},{1,5},{5,9},{9,13},{13,1},{2,6},{6,10},{... | collective-permute-start | bytes 393224 | tf_op jit(solution)/shard_map/ppermute | solution.py:274
  5.2 3.9 %copy-start.5 = (bf16[2,512]{1,0:T(2,128)(2,1)S(1)}, bf16[2,512]{1,0:T(2,128)(2,1)}, u32[]{:S(2)}) copy-start(bf16[2,512]{1,0:T(2,128)(2,1)} %bias_ref.1) | copy-start | bytes 6148
  5.2 11.2 %collective-permute-start.1 = (bf16[1,128,512]{2,1,0:T(8,128)(2,1)S(1)}, bf16[1,128,512]{2,1,0:T(8,128)(2,1)S(1)}, u32[]{:S(2)}, u32[]{:S(2)}) collective-permute-start(bf16[1,128,512]{2,1,0:T(8,128)(2,1)S(1)} %get-tuple-element.27), channel_id=1, source_target_pairs={{0,8},{4,12},{8,0},{12,4},{1,9},{5,13},{9,1},{13,5},{2,10},{6,14},... | collective-permute-start | bytes 393224 | tf_op jit(solution)/shard_map/ppermute | solution.py:274
  7.8 8.6 %collective-permute-start.2 = (bf16[1,128,512]{2,1,0:T(8,128)(2,1)S(1)}, bf16[1,128,512]{2,1,0:T(8,128)(2,1)S(1)}, u32[]{:S(2)}, u32[]{:S(2)}) collective-permute-start(bf16[1,128,512]{2,1,0:T(8,128)(2,1)S(1)} %get-tuple-element.28), channel_id=1, source_target_pairs={{0,12},{4,0},{8,4},{12,8},{1,13},{5,1},{9,5},{13,9},{2,14},{6,2},{... | collective-permute-start | bytes 393224 | tf_op jit(solution)/shard_map/ppermute | solution.py:274
  9.1 1.0 %copy-start.1 = (bf16[2,1,4,4,16,512]{5,4,3,2,1,0:T(8,128)(2,1)S(1)}, bf16[2,1,4,4,16,512]{5,4,3,2,1,0:T(8,128)(2,1)}, u32[]{:S(2)}) copy-start(bf16[2,1,4,4,16,512]{5,4,3,2,1,0:T(8,128)(2,1)} %param.7) | copy-start | bytes 1572868
  10.2 6.3 %copy-start.4 = (bf16[4,2,128,128]{3,2,1,0:T(8,128)(2,1)S(1)}, bf16[4,2,128,128]{3,2,1,0:T(8,128)(2,1)}, u32[]{:S(2)}) copy-start(bf16[4,2,128,128]{3,2,1,0:T(8,128)(2,1)} %refs_6_.1) | copy-start | bytes 786436
  17.2 8.7 %collective-permute-start.4 = (bf16[1,128,512]{2,1,0:T(8,128)(2,1)S(1)}, bf16[1,128,512]{2,1,0:T(8,128)(2,1)S(1)}, u32[]{:S(2)}, u32[]{:S(2)}) collective-permute-start(bf16[1,128,512]{2,1,0:T(8,128)(2,1)S(1)} %get-tuple-element.32), channel_id=1, source_target_pairs={{0,8},{4,12},{8,0},{12,4},{1,9},{5,13},{9,1},{13,5},{2,10},{6,14},... | collective-permute-start | bytes 393224 | tf_op jit(solution)/shard_map/ppermute | solution.py:274
  20.0 6.5 %collective-permute-start.6 = (bf16[4,32,512]{2,1,0:T(8,128)(2,1)S(1)}, bf16[4,32,512]{2,1,0:T(8,128)(2,1)S(1)}, u32[]{:S(2)}, u32[]{:S(2)}) collective-permute-start(bf16[4,32,512]{2,1,0:T(8,128)(2,1)S(1)} %get-tuple-element.39), channel_id=1, source_target_pairs={{0,2},{2,0},{1,3},{3,1},{4,6},{6,4},{5,7},{7,5},{8,10},{10,8},{9,1... | collective-permute-start | bytes 393224 | tf_op jit(solution)/shard_map/ppermute | solution.py:274
  21.6 6.5 %collective-permute-start.7 = (bf16[4,32,512]{2,1,0:T(8,128)(2,1)S(1)}, bf16[4,32,512]{2,1,0:T(8,128)(2,1)S(1)}, u32[]{:S(2)}, u32[]{:S(2)}) collective-permute-start(bf16[4,32,512]{2,1,0:T(8,128)(2,1)S(1)} %get-tuple-element.40), channel_id=1, source_target_pairs={{0,2},{2,0},{1,3},{3,1},{4,6},{6,4},{5,7},{7,5},{8,10},{10,8},{9,1... | collective-permute-start | bytes 393224 | tf_op jit(solution)/shard_map/ppermute | solution.py:274
  22.1 10.1 %collective-permute-start.3 = (bf16[1,128,512]{2,1,0:T(8,128)(2,1)S(1)}, bf16[1,128,512]{2,1,0:T(8,128)(2,1)S(1)}, u32[]{:S(2)}, u32[]{:S(2)}) collective-permute-start(bf16[1,128,512]{2,1,0:T(8,128)(2,1)S(1)} %get-tuple-element.31), channel_id=1, source_target_pairs={{0,4},{4,8},{8,12},{12,0},{1,5},{5,9},{9,13},{13,1},{2,6},{6,10},{... | collective-permute-start | bytes 393224 | tf_op jit(solution)/shard_map/ppermute | solution.py:274
  24.8 7.4 %collective-permute-start.5 = (bf16[1,128,512]{2,1,0:T(8,128)(2,1)S(1)}, bf16[1,128,512]{2,1,0:T(8,128)(2,1)S(1)}, u32[]{:S(2)}, u32[]{:S(2)}) collective-permute-start(bf16[1,128,512]{2,1,0:T(8,128)(2,1)S(1)} %get-tuple-element.33), channel_id=1, source_target_pairs={{0,12},{4,0},{8,4},{12,8},{1,13},{5,1},{9,5},{13,9},{2,14},{6,2},{... | collective-permute-start | bytes 393224 | tf_op jit(solution)/shard_map/ppermute | solution.py:274
  28.0 4.2 %copy-start.3 = (bf16[4,256,128]{2,1,0:T(8,128)(2,1)S(1)}, bf16[4,256,128]{2,1,0:T(8,128)(2,1)}, u32[]{:S(2)}) copy-start(bf16[4,256,128]{2,1,0:T(8,128)(2,1)} %constant.2.clone.table_ref) | copy-start | bytes 786436
  28.1 6.9 %collective-permute-start.8 = (bf16[64,512]{1,0:T(8,128)(2,1)S(1)}, bf16[64,512]{1,0:T(8,128)(2,1)S(1)}, u32[]{:S(2)}, u32[]{:S(2)}) collective-permute-start(bf16[64,512]{1,0:T(8,128)(2,1)S(1)} %get-tuple-element.42), channel_id=1, source_target_pairs={{0,4},{4,8},{8,12},{12,0},{1,5},{5,9},{9,13},{13,1},{2,6},{6,10},{... | collective-permute-start | bytes 196616 | tf_op jit(solution)/shard_map/ppermute | solution.py:274
  29.8 7.0 %collective-permute-start.9 = (bf16[64,512]{1,0:T(8,128)(2,1)S(1)}, bf16[64,512]{1,0:T(8,128)(2,1)S(1)}, u32[]{:S(2)}, u32[]{:S(2)}) collective-permute-start(bf16[64,512]{1,0:T(8,128)(2,1)S(1)} %get-tuple-element.43), channel_id=1, source_target_pairs={{0,8},{4,12},{8,0},{12,4},{1,9},{5,13},{9,1},{13,5},{2,10},{6,14},... | collective-permute-start | bytes 196616 | tf_op jit(solution)/shard_map/ppermute | solution.py:274
  32.1 4.8 %collective-permute-start.10 = (bf16[64,512]{1,0:T(8,128)(2,1)S(1)}, bf16[64,512]{1,0:T(8,128)(2,1)S(1)}, u32[]{:S(2)}, u32[]{:S(2)}) collective-permute-start(bf16[64,512]{1,0:T(8,128)(2,1)S(1)} %get-tuple-element.44), channel_id=1, source_target_pairs={{0,12},{4,0},{8,4},{12,8},{1,13},{5,1},{9,5},{13,9},{2,14},{6,2},{... | collective-permute-start | bytes 196616 | tf_op jit(solution)/shard_map/ppermute | solution.py:274

commit v3 on v1

v3 whole, which is shorter than its diff:
```python
import functools
import math

import jax
import jax.numpy as jnp
import numpy as np
from jax import lax
from jax.experimental import pallas as pl
from jax.experimental.pallas import tpu as pltpu
from jax.sharding import PartitionSpec as P

inv_root_two = 1.0 / math.sqrt(2.0)
inv_root_tau = 1.0 / math.sqrt(2.0 * math.pi)
f32 = jnp.float32
bf16 = jnp.bfloat16
vmem_bytes = 24 * 1024 * 1024


def phase_table(length_y, length_z):
    whole = math.lcm(length_y, length_z)
    y = np.arange(length_y)
    z = np.arange(length_z)
    turns = (
        (y[:, None, None, None] * y[None, None, :, None]) * (whole // length_y)
        + (z[None, :, None, None] * z[None, None, None, :]) * (whole // length_z)
    ) % whole
    cells = length_y * length_z
    return turns.reshape(cells, cells) * (2.0 * math.pi / whole)


def round_scaled(table):
    levels = np.unique(np.abs(table).round(12))
    factors = np.linspace(1.0, 2.0, 2049)[:-1]
    scaled = factors[:, None] * levels
    error = np.abs(scaled.astype(bf16).astype(np.float64) / factors[:, None] - levels).max(axis=1)
    factor = float(factors[np.argmin(error)])
    return (table * factor).astype(bf16), factor


def inverse_table(length_y, length_z, count):
    angles = phase_table(length_y, length_z)
    cells = length_y * length_z
    rows = cells // count
    both = np.stack([np.cos(angles), -np.sin(angles)]).reshape(2, count, rows, cells)
    table, factor = round_scaled(both.transpose(1, 3, 0, 2).reshape(count, cells, 2 * rows))
    return table, factor


def turn(real, imag, step, length, orient):
    step %= length
    if step == 0:
        return real, imag
    if 2 * step == length:
        return -real, -imag
    if 4 * step == length or 4 * step == 3 * length:
        sign = orient if 4 * step == length else -orient
        return (-imag, real) if sign > 0 else (imag, -real)
    cosine = math.cos(2.0 * math.pi * step / length)
    sine = orient * math.sin(2.0 * math.pi * step / length)
    return cosine * real - sine * imag, sine * real + cosine * imag


def short_transform(pairs, orient):
    length = len(pairs)
    if length == 1:
        return pairs
    if length % 2 == 0:
        even = short_transform(pairs[0::2], orient)
        odd = short_transform(pairs[1::2], orient)
        half = length // 2
        out = [None] * length
        for k in range(half):
            real, imag = turn(*odd[k], k, length, orient)
            out[k] = (even[k][0] + real, even[k][1] + imag)
            out[k + half] = (even[k][0] - real, even[k][1] - imag)
        return out
    out = []
    for k in range(length):
        terms = [turn(*pairs[x], k * x, length, orient) for x in range(length)]
        out.append((sum(t[0] for t in terms), sum(t[1] for t in terms)))
    return out


def paired(weight_ref, at):
    real = weight_ref[at, 0]
    imag = weight_ref[at, 1]
    return jnp.concatenate(
        [jnp.concatenate([real, imag], axis=1), jnp.concatenate([-imag, real], axis=1)], axis=0
    )


def wave_rows(length, cells, inner, outer):
    row = lax.broadcasted_iota(jnp.int32, (length, cells), 0)
    cell = lax.broadcasted_iota(jnp.int32, (length, cells), 1)
    angle = lax.rem(row * lax.rem(cell // inner, outer), length).astype(f32) * (2.0 * math.pi / length)
    return jnp.cos(angle), jnp.sin(angle)


RING = (0, 0, 1)
EARLY = (2, 3)
AFTER = 1
TIE = 2


def ring_order(count, phase):
    if not RING[phase]:
        return list(range(count))
    return [0] + list(range(1, count, 2)) + list(range(count - 2 + count % 2, 0, -2))


def neighbour(me, step, count, phase):
    order = ring_order(count, phase)
    home = jnp.int32(0)
    for at, here in enumerate(order):
        home = jnp.where(me == here, order[(at + step) % count], home)
    return home


def forward_kernel(count, factor, length_y, length_z, cell_ref, *refs):
    out_refs, table_ref = refs[:-1], refs[-1]
    me = lax.axis_index("space")
    planes, cells, _ = cell_ref.shape
    rows = cells // count
    cos_y, sin_y = wave_rows(length_y, cells, length_z, length_y)
    cos_z, sin_z = wave_rows(length_z, cells, 1, length_z)
    cos_z, sin_z = cos_z * factor, sin_z * factor
    each = length_y // count
    for ky in range(length_y):
        cos_k, sin_k = cos_y[ky : ky + 1], sin_y[ky : ky + 1]
        start = ky % each * length_z
        table_ref[ky // each, start : start + length_z] = (cos_z * cos_k - sin_z * sin_k).astype(bf16)
        table_ref[ky // each, rows + start : rows + start + length_z] = (
            -(cos_z * sin_k) - sin_z * cos_k
        ).astype(bf16)
    for step, out_ref in enumerate(out_refs):
        table = table_ref[neighbour(me, step, count, 0)]
        for plane in range(planes):
            product = jnp.dot(table, cell_ref[plane], preferred_element_type=f32) * (1.0 / factor)
            out_ref[plane] = product.astype(bf16)


def activation_kernel(
    saved_ref, first_ref, bias_ref, second_ref, act_ref, flip_ref, slope_ref, first_back_ref, second_back_ref
):
    count, _, block, _ = first_ref.shape
    for at in range(count):
        lanes = slice(at * block, (at + 1) * block)
        first = paired(first_ref, at)
        first_back_ref[at] = first.T
        second_back_ref[at] = paired(second_ref, at).T
        saved = jnp.concatenate([saved_ref[0, :, lanes], saved_ref[1, :, lanes]], axis=1)
        bias = jnp.concatenate([bias_ref[0:1, lanes], bias_ref[1:2, lanes]], axis=1).astype(f32)
        pre = jnp.dot(saved, first, preferred_element_type=f32) + bias
        share = 0.5 * (1.0 + lax.erf(pre * inv_root_two))
        act_ref[at] = (pre * share).astype(bf16).T
        flip_ref[at] = saved.T
        slope_ref[at] = share + pre * jnp.exp(-0.5 * pre * pre) * inv_root_tau


def filter_kernel(
    count, samples, norm_scale, part_refs, slope_ref, first_back_ref, second_back_ref, back_refs,
    value_ref, delta_ref, pencil, inner, returned,
):
    me = lax.axis_index("space")
    blocks = slope_ref.shape[0]
    block = first_back_ref.shape[1] // 2
    planes = part_refs[0].shape[0] // samples
    rows = part_refs[0].shape[1] // 2
    length_x = count * planes
    tile = 16 if rows % 16 == 0 else rows
    for step, part_ref in enumerate(part_refs):
        home = neighbour(me, -step, count, 0)
        for sample in range(samples):
            for plane in range(planes):
                pencil[sample, home * planes + plane] = part_ref[sample * planes + plane]
    for at in range(blocks):
        lanes = slice(at * block, (at + 1) * block)
        for sample in range(samples):
            for start in range(0, rows, tile):
                pairs = [
                    (
                        pencil[sample, x, start : start + tile, lanes].astype(f32),
                        pencil[sample, x, rows + start : rows + start + tile, lanes].astype(f32),
                    )
                    for x in range(length_x)
                ]
                for x, (real, imag) in enumerate(short_transform(pairs, -1)):
                    base = (sample * length_x + x) * rows + start
                    value_ref[at, base : base + tile, :block] = (real * norm_scale).astype(bf16)
                    value_ref[at, base : base + tile, block:] = (imag * norm_scale).astype(bf16)
        back = jnp.dot(value_ref[at], second_back_ref[at], preferred_element_type=f32)
        delta = (back * slope_ref[at]).astype(bf16)
        delta_ref[at] = delta
        inner[at] = jnp.dot(delta, first_back_ref[at], preferred_element_type=f32)
        for sample in range(samples):
            for start in range(0, rows, tile):
                pairs = []
                for x in range(length_x):
                    base = (sample * length_x + x) * rows + start
                    pairs.append((inner[at, base : base + tile, :block], inner[at, base : base + tile, block:]))
                for x, (real, imag) in enumerate(short_transform(pairs, 1)):
                    returned[sample, x, start : start + tile, lanes] = real.astype(bf16)
                    returned[sample, x, rows + start : rows + start + tile, lanes] = imag.astype(bf16)
    for step, back_ref in enumerate(back_refs):
        home = neighbour(me, step, count, 1)
        for sample in range(samples):
            for plane in range(planes):
                back_ref[sample * planes + plane] = returned[sample, home * planes + plane]


def weight_kernel(count, scale, exchange, groups, act_ref, flip_ref, value_ref, delta_ref, *term_refs):
    block = act_ref.shape[1] // 2
    for at in range(act_ref.shape[0]):
        lanes = slice(at * block, (at + 1) * block)
        for which, left, right in ((0, flip_ref, delta_ref), (1, act_ref, value_ref)):
            square = jnp.dot(left[at], right[at], preferred_element_type=f32) * scale
            real = square[:block, :block] + square[block:, block:]
            imag = square[:block, block:] - square[block:, :block]
            for part, term in ((0, real), (1, imag)):
                if exchange:
                    keep_ref, send_ref = term_refs[0], term_refs[-1]
                    piece = block // (2 * count)
                    split = term.reshape(count, 2, piece, block)
                    mine = lax.axis_index("dp") == 0
                    place = slice((2 * which + part) * piece, (2 * which + part + 1) * piece)
                    keep_ref[:, place, lanes] = jnp.where(mine, split[:, 0], split[:, 1])
                    send_ref[:, place, lanes] = jnp.where(mine, split[:, 1], split[:, 0]).astype(bf16)
                else:
                    term_refs[0][which, at, part] = term.astype(bf16)
    if exchange:
        me = lax.axis_index("space")
        for steps, out_ref in zip(groups, term_refs[1:-1]):
            for slot, step in enumerate(steps):
                out_ref[slot] = term_refs[-1][neighbour(me, step, count, 2)]


def inverse_kernel(count, scale, table_ref, *refs):
    me = lax.axis_index("space")
    back_refs, out_ref = refs[:-1], refs[-1]
    for plane in range(out_ref.shape[0]):
        total = None
        for step, back_ref in enumerate(back_refs):
            table = table_ref[neighbour(me, -step, count, 1)]
            product = jnp.dot(table, back_ref[plane], preferred_element_type=f32)
            total = product if total is None else total + product
        out_ref[plane] = (total * scale).astype(bf16)


def pair_sum_kernel(count, steps, keep_ref, got_ref, *refs):
    me = lax.axis_index("space")
    for slot, step in enumerate(steps):
        out_ref = refs[len(refs) - len(steps) + slot]
        out_ref[...] = (keep_ref[neighbour(me, step, count, 2)] + got_ref[slot].astype(f32)).astype(out_ref.dtype)


def last_sum_kernel(*refs):
    got_refs, out_refs = refs[:-2], refs[-2:]
    blocks, _, piece, block = out_refs[0].shape
    total = got_refs[0][...]
    for got_ref in got_refs[1:]:
        total = total + got_ref[...].astype(f32)
    for at in range(blocks):
        for which in range(2):
            for part in range(2):
                place = (2 * which + part) * piece
                out_refs[which][at, part] = total[place : place + piece, at * block : (at + 1) * block]


def call(kernel, outs, args, scratch=(), loose=0, name=None):
    whole = pl.BlockSpec(memory_space=pltpu.VMEM)
    return pl.pallas_call(
        kernel,
        out_shape=tuple(outs),
        in_specs=[whole] * (len(args) - loose) + [pl.BlockSpec(memory_space=pl.ANY)] * loose,
        out_specs=(whole,) * len(outs),
        scratch_shapes=list(scratch),
        compiler_params=pltpu.CompilerParams(vmem_limit_bytes=vmem_bytes),
        name=name,
    )(*args)


def spread(values, count, phase):
    order = ring_order(count, phase)
    moved = []
    for step in range(1, count):
        pairs = [(order[at], order[(at + step) % count]) for at in range(count)]
        moved.append(lax.ppermute(values[step], "space", pairs))
    return [values[0]] + moved


def body(grad_out, saved_spectrum, w_first, bias_first, w_second):
    samples, planes, length_y, length_z, width = grad_out.shape
    blocks, _, block, _ = w_first.shape
    count = lax.axis_size("space")
    pair = lax.axis_size("dp")
    length_x = planes * count
    cells = length_y * length_z
    rows = cells // count
    lines = samples * length_x * rows
    slabs = samples * planes
    norm_scale = 1.0 / math.sqrt(length_x * cells)
    grad_scale = 1.0 / math.sqrt(length_x * cells * samples * pair)
    piece = block // (pair * count)
    exchange = pair == 2 and piece * pair * count == block and piece % 16 == 0
    inverse, factor = inverse_table(length_y, length_z, count)
    shape = jax.ShapeDtypeStruct
    slab = shape((slabs, 2 * rows, width), bf16)
    square = shape((blocks, 2 * block, 2 * block), bf16)
    tall = shape((blocks, lines, 2 * block), bf16)
    wide = shape((blocks, 2 * block, lines), bf16)

    parts = spread(
        call(
            functools.partial(forward_kernel, count, factor, length_y, length_z),
            [slab] * count,
            [grad_out.reshape(slabs, cells, width)],
            scratch=[pltpu.VMEM((count, 2 * rows, cells), bf16)],
            name="forward",
        ),
        count,
        0,
    )
    act, flip, slope, first_back, second_back = call(
        activation_kernel,
        [wide, wide, shape((blocks, lines, 2 * block), f32), square, square],
        [saved_spectrum.reshape(2, lines, width), w_first, bias_first, w_second],
        name="activation",
    )

    def filter_body(*refs):
        filter_kernel(
            count, samples, norm_scale, refs[:count], *refs[count : count + 3], refs[count + 3 : 2 * count + 3],
            *refs[2 * count + 3 :],
        )

    *backs, value, delta = call(
        filter_body,
        [slab] * count + [tall, tall],
        [*parts, slope, first_back, second_back],
        scratch=[
            pltpu.VMEM((samples, length_x, 2 * rows, width), bf16),
            pltpu.VMEM((blocks, lines, 2 * block), f32),
            pltpu.VMEM((samples, length_x, 2 * rows, width), bf16),
        ],
        name="filter",
    )
    backs = spread(backs, count, 1)
    early = EARLY if count == 4 else tuple(range(1, count // 2 + 1))
    groups = (early, (0,) + tuple(step for step in range(1, count) if step not in early))
    if exchange:
        terms = [shape((count, 4 * piece, width), f32)]
        terms += [shape((len(steps), 4 * piece, width), bf16) for steps in groups]
        scratch = [pltpu.VMEM((count, 4 * piece, width), bf16)]
    else:
        terms = [shape((2, blocks, 2, block, block), bf16)]
        scratch = []
    terms = call(
        functools.partial(weight_kernel, count, grad_scale, exchange, groups), terms, [act, flip, value, delta],
        scratch=scratch, name="weight",
    )
    if exchange:
        keep, *sends = terms
        got = [lax.ppermute(send, "dp", [(0, 1), (1, 0)]) for send in sends]
        sums = {}
        for at, steps in enumerate(groups):
            after = [backs[TIE]] if at == AFTER else []
            outs = call(
                functools.partial(pair_sum_kernel, count, steps),
                [shape((4 * piece, width), bf16 if step else f32) for step in steps],
                [keep, got[at], *after],
                loose=len(after),
                name="pair_sum" + str(at),
            )
            sums.update(zip(steps, outs))
        grad_first, grad_second = call(
            last_sum_kernel, [shape((blocks, 2, piece, block), f32)] * 2, spread([sums[step] for step in range(count)], count, 2), name="last_sum"
        )
    else:
        term = lax.psum_scatter(terms[0], "space", scatter_dimension=3, tiled=True)
        term = lax.psum_scatter(term, "dp", scatter_dimension=3, tiled=True).astype(f32)
        grad_first, grad_second = term[0], term[1]
    (grad_in,) = call(
        functools.partial(inverse_kernel, count, norm_scale / factor),
        [shape((slabs, cells, width), bf16)],
        [jnp.asarray(inverse), *backs],
        name="inverse",
    )
    return grad_in.reshape(grad_out.shape), grad_first, grad_second


def solution(mesh):
    in_specs = (
        P(("parts", "dp"), "space", None, None, "chan"),
        P(None, ("parts", "dp"), None, "space", None, "chan"),
        P("chan", None, None, None),
        P(None, "chan"),
        P("chan", None, None, None),
    )
    out_specs = (
        P(("parts", "dp"), "space", None, None, "chan"),
        P(("parts", "chan"), None, ("space", "dp"), None),
        P(("parts", "chan"), None, ("space", "dp"), None),
    )
    return jax.shard_map(body, mesh=mesh, in_specs=in_specs, out_specs=out_specs, check_vma=False)
```

time: 41.1 us -> 37 us (0.900)
  waiting for transfers between devices: 12.8 us -> 6.76 us
  starting transfers between devices: 20.1 us -> 21.9 us
    ppermute x10 -> x11, waiting for transfers between devices: 12.8 us -> 6.76 us  [the longest x9 6.22 us: spread(): moved.append(lax.ppermute(values[step], 'space', pairs))]
    ppermute x10 -> x11, starting transfers between devices: 20.1 us -> 21.9 us  [the longest x9 19.9 us: spread(): moved.append(lax.ppermute(values[step], 'space', pairs))]
    pallas_call x6 -> x8, Pallas kernels: 4.33 us -> 4.39 us  [call(): pl.pallas_call(kernel, out_shape=tuple(outs), in_specs=[whole] * (len(arg...]
    unnamed x14 -> x12, local copies, waits for them, and re-layouts: 2.95 us -> 2.95 us
  transfers between devices with their start and end apart: 10 -> 11, of which waited for: 5 -> 4; matrix products, arithmetic and copies ran while one was open for 0% -> 0% of each run, Pallas kernels for 5% -> 7%
where the time goes in v3:
time: 37 us; the launch traced here: 36.8 us
  starting transfers between devices  21.9 us (59%)
  waiting for transfers between devices  6.76 us (18%)
  Pallas kernels  4.39 us (12%)
  local copies, waits for them, and re-layouts  2.95 us (8%)
  between operations  0.71 us (2%)
    ppermute x9, starting transfers between devices, spread(): moved.append(lax.ppermute(values[step], 'space', pairs))  19.9 us
    ppermute x9, waiting for transfers between devices, spread(): moved.append(lax.ppermute(values[step], 'space', pairs))  6.22 us
    pallas_call x8, Pallas kernels, call(): pl.pallas_call(kernel, out_shape=tuple(outs), in_specs=[whole] * (len(arg...  4.39 us
    unnamed x12, local copies, waits for them, and re-layouts  2.95 us
    ppermute x2, starting transfers between devices, body(): got = [lax.ppermute(send, 'dp', [(0, 1), (1, 0)]) for send in sends]  2.09 us
  transfers between devices with their start and end apart: 11, of which 4 were waited for; matrix products, arithmetic and copies ran while one was open for 0% of the time, Pallas kernels for 7%

profile of v3, /device:TPU:0, one launch (start us, length us, event | category | flops | bytes accessed | tf_op | source)
XLA Modules:
  0.0 36.8 jit_solution(17111543661598838011)
XLA Ops:
  0.6 0.9 %copy-done.1 = bf16[1,1,16,16,512]{4,3,2,1,0:T(8,128)(2,1)S(1)} copy-done((bf16[1,1,16,16,512]{4,3,2,1,0:T(8,128)(2,1)S(1)}, bf16[1,1,16,16,512]{4,3,2,1,0:T(8,128)(2,1)}, u32[]{:S(2)}) %copy-start.1) | copy-done | bytes 262168
  1.6 0.5 %forward.1 = (bf16[1,128,512]{2,1,0:T(8,128)(2,1)S(1)}, bf16[1,128,512]{2,1,0:T(8,128)(2,1)S(1)}, bf16[1,128,512]{2,1,0:T(8,128)(2,1)S(1)}, bf16[1,128,512]{2,1,0:T(8,128)(2,1)S(1)}) custom-call(bf16[1,256,512]{2,1,0:T(8,128)(2,1)S(1)} %bitcast.4), custom_call_target="tpu_custom_call" | custom-call | tf_op jit(solution)/shard_map/forward/pallas_call | solution.py:271
  2.1 3.1 %collective-permute-start = (bf16[1,128,512]{2,1,0:T(8,128)(2,1)S(1)}, bf16[1,128,512]{2,1,0:T(8,128)(2,1)S(1)}, u32[]{:S(2)}, u32[]{:S(2)}) collective-permute-start(bf16[1,128,512]{2,1,0:T(8,128)(2,1)S(1)} %get-tuple-element.28), channel_id=1, source_target_pairs={{0,4},{4,8},{8,12},{12,0},{1,5},{5,9},{9,13},{13,1},{2,6},{6,10},{... | collective-permute-start | bytes 393224 | tf_op jit(solution)/shard_map/ppermute | solution.py:287
  5.2 2.6 %collective-permute-start.1 = (bf16[1,128,512]{2,1,0:T(8,128)(2,1)S(1)}, bf16[1,128,512]{2,1,0:T(8,128)(2,1)S(1)}, u32[]{:S(2)}, u32[]{:S(2)}) collective-permute-start(bf16[1,128,512]{2,1,0:T(8,128)(2,1)S(1)} %get-tuple-element.29), channel_id=1, source_target_pairs={{0,8},{4,12},{8,0},{12,4},{1,9},{5,13},{9,1},{13,5},{2,10},{6,14},... | collective-permute-start | bytes 393224 | tf_op jit(solution)/shard_map/ppermute | solution.py:287
  7.8 1.3 %collective-permute-start.2 = (bf16[1,128,512]{2,1,0:T(8,128)(2,1)S(1)}, bf16[1,128,512]{2,1,0:T(8,128)(2,1)S(1)}, u32[]{:S(2)}, u32[]{:S(2)}) collective-permute-start(bf16[1,128,512]{2,1,0:T(8,128)(2,1)S(1)} %get-tuple-element.30), channel_id=1, source_target_pairs={{0,12},{4,0},{8,4},{12,8},{1,13},{5,1},{9,5},{13,9},{2,14},{6,2},{... | collective-permute-start | bytes 393224 | tf_op jit(solution)/shard_map/ppermute | solution.py:287
  9.1 1.0 %copy-done = bf16[2,1,4,4,16,512]{5,4,3,2,1,0:T(8,128)(2,1)S(1)} copy-done((bf16[2,1,4,4,16,512]{5,4,3,2,1,0:T(8,128)(2,1)S(1)}, bf16[2,1,4,4,16,512]{5,4,3,2,1,0:T(8,128)(2,1)}, u32[]{:S(2)}) %copy-start) | copy-done | bytes 524312
  10.1 0.9 %copy-done.3 = bf16[4,2,128,128]{3,2,1,0:T(8,128)(2,1)S(1)} copy-done((bf16[4,2,128,128]{3,2,1,0:T(8,128)(2,1)S(1)}, bf16[4,2,128,128]{3,2,1,0:T(8,128)(2,1)}, u32[]{:S(2)}) %copy-start.3) | copy-done | bytes 262168
  11.1 0.8 %activation.1 = (bf16[4,256,256]{2,1,0:T(8,128)(2,1)S(1)}, bf16[4,256,256]{2,1,0:T(8,128)(2,1)S(1)}, f32[4,256,256]{2,1,0:T(8,128)S(1)}, bf16[4,256,256]{2,1,0:T(8,128)(2,1)S(1)}, bf16[4,256,256]{2,1,0:T(8,128)(2,1)S(1)}) custom-call(bf16[2,256,512]{2,1,0:T(8,128)(2,1)S(1)} %bitcast.3, bf16[4,2,128,128]{3,2,1,0:T(8,128)(2,1)S(1)} %copy-done.2, ...), custom_call_target="tpu_custom_call" | custom-call | tf_op jit(solution)/shard_map/activation/pallas_call | solution.py:271
  11.9 4.5 %collective-permute-done.1.refs_2_ = bf16[1,128,512]{2,1,0:T(8,128)(2,1)S(1)} collective-permute-done((bf16[1,128,512]{2,1,0:T(8,128)(2,1)S(1)}, bf16[1,128,512]{2,1,0:T(8,128)(2,1)S(1)}, u32[]{:S(2)}, u32[]{:S(2)}) %collective-permute-start.1) | collective-permute-done | bytes 131104 | tf_op jit(solution)/shard_map/ppermute | solution.py:287
  16.4 0.7 %filter.1 = (bf16[1,128,512]{2,1,0:T(8,128)(2,1)S(1)}, bf16[1,128,512]{2,1,0:T(8,128)(2,1)S(1)}, bf16[1,128,512]{2,1,0:T(8,128)(2,1)S(1)}, bf16[1,128,512]{2,1,0...) custom-call(bf16[1,128,512]{2,1,0:T(8,128)(2,1)S(1)} %get-tuple-element.27.refs_0_, ...), custom_call_target="tpu_custom_call" | custom-call | tf_op jit(solution)/shard_map/filter/pallas_call | solution.py:271
  17.2 2.3 %collective-permute-start.4 = (bf16[1,128,512]{2,1,0:T(8,128)(2,1)S(1)}, bf16[1,128,512]{2,1,0:T(8,128)(2,1)S(1)}, u32[]{:S(2)}, u32[]{:S(2)}) collective-permute-start(bf16[1,128,512]{2,1,0:T(8,128)(2,1)S(1)} %get-tuple-element.36), channel_id=1, source_target_pairs={{0,8},{4,12},{8,0},{12,4},{1,9},{5,13},{9,1},{13,5},{2,10},{6,14},... | collective-permute-start | bytes 393224 | tf_op jit(solution)/shard_map/ppermute | solution.py:287
  19.5 0.5 %weight.1 = (f32[4,64,512]{2,1,0:T(8,128)S(1)}, bf16[2,64,512]{2,1,0:T(8,128)(2,1)S(1)}, bf16[2,64,512]{2,1,0:T(8,128)(2,1)S(1)}) custom-call(bf16[4,256,256]{2,1,0:T(8,128)(2,1)S(1)} %get-tuple-element.38.act_ref, bf16[4,256,256]{2,1,0:T(8,128)(2,1)S(1)} %get-tuple-element.39.flip_ref, bf16[4,256,256]{2,1,0:T(8,128)(2,1)S(1)} %get-tuple-element.40.value_ref, ...), custom_call_target="tpu_custom_call" | custom-call | tf_op jit(solution)/shard_map/weight/pallas_call | solution.py:271
  20.0 1.6 %collective-permute-start.6 = (bf16[2,64,512]{2,1,0:T(8,128)(2,1)S(1)}, bf16[2,64,512]{2,1,0:T(8,128)(2,1)S(1)}, u32[]{:S(2)}, u32[]{:S(2)}) collective-permute-start(bf16[2,64,512]{2,1,0:T(8,128)(2,1)S(1)} %get-tuple-element.43), channel_id=1, source_target_pairs={{0,2},{2,0},{1,3},{3,1},{4,6},{6,4},{5,7},{7,5},{8,10},{10,8},{9,1... | collective-permute-start | bytes 393224 | tf_op jit(solution)/shard_map/ppermute | solution.py:363
  21.5 0.5 %collective-permute-start.8 = (bf16[2,64,512]{2,1,0:T(8,128)(2,1)S(1)}, bf16[2,64,512]{2,1,0:T(8,128)(2,1)S(1)}, u32[]{:S(2)}, u32[]{:S(2)}) collective-permute-start(bf16[2,64,512]{2,1,0:T(8,128)(2,1)S(1)} %get-tuple-element.46), channel_id=1, source_target_pairs={{0,2},{2,0},{1,3},{3,1},{4,6},{6,4},{5,7},{7,5},{8,10},{10,8},{9,1... | collective-permute-start | bytes 393224 | tf_op jit(solution)/shard_map/ppermute | solution.py:363
  22.1 2.6 %collective-permute-start.3 = (bf16[1,128,512]{2,1,0:T(8,128)(2,1)S(1)}, bf16[1,128,512]{2,1,0:T(8,128)(2,1)S(1)}, u32[]{:S(2)}, u32[]{:S(2)}) collective-permute-start(bf16[1,128,512]{2,1,0:T(8,128)(2,1)S(1)} %get-tuple-element.35), channel_id=1, source_target_pairs={{0,4},{4,8},{8,12},{12,0},{1,5},{5,9},{9,13},{13,1},{2,6},{6,10},{... | collective-permute-start | bytes 393224 | tf_op jit(solution)/shard_map/ppermute | solution.py:287
  24.7 1.2 %collective-permute-start.5 = (bf16[1,128,512]{2,1,0:T(8,128)(2,1)S(1)}, bf16[1,128,512]{2,1,0:T(8,128)(2,1)S(1)}, u32[]{:S(2)}, u32[]{:S(2)}) collective-permute-start(bf16[1,128,512]{2,1,0:T(8,128)(2,1)S(1)} %get-tuple-element.37), channel_id=1, source_target_pairs={{0,12},{4,0},{8,4},{12,8},{1,13},{5,1},{9,5},{13,9},{2,14},{6,2},{... | collective-permute-start | bytes 393224 | tf_op jit(solution)/shard_map/ppermute | solution.py:287
  25.9 0.5 %collective-permute-done.6.got_ref = bf16[2,64,512]{2,1,0:T(8,128)(2,1)S(1)} collective-permute-done((bf16[2,64,512]{2,1,0:T(8,128)(2,1)S(1)}, bf16[2,64,512]{2,1,0:T(8,128)(2,1)S(1)}, u32[]{:S(2)}, u32[]{:S(2)}) %collective-permute-start.6) | collective-permute-done | bytes 131104 | tf_op jit(solution)/shard_map/ppermute | solution.py:363
  26.5 1.8 %collective-permute-start.7 = (bf16[64,512]{1,0:T(8,128)(2,1)S(1)}, bf16[64,512]{1,0:T(8,128)(2,1)S(1)}, u32[]{:S(2)}, u32[]{:S(2)}) collective-permute-start(bf16[64,512]{1,0:T(8,128)(2,1)S(1)} %get-tuple-element.45), channel_id=1, source_target_pairs={{0,4},{4,12},{12,8},{8,0},{1,5},{5,13},{13,9},{9,1},{2,6},{6,14},{... | collective-permute-start | bytes 196616 | tf_op jit(solution)/shard_map/ppermute | solution.py:287
  28.3 3.1 %collective-permute-start.9 = (bf16[64,512]{1,0:T(8,128)(2,1)S(1)}, bf16[64,512]{1,0:T(8,128)(2,1)S(1)}, u32[]{:S(2)}, u32[]{:S(2)}) collective-permute-start(bf16[64,512]{1,0:T(8,128)(2,1)S(1)} %get-tuple-element.47), channel_id=1, source_target_pairs={{0,12},{4,8},{12,0},{8,4},{1,13},{5,9},{13,1},{9,5},{2,14},{6,10},... | collective-permute-start | bytes 196616 | tf_op jit(solution)/shard_map/ppermute | solution.py:287
  31.5 1.7 %collective-permute-start.10 = (bf16[64,512]{1,0:T(8,128)(2,1)S(1)}, bf16[64,512]{1,0:T(8,128)(2,1)S(1)}, u32[]{:S(2)}, u32[]{:S(2)}) collective-permute-start(bf16[64,512]{1,0:T(8,128)(2,1)S(1)} %get-tuple-element.48), channel_id=1, source_target_pairs={{0,8},{4,0},{12,4},{8,12},{1,9},{5,1},{13,5},{9,13},{2,10},{6,2},{... | collective-permute-start | bytes 196616 | tf_op jit(solution)/shard_map/ppermute | solution.py:287
  33.2 1.1 %inverse.1 = bf16[1,256,512]{2,1,0:T(8,128)(2,1)} custom-call(bf16[4,256,128]{2,1,0:T(8,128)(2,1)S(1)} %copy-done.4, bf16[1,128,512]{2,1,0:T(8,128)(2,1)S(1)} %get-tuple-element.34.refs_0_, bf16[1,128,512]{2,1,0:T(8,128)(2,1)S(1)} %collective-permute-done.3.refs_1_, bf16[1,128,512]{2,1,0:T(8,128)(2,1)S(1)} %collective-permute-done.4.refs_2_.refs_0_, ...), custom_call_target="tpu_custom_call" | custom-call | tf_op jit(solution)/shard_map/inverse/pallas_call | solution.py:271
  34.4 1.1 %collective-permute-done.7.refs_1_ = bf16[64,512]{1,0:T(8,128)(2,1)S(1)} collective-permute-done((bf16[64,512]{1,0:T(8,128)(2,1)S(1)}, bf16[64,512]{1,0:T(8,128)(2,1)S(1)}, u32[]{:S(2)}, u32[]{:S(2)}) %collective-permute-start.7) | collective-permute-done | bytes 65568 | tf_op jit(solution)/shard_map/ppermute | solution.py:287
  35.5 0.6 %collective-permute-done.10.refs_3_ = bf16[64,512]{1,0:T(8,128)(2,1)S(1)} collective-permute-done((bf16[64,512]{1,0:T(8,128)(2,1)S(1)}, bf16[64,512]{1,0:T(8,128)(2,1)S(1)}, u32[]{:S(2)}, u32[]{:S(2)}) %collective-permute-start.10) | collective-permute-done | bytes 65568 | tf_op jit(solution)/shard_map/ppermute | solution.py:287
  36.1 0.7 %last_sum.1 = (f32[4,2,16,128]{3,2,1,0:T(8,128)}, f32[4,2,16,128]{3,2,1,0:T(8,128)}) custom-call(f32[64,512]{1,0:T(8,128)S(1)} %get-tuple-element.44.refs_0_, bf16[64,512]{1,0:T(8,128)(2,1)S(1)} %collective-permute-done.7.refs_1_, bf16[64,512]{1,0:T(8,128)(2,1)S(1)} %collective-permute-done.9.refs_2_, bf16[64,512]{1,0:T(8,128)(2,1)S(1)} %collective-permute-done.10.refs_3_), custom_call_target="tpu_custom_call" | custom-call | tf_op jit(solution)/shard_map/last_sum/pallas_call | solution.py:271
  (18 shorter events, 0.1 us)
Async XLA Ops:
  0.6 1.0 %copy-start.1 = (bf16[1,1,16,16,512]{4,3,2,1,0:T(8,128)(2,1)S(1)}, bf16[1,1,16,16,512]{4,3,2,1,0:T(8,128)(2,1)}, u32[]{:S(2)}) copy-start(bf16[1,1,16,16,512]{4,3,2,1,0:T(8,128)(2,1)} %param.6) | copy-start | bytes 786436
  1.6 7.5 %copy-start.2 = (bf16[4,2,128,128]{3,2,1,0:T(8,128)(2,1)S(1)}, bf16[4,2,128,128]{3,2,1,0:T(8,128)(2,1)}, u32[]{:S(2)}) copy-start(bf16[4,2,128,128]{3,2,1,0:T(8,128)(2,1)} %first_ref.1) | copy-start | bytes 786436
  2.1 9.8 %collective-permute-start = (bf16[1,128,512]{2,1,0:T(8,128)(2,1)S(1)}, bf16[1,128,512]{2,1,0:T(8,128)(2,1)S(1)}, u32[]{:S(2)}, u32[]{:S(2)}) collective-permute-start(bf16[1,128,512]{2,1,0:T(8,128)(2,1)S(1)} %get-tuple-element.28), channel_id=1, source_target_pairs={{0,4},{4,8},{8,12},{12,0},{1,5},{5,9},{9,13},{13,1},{2,6},{6,10},{... | collective-permute-start | bytes 393224 | tf_op jit(solution)/shard_map/ppermute | solution.py:287
  5.2 3.9 %copy-start.5 = (bf16[2,512]{1,0:T(2,128)(2,1)S(1)}, bf16[2,512]{1,0:T(2,128)(2,1)}, u32[]{:S(2)}) copy-start(bf16[2,512]{1,0:T(2,128)(2,1)} %bias_ref.1) | copy-start | bytes 6148
  5.2 11.2 %collective-permute-start.1 = (bf16[1,128,512]{2,1,0:T(8,128)(2,1)S(1)}, bf16[1,128,512]{2,1,0:T(8,128)(2,1)S(1)}, u32[]{:S(2)}, u32[]{:S(2)}) collective-permute-start(bf16[1,128,512]{2,1,0:T(8,128)(2,1)S(1)} %get-tuple-element.29), channel_id=1, source_target_pairs={{0,8},{4,12},{8,0},{12,4},{1,9},{5,13},{9,1},{13,5},{2,10},{6,14},... | collective-permute-start | bytes 393224 | tf_op jit(solution)/shard_map/ppermute | solution.py:287
  7.8 8.7 %collective-permute-start.2 = (bf16[1,128,512]{2,1,0:T(8,128)(2,1)S(1)}, bf16[1,128,512]{2,1,0:T(8,128)(2,1)S(1)}, u32[]{:S(2)}, u32[]{:S(2)}) collective-permute-start(bf16[1,128,512]{2,1,0:T(8,128)(2,1)S(1)} %get-tuple-element.30), channel_id=1, source_target_pairs={{0,12},{4,0},{8,4},{12,8},{1,13},{5,1},{9,5},{13,9},{2,14},{6,2},{... | collective-permute-start | bytes 393224 | tf_op jit(solution)/shard_map/ppermute | solution.py:287
  9.1 1.0 %copy-start = (bf16[2,1,4,4,16,512]{5,4,3,2,1,0:T(8,128)(2,1)S(1)}, bf16[2,1,4,4,16,512]{5,4,3,2,1,0:T(8,128)(2,1)}, u32[]{:S(2)}) copy-start(bf16[2,1,4,4,16,512]{5,4,3,2,1,0:T(8,128)(2,1)} %param.7) | copy-start | bytes 1572868
  10.1 0.9 %copy-start.3 = (bf16[4,2,128,128]{3,2,1,0:T(8,128)(2,1)S(1)}, bf16[4,2,128,128]{3,2,1,0:T(8,128)(2,1)}, u32[]{:S(2)}) copy-start(bf16[4,2,128,128]{3,2,1,0:T(8,128)(2,1)} %second_ref.1) | copy-start | bytes 786436
  17.2 8.7 %collective-permute-start.4 = (bf16[1,128,512]{2,1,0:T(8,128)(2,1)S(1)}, bf16[1,128,512]{2,1,0:T(8,128)(2,1)S(1)}, u32[]{:S(2)}, u32[]{:S(2)}) collective-permute-start(bf16[1,128,512]{2,1,0:T(8,128)(2,1)S(1)} %get-tuple-element.36), channel_id=1, source_target_pairs={{0,8},{4,12},{8,0},{12,4},{1,9},{5,13},{9,1},{13,5},{2,10},{6,14},... | collective-permute-start | bytes 393224 | tf_op jit(solution)/shard_map/ppermute | solution.py:287
  20.0 6.5 %collective-permute-start.6 = (bf16[2,64,512]{2,1,0:T(8,128)(2,1)S(1)}, bf16[2,64,512]{2,1,0:T(8,128)(2,1)S(1)}, u32[]{:S(2)}, u32[]{:S(2)}) collective-permute-start(bf16[2,64,512]{2,1,0:T(8,128)(2,1)S(1)} %get-tuple-element.43), channel_id=1, source_target_pairs={{0,2},{2,0},{1,3},{3,1},{4,6},{6,4},{5,7},{7,5},{8,10},{10,8},{9,1... | collective-permute-start | bytes 393224 | tf_op jit(solution)/shard_map/ppermute | solution.py:363
  21.5 6.8 %collective-permute-start.8 = (bf16[2,64,512]{2,1,0:T(8,128)(2,1)S(1)}, bf16[2,64,512]{2,1,0:T(8,128)(2,1)S(1)}, u32[]{:S(2)}, u32[]{:S(2)}) collective-permute-start(bf16[2,64,512]{2,1,0:T(8,128)(2,1)S(1)} %get-tuple-element.46), channel_id=1, source_target_pairs={{0,2},{2,0},{1,3},{3,1},{4,6},{6,4},{5,7},{7,5},{8,10},{10,8},{9,1... | collective-permute-start | bytes 393224 | tf_op jit(solution)/shard_map/ppermute | solution.py:363
  22.1 11.1 %collective-permute-start.3 = (bf16[1,128,512]{2,1,0:T(8,128)(2,1)S(1)}, bf16[1,128,512]{2,1,0:T(8,128)(2,1)S(1)}, u32[]{:S(2)}, u32[]{:S(2)}) collective-permute-start(bf16[1,128,512]{2,1,0:T(8,128)(2,1)S(1)} %get-tuple-element.35), channel_id=1, source_target_pairs={{0,4},{4,8},{8,12},{12,0},{1,5},{5,9},{9,13},{13,1},{2,6},{6,10},{... | collective-permute-start | bytes 393224 | tf_op jit(solution)/shard_map/ppermute | solution.py:287
  24.7 8.5 %collective-permute-start.5 = (bf16[1,128,512]{2,1,0:T(8,128)(2,1)S(1)}, bf16[1,128,512]{2,1,0:T(8,128)(2,1)S(1)}, u32[]{:S(2)}, u32[]{:S(2)}) collective-permute-start(bf16[1,128,512]{2,1,0:T(8,128)(2,1)S(1)} %get-tuple-element.37), channel_id=1, source_target_pairs={{0,12},{4,0},{8,4},{12,8},{1,13},{5,1},{9,5},{13,9},{2,14},{6,2},{... | collective-permute-start | bytes 393224 | tf_op jit(solution)/shard_map/ppermute | solution.py:287
  26.5 6.8 %copy-start.4 = (bf16[4,256,128]{2,1,0:T(8,128)(2,1)S(1)}, bf16[4,256,128]{2,1,0:T(8,128)(2,1)}, u32[]{:S(2)}) copy-start(bf16[4,256,128]{2,1,0:T(8,128)(2,1)} %constant.2.clone.table_ref) | copy-start | bytes 786436
  26.5 9.0 %collective-permute-start.7 = (bf16[64,512]{1,0:T(8,128)(2,1)S(1)}, bf16[64,512]{1,0:T(8,128)(2,1)S(1)}, u32[]{:S(2)}, u32[]{:S(2)}) collective-permute-start(bf16[64,512]{1,0:T(8,128)(2,1)S(1)} %get-tuple-element.45), channel_id=1, source_target_pairs={{0,4},{4,12},{12,8},{8,0},{1,5},{5,13},{13,9},{9,1},{2,6},{6,14},{... | collective-permute-start | bytes 196616 | tf_op jit(solution)/shard_map/ppermute | solution.py:287
  28.3 7.1 %collective-permute-start.9 = (bf16[64,512]{1,0:T(8,128)(2,1)S(1)}, bf16[64,512]{1,0:T(8,128)(2,1)S(1)}, u32[]{:S(2)}, u32[]{:S(2)}) collective-permute-start(bf16[64,512]{1,0:T(8,128)(2,1)S(1)} %get-tuple-element.47), channel_id=1, source_target_pairs={{0,12},{4,8},{12,0},{8,4},{1,13},{5,9},{13,1},{9,5},{2,14},{6,10},... | collective-permute-start | bytes 196616 | tf_op jit(solution)/shard_map/ppermute | solution.py:287
  31.5 4.6 %collective-permute-start.10 = (bf16[64,512]{1,0:T(8,128)(2,1)S(1)}, bf16[64,512]{1,0:T(8,128)(2,1)S(1)}, u32[]{:S(2)}, u32[]{:S(2)}) collective-permute-start(bf16[64,512]{1,0:T(8,128)(2,1)S(1)} %get-tuple-element.48), channel_id=1, source_target_pairs={{0,8},{4,0},{12,4},{8,12},{1,9},{5,1},{13,5},{9,13},{2,10},{6,2},{... | collective-permute-start | bytes 196616 | tf_op jit(solution)/shard_map/ppermute | solution.py:287

commit v4 on v3

--- a/solution.py
+++ b/solution.py
@@ -96,20 +96,16 @@
     return jnp.cos(angle), jnp.sin(angle)
 
 
-RING = (0, 0, 1)
-EARLY = (2, 3)
-AFTER = 1
-TIE = 2
-
-
-def ring_order(count, phase):
-    if not RING[phase]:
+def ring(count, folded):
+    if not folded:
         return list(range(count))
     return [0] + list(range(1, count, 2)) + list(range(count - 2 + count % 2, 0, -2))
 
 
-def neighbour(me, step, count, phase):
-    order = ring_order(count, phase)
+def neighbour(me, step, count, folded=False):
+    order = ring(count, folded)
+    if not folded:
+        return lax.rem(me + step + count, count)
     home = jnp.int32(0)
     for at, here in enumerate(order):
         home = jnp.where(me == here, order[(at + step) % count], home)
@@ -133,7 +129,7 @@
             -(cos_z * sin_k) - sin_z * cos_k
         ).astype(bf16)
     for step, out_ref in enumerate(out_refs):
-        table = table_ref[neighbour(me, step, count, 0)]
+        table = table_ref[neighbour(me, step, count)]
         for plane in range(planes):
             product = jnp.dot(table, cell_ref[plane], preferred_element_type=f32) * (1.0 / factor)
             out_ref[plane] = product.astype(bf16)
@@ -169,7 +165,7 @@
     length_x = count * planes
     tile = 16 if rows % 16 == 0 else rows
     for step, part_ref in enumerate(part_refs):
-        home = neighbour(me, -step, count, 0)
+        home = neighbour(me, -step, count)
         for sample in range(samples):
             for plane in range(planes):
                 pencil[sample, home * planes + plane] = part_ref[sample * planes + plane]
@@ -202,7 +198,7 @@
                     returned[sample, x, start : start + tile, lanes] = real.astype(bf16)
                     returned[sample, x, rows + start : rows + start + tile, lanes] = imag.astype(bf16)
     for step, back_ref in enumerate(back_refs):
-        home = neighbour(me, step, count, 1)
+        home = neighbour(me, step, count)
         for sample in range(samples):
             for plane in range(planes):
                 back_ref[sample * planes + plane] = returned[sample, home * planes + plane]
@@ -231,7 +227,7 @@
         me = lax.axis_index("space")
         for steps, out_ref in zip(groups, term_refs[1:-1]):
             for slot, step in enumerate(steps):
-                out_ref[slot] = term_refs[-1][neighbour(me, step, count, 2)]
+                out_ref[slot] = term_refs[-1][neighbour(me, step, count, True)]
 
 
 def inverse_kernel(count, scale, table_ref, *refs):
@@ -240,7 +236,7 @@
     for plane in range(out_ref.shape[0]):
         total = None
         for step, back_ref in enumerate(back_refs):
-            table = table_ref[neighbour(me, -step, count, 1)]
+            table = table_ref[neighbour(me, -step, count)]
             product = jnp.dot(table, back_ref[plane], preferred_element_type=f32)
             total = product if total is None else total + product
         out_ref[plane] = (total * scale).astype(bf16)
@@ -250,7 +246,7 @@
     me = lax.axis_index("space")
     for slot, step in enumerate(steps):
         out_ref = refs[len(refs) - len(steps) + slot]
-        out_ref[...] = (keep_ref[neighbour(me, step, count, 2)] + got_ref[slot].astype(f32)).astype(out_ref.dtype)
+        out_ref[...] = (keep_ref[neighbour(me, step, count, True)] + got_ref[slot].astype(f32)).astype(out_ref.dtype)
 
 
 def last_sum_kernel(*refs):
@@ -279,8 +275,8 @@
     )(*args)
 
 
-def spread(values, count, phase):
-    order = ring_order(count, phase)
+def spread(values, count, folded=False):
+    order = ring(count, folded)
     moved = []
     for step in range(1, count):
         pairs = [(order[at], order[(at + step) % count]) for at in range(count)]
@@ -301,7 +297,7 @@
     norm_scale = 1.0 / math.sqrt(length_x * cells)
     grad_scale = 1.0 / math.sqrt(length_x * cells * samples * pair)
     piece = block // (pair * count)
-    exchange = pair == 2 and piece * pair * count == block and piece % 16 == 0
+    exchange = pair == 2 and count > 1 and piece * pair * count == block and piece % 16 == 0
     inverse, factor = inverse_table(length_y, length_z, count)
     shape = jax.ShapeDtypeStruct
     slab = shape((slabs, 2 * rows, width), bf16)
@@ -318,7 +314,6 @@
             name="forward",
         ),
         count,
-        0,
     )
     act, flip, slope, first_back, second_back = call(
         activation_kernel,
@@ -344,9 +339,9 @@
         ],
         name="filter",
     )
-    backs = spread(backs, count, 1)
-    early = EARLY if count == 4 else tuple(range(1, count // 2 + 1))
-    groups = (early, (0,) + tuple(step for step in range(1, count) if step not in early))
+    backs = spread(backs, count)
+    half = count // 2
+    groups = (tuple(range(half, count)), tuple(range(half)))
     if exchange:
         terms = [shape((count, 4 * piece, width), f32)]
         terms += [shape((len(steps), 4 * piece, width), bf16) for steps in groups]
@@ -363,7 +358,7 @@
         got = [lax.ppermute(send, "dp", [(0, 1), (1, 0)]) for send in sends]
         sums = {}
         for at, steps in enumerate(groups):
-            after = [backs[TIE]] if at == AFTER else []
+            after = [backs[half]] if at == 1 else []
             outs = call(
                 functools.partial(pair_sum_kernel, count, steps),
                 [shape((4 * piece, width), bf16 if step else f32) for step in steps],
@@ -373,7 +368,7 @@
             )
             sums.update(zip(steps, outs))
         grad_first, grad_second = call(
-            last_sum_kernel, [shape((blocks, 2, piece, block), f32)] * 2, spread([sums[step] for step in range(count)], count, 2), name="last_sum"
+            last_sum_kernel, [shape((blocks, 2, piece, block), f32)] * 2, spread([sums[step] for step in range(count)], count, True), name="last_sum"
         )
     else:
         term = lax.psum_scatter(terms[0], "space", scatter_dimension=3, tiled=True)

time: 37 us -> 37 us (level)
  no operation moved by 1% of the time
where the time goes in v4:
time: 37 us; the launch traced here: 36.8 us
  starting transfers between devices  21.9 us (59%)
  waiting for transfers between devices  6.77 us (18%)
  Pallas kernels  4.39 us (12%)
  local copies, waits for them, and re-layouts  2.95 us (8%)
  between operations  0.71 us (2%)
    ppermute x9, starting transfers between devices, spread(): moved.append(lax.ppermute(values[step], 'space', pairs))  19.8 us
    ppermute x9, waiting for transfers between devices, spread(): moved.append(lax.ppermute(values[step], 'space', pairs))  6.22 us
    pallas_call x8, Pallas kernels, call(): pl.pallas_call(kernel, out_shape=tuple(outs), in_specs=[whole] * (len(arg...  4.39 us
    unnamed x12, local copies, waits for them, and re-layouts  2.95 us
    ppermute x2, starting transfers between devices, body(): got = [lax.ppermute(send, 'dp', [(0, 1), (1, 0)]) for send in sends]  2.09 us
  transfers between devices with their start and end apart: 11, of which 4 were waited for; matrix products, arithmetic and copies ran while one was open for 0% of the time, Pallas kernels for 7%

profile of v4, /device:TPU:0, one launch (start us, length us, event | category | flops | bytes accessed | tf_op | source)
XLA Modules:
  0.0 36.8 jit_solution(6615330453214630020)
XLA Ops:
  0.6 0.9 %copy-done.1 = bf16[1,1,16,16,512]{4,3,2,1,0:T(8,128)(2,1)S(1)} copy-done((bf16[1,1,16,16,512]{4,3,2,1,0:T(8,128)(2,1)S(1)}, bf16[1,1,16,16,512]{4,3,2,1,0:T(8,128)(2,1)}, u32[]{:S(2)}) %copy-start.1) | copy-done | bytes 262168
  1.6 0.5 %forward.1 = (bf16[1,128,512]{2,1,0:T(8,128)(2,1)S(1)}, bf16[1,128,512]{2,1,0:T(8,128)(2,1)S(1)}, bf16[1,128,512]{2,1,0:T(8,128)(2,1)S(1)}, bf16[1,128,512]{2,1,0:T(8,128)(2,1)S(1)}) custom-call(bf16[1,256,512]{2,1,0:T(8,128)(2,1)S(1)} %bitcast.4), custom_call_target="tpu_custom_call" | custom-call | tf_op jit(solution)/shard_map/forward/pallas_call | solution.py:267
  2.1 3.1 %collective-permute-start = (bf16[1,128,512]{2,1,0:T(8,128)(2,1)S(1)}, bf16[1,128,512]{2,1,0:T(8,128)(2,1)S(1)}, u32[]{:S(2)}, u32[]{:S(2)}) collective-permute-start(bf16[1,128,512]{2,1,0:T(8,128)(2,1)S(1)} %get-tuple-element.28), channel_id=1, source_target_pairs={{0,4},{4,8},{8,12},{12,0},{1,5},{5,9},{9,13},{13,1},{2,6},{6,10},{... | collective-permute-start | bytes 393224 | tf_op jit(solution)/shard_map/ppermute | solution.py:283
  5.2 2.6 %collective-permute-start.1 = (bf16[1,128,512]{2,1,0:T(8,128)(2,1)S(1)}, bf16[1,128,512]{2,1,0:T(8,128)(2,1)S(1)}, u32[]{:S(2)}, u32[]{:S(2)}) collective-permute-start(bf16[1,128,512]{2,1,0:T(8,128)(2,1)S(1)} %get-tuple-element.29), channel_id=1, source_target_pairs={{0,8},{4,12},{8,0},{12,4},{1,9},{5,13},{9,1},{13,5},{2,10},{6,14},... | collective-permute-start | bytes 393224 | tf_op jit(solution)/shard_map/ppermute | solution.py:283
  7.8 1.3 %collective-permute-start.2 = (bf16[1,128,512]{2,1,0:T(8,128)(2,1)S(1)}, bf16[1,128,512]{2,1,0:T(8,128)(2,1)S(1)}, u32[]{:S(2)}, u32[]{:S(2)}) collective-permute-start(bf16[1,128,512]{2,1,0:T(8,128)(2,1)S(1)} %get-tuple-element.30), channel_id=1, source_target_pairs={{0,12},{4,0},{8,4},{12,8},{1,13},{5,1},{9,5},{13,9},{2,14},{6,2},{... | collective-permute-start | bytes 393224 | tf_op jit(solution)/shard_map/ppermute | solution.py:283
  9.1 1.0 %copy-done = bf16[2,1,4,4,16,512]{5,4,3,2,1,0:T(8,128)(2,1)S(1)} copy-done((bf16[2,1,4,4,16,512]{5,4,3,2,1,0:T(8,128)(2,1)S(1)}, bf16[2,1,4,4,16,512]{5,4,3,2,1,0:T(8,128)(2,1)}, u32[]{:S(2)}) %copy-start) | copy-done | bytes 524312
  10.1 0.9 %copy-done.3 = bf16[4,2,128,128]{3,2,1,0:T(8,128)(2,1)S(1)} copy-done((bf16[4,2,128,128]{3,2,1,0:T(8,128)(2,1)S(1)}, bf16[4,2,128,128]{3,2,1,0:T(8,128)(2,1)}, u32[]{:S(2)}) %copy-start.3) | copy-done | bytes 262168
  11.1 0.8 %activation.1 = (bf16[4,256,256]{2,1,0:T(8,128)(2,1)S(1)}, bf16[4,256,256]{2,1,0:T(8,128)(2,1)S(1)}, f32[4,256,256]{2,1,0:T(8,128)S(1)}, bf16[4,256,256]{2,1,0:T(8,128)(2,1)S(1)}, bf16[4,256,256]{2,1,0:T(8,128)(2,1)S(1)}) custom-call(bf16[2,256,512]{2,1,0:T(8,128)(2,1)S(1)} %bitcast.3, bf16[4,2,128,128]{3,2,1,0:T(8,128)(2,1)S(1)} %copy-done.2, ...), custom_call_target="tpu_custom_call" | custom-call | tf_op jit(solution)/shard_map/activation/pallas_call | solution.py:267
  11.9 4.5 %collective-permute-done.1.refs_2_ = bf16[1,128,512]{2,1,0:T(8,128)(2,1)S(1)} collective-permute-done((bf16[1,128,512]{2,1,0:T(8,128)(2,1)S(1)}, bf16[1,128,512]{2,1,0:T(8,128)(2,1)S(1)}, u32[]{:S(2)}, u32[]{:S(2)}) %collective-permute-start.1) | collective-permute-done | bytes 131104 | tf_op jit(solution)/shard_map/ppermute | solution.py:283
  16.4 0.7 %filter.1 = (bf16[1,128,512]{2,1,0:T(8,128)(2,1)S(1)}, bf16[1,128,512]{2,1,0:T(8,128)(2,1)S(1)}, bf16[1,128,512]{2,1,0:T(8,128)(2,1)S(1)}, bf16[1,128,512]{2,1,0...) custom-call(bf16[1,128,512]{2,1,0:T(8,128)(2,1)S(1)} %get-tuple-element.27.refs_0_, ...), custom_call_target="tpu_custom_call" | custom-call | tf_op jit(solution)/shard_map/filter/pallas_call | solution.py:267
  17.2 2.3 %collective-permute-start.4 = (bf16[1,128,512]{2,1,0:T(8,128)(2,1)S(1)}, bf16[1,128,512]{2,1,0:T(8,128)(2,1)S(1)}, u32[]{:S(2)}, u32[]{:S(2)}) collective-permute-start(bf16[1,128,512]{2,1,0:T(8,128)(2,1)S(1)} %get-tuple-element.36), channel_id=1, source_target_pairs={{0,8},{4,12},{8,0},{12,4},{1,9},{5,13},{9,1},{13,5},{2,10},{6,14},... | collective-permute-start | bytes 393224 | tf_op jit(solution)/shard_map/ppermute | solution.py:283
  19.5 0.5 %weight.1 = (f32[4,64,512]{2,1,0:T(8,128)S(1)}, bf16[2,64,512]{2,1,0:T(8,128)(2,1)S(1)}, bf16[2,64,512]{2,1,0:T(8,128)(2,1)S(1)}) custom-call(bf16[4,256,256]{2,1,0:T(8,128)(2,1)S(1)} %get-tuple-element.38.act_ref, bf16[4,256,256]{2,1,0:T(8,128)(2,1)S(1)} %get-tuple-element.39.flip_ref, bf16[4,256,256]{2,1,0:T(8,128)(2,1)S(1)} %get-tuple-element.40.value_ref, ...), custom_call_target="tpu_custom_call" | custom-call | tf_op jit(solution)/shard_map/weight/pallas_call | solution.py:267
  20.0 1.6 %collective-permute-start.6 = (bf16[2,64,512]{2,1,0:T(8,128)(2,1)S(1)}, bf16[2,64,512]{2,1,0:T(8,128)(2,1)S(1)}, u32[]{:S(2)}, u32[]{:S(2)}) collective-permute-start(bf16[2,64,512]{2,1,0:T(8,128)(2,1)S(1)} %get-tuple-element.43), channel_id=1, source_target_pairs={{0,2},{2,0},{1,3},{3,1},{4,6},{6,4},{5,7},{7,5},{8,10},{10,8},{9,1... | collective-permute-start | bytes 393224 | tf_op jit(solution)/shard_map/ppermute | solution.py:358
  21.5 0.5 %collective-permute-start.8 = (bf16[2,64,512]{2,1,0:T(8,128)(2,1)S(1)}, bf16[2,64,512]{2,1,0:T(8,128)(2,1)S(1)}, u32[]{:S(2)}, u32[]{:S(2)}) collective-permute-start(bf16[2,64,512]{2,1,0:T(8,128)(2,1)S(1)} %get-tuple-element.46), channel_id=1, source_target_pairs={{0,2},{2,0},{1,3},{3,1},{4,6},{6,4},{5,7},{7,5},{8,10},{10,8},{9,1... | collective-permute-start | bytes 393224 | tf_op jit(solution)/shard_map/ppermute | solution.py:358
  22.1 2.7 %collective-permute-start.3 = (bf16[1,128,512]{2,1,0:T(8,128)(2,1)S(1)}, bf16[1,128,512]{2,1,0:T(8,128)(2,1)S(1)}, u32[]{:S(2)}, u32[]{:S(2)}) collective-permute-start(bf16[1,128,512]{2,1,0:T(8,128)(2,1)S(1)} %get-tuple-element.35), channel_id=1, source_target_pairs={{0,4},{4,8},{8,12},{12,0},{1,5},{5,9},{9,13},{13,1},{2,6},{6,10},{... | collective-permute-start | bytes 393224 | tf_op jit(solution)/shard_map/ppermute | solution.py:283
  24.7 1.2 %collective-permute-start.5 = (bf16[1,128,512]{2,1,0:T(8,128)(2,1)S(1)}, bf16[1,128,512]{2,1,0:T(8,128)(2,1)S(1)}, u32[]{:S(2)}, u32[]{:S(2)}) collective-permute-start(bf16[1,128,512]{2,1,0:T(8,128)(2,1)S(1)} %get-tuple-element.37), channel_id=1, source_target_pairs={{0,12},{4,0},{8,4},{12,8},{1,13},{5,1},{9,5},{13,9},{2,14},{6,2},{... | collective-permute-start | bytes 393224 | tf_op jit(solution)/shard_map/ppermute | solution.py:283
  25.9 0.5 %collective-permute-done.6.got_ref = bf16[2,64,512]{2,1,0:T(8,128)(2,1)S(1)} collective-permute-done((bf16[2,64,512]{2,1,0:T(8,128)(2,1)S(1)}, bf16[2,64,512]{2,1,0:T(8,128)(2,1)S(1)}, u32[]{:S(2)}, u32[]{:S(2)}) %collective-permute-start.6) | collective-permute-done | bytes 131104 | tf_op jit(solution)/shard_map/ppermute | solution.py:358
  26.5 1.8 %collective-permute-start.7 = (bf16[64,512]{1,0:T(8,128)(2,1)S(1)}, bf16[64,512]{1,0:T(8,128)(2,1)S(1)}, u32[]{:S(2)}, u32[]{:S(2)}) collective-permute-start(bf16[64,512]{1,0:T(8,128)(2,1)S(1)} %get-tuple-element.45), channel_id=1, source_target_pairs={{0,4},{4,12},{12,8},{8,0},{1,5},{5,13},{13,9},{9,1},{2,6},{6,14},{... | collective-permute-start | bytes 196616 | tf_op jit(solution)/shard_map/ppermute | solution.py:283
  28.3 3.1 %collective-permute-start.9 = (bf16[64,512]{1,0:T(8,128)(2,1)S(1)}, bf16[64,512]{1,0:T(8,128)(2,1)S(1)}, u32[]{:S(2)}, u32[]{:S(2)}) collective-permute-start(bf16[64,512]{1,0:T(8,128)(2,1)S(1)} %get-tuple-element.47), channel_id=1, source_target_pairs={{0,12},{4,8},{12,0},{8,4},{1,13},{5,9},{13,1},{9,5},{2,14},{6,10},... | collective-permute-start | bytes 196616 | tf_op jit(solution)/shard_map/ppermute | solution.py:283
  31.5 1.7 %collective-permute-start.10 = (bf16[64,512]{1,0:T(8,128)(2,1)S(1)}, bf16[64,512]{1,0:T(8,128)(2,1)S(1)}, u32[]{:S(2)}, u32[]{:S(2)}) collective-permute-start(bf16[64,512]{1,0:T(8,128)(2,1)S(1)} %get-tuple-element.48), channel_id=1, source_target_pairs={{0,8},{4,0},{12,4},{8,12},{1,9},{5,1},{13,5},{9,13},{2,10},{6,2},{... | collective-permute-start | bytes 196616 | tf_op jit(solution)/shard_map/ppermute | solution.py:283
  33.2 1.1 %inverse.1 = bf16[1,256,512]{2,1,0:T(8,128)(2,1)} custom-call(bf16[4,256,128]{2,1,0:T(8,128)(2,1)S(1)} %copy-done.4, bf16[1,128,512]{2,1,0:T(8,128)(2,1)S(1)} %get-tuple-element.34.refs_0_, bf16[1,128,512]{2,1,0:T(8,128)(2,1)S(1)} %collective-permute-done.3.refs_1_, bf16[1,128,512]{2,1,0:T(8,128)(2,1)S(1)} %collective-permute-done.4.refs_2_.refs_0_, ...), custom_call_target="tpu_custom_call" | custom-call | tf_op jit(solution)/shard_map/inverse/pallas_call | solution.py:267
  34.4 1.1 %collective-permute-done.7.refs_1_ = bf16[64,512]{1,0:T(8,128)(2,1)S(1)} collective-permute-done((bf16[64,512]{1,0:T(8,128)(2,1)S(1)}, bf16[64,512]{1,0:T(8,128)(2,1)S(1)}, u32[]{:S(2)}, u32[]{:S(2)}) %collective-permute-start.7) | collective-permute-done | bytes 65568 | tf_op jit(solution)/shard_map/ppermute | solution.py:283
  35.5 0.6 %collective-permute-done.10.refs_3_ = bf16[64,512]{1,0:T(8,128)(2,1)S(1)} collective-permute-done((bf16[64,512]{1,0:T(8,128)(2,1)S(1)}, bf16[64,512]{1,0:T(8,128)(2,1)S(1)}, u32[]{:S(2)}, u32[]{:S(2)}) %collective-permute-start.10) | collective-permute-done | bytes 65568 | tf_op jit(solution)/shard_map/ppermute | solution.py:283
  36.1 0.7 %last_sum.1 = (f32[4,2,16,128]{3,2,1,0:T(8,128)}, f32[4,2,16,128]{3,2,1,0:T(8,128)}) custom-call(f32[64,512]{1,0:T(8,128)S(1)} %get-tuple-element.44.refs_0_, bf16[64,512]{1,0:T(8,128)(2,1)S(1)} %collective-permute-done.7.refs_1_, bf16[64,512]{1,0:T(8,128)(2,1)S(1)} %collective-permute-done.9.refs_2_, bf16[64,512]{1,0:T(8,128)(2,1)S(1)} %collective-permute-done.10.refs_3_), custom_call_target="tpu_custom_call" | custom-call | tf_op jit(solution)/shard_map/last_sum/pallas_call | solution.py:267
  (18 shorter events, 0.1 us)
Async XLA Ops:
  0.6 1.0 %copy-start.1 = (bf16[1,1,16,16,512]{4,3,2,1,0:T(8,128)(2,1)S(1)}, bf16[1,1,16,16,512]{4,3,2,1,0:T(8,128)(2,1)}, u32[]{:S(2)}) copy-start(bf16[1,1,16,16,512]{4,3,2,1,0:T(8,128)(2,1)} %param.6) | copy-start | bytes 786436
  1.6 7.5 %copy-start.2 = (bf16[4,2,128,128]{3,2,1,0:T(8,128)(2,1)S(1)}, bf16[4,2,128,128]{3,2,1,0:T(8,128)(2,1)}, u32[]{:S(2)}) copy-start(bf16[4,2,128,128]{3,2,1,0:T(8,128)(2,1)} %first_ref.1) | copy-start | bytes 786436
  2.1 9.8 %collective-permute-start = (bf16[1,128,512]{2,1,0:T(8,128)(2,1)S(1)}, bf16[1,128,512]{2,1,0:T(8,128)(2,1)S(1)}, u32[]{:S(2)}, u32[]{:S(2)}) collective-permute-start(bf16[1,128,512]{2,1,0:T(8,128)(2,1)S(1)} %get-tuple-element.28), channel_id=1, source_target_pairs={{0,4},{4,8},{8,12},{12,0},{1,5},{5,9},{9,13},{13,1},{2,6},{6,10},{... | collective-permute-start | bytes 393224 | tf_op jit(solution)/shard_map/ppermute | solution.py:283
  5.2 3.9 %copy-start.5 = (bf16[2,512]{1,0:T(2,128)(2,1)S(1)}, bf16[2,512]{1,0:T(2,128)(2,1)}, u32[]{:S(2)}) copy-start(bf16[2,512]{1,0:T(2,128)(2,1)} %bias_ref.1) | copy-start | bytes 6148
  5.2 11.2 %collective-permute-start.1 = (bf16[1,128,512]{2,1,0:T(8,128)(2,1)S(1)}, bf16[1,128,512]{2,1,0:T(8,128)(2,1)S(1)}, u32[]{:S(2)}, u32[]{:S(2)}) collective-permute-start(bf16[1,128,512]{2,1,0:T(8,128)(2,1)S(1)} %get-tuple-element.29), channel_id=1, source_target_pairs={{0,8},{4,12},{8,0},{12,4},{1,9},{5,13},{9,1},{13,5},{2,10},{6,14},... | collective-permute-start | bytes 393224 | tf_op jit(solution)/shard_map/ppermute | solution.py:283
  7.8 8.6 %collective-permute-start.2 = (bf16[1,128,512]{2,1,0:T(8,128)(2,1)S(1)}, bf16[1,128,512]{2,1,0:T(8,128)(2,1)S(1)}, u32[]{:S(2)}, u32[]{:S(2)}) collective-permute-start(bf16[1,128,512]{2,1,0:T(8,128)(2,1)S(1)} %get-tuple-element.30), channel_id=1, source_target_pairs={{0,12},{4,0},{8,4},{12,8},{1,13},{5,1},{9,5},{13,9},{2,14},{6,2},{... | collective-permute-start | bytes 393224 | tf_op jit(solution)/shard_map/ppermute | solution.py:283
  9.1 1.0 %copy-start = (bf16[2,1,4,4,16,512]{5,4,3,2,1,0:T(8,128)(2,1)S(1)}, bf16[2,1,4,4,16,512]{5,4,3,2,1,0:T(8,128)(2,1)}, u32[]{:S(2)}) copy-start(bf16[2,1,4,4,16,512]{5,4,3,2,1,0:T(8,128)(2,1)} %param.7) | copy-start | bytes 1572868
  10.1 0.9 %copy-start.3 = (bf16[4,2,128,128]{3,2,1,0:T(8,128)(2,1)S(1)}, bf16[4,2,128,128]{3,2,1,0:T(8,128)(2,1)}, u32[]{:S(2)}) copy-start(bf16[4,2,128,128]{3,2,1,0:T(8,128)(2,1)} %second_ref.1) | copy-start | bytes 786436
  17.2 8.7 %collective-permute-start.4 = (bf16[1,128,512]{2,1,0:T(8,128)(2,1)S(1)}, bf16[1,128,512]{2,1,0:T(8,128)(2,1)S(1)}, u32[]{:S(2)}, u32[]{:S(2)}) collective-permute-start(bf16[1,128,512]{2,1,0:T(8,128)(2,1)S(1)} %get-tuple-element.36), channel_id=1, source_target_pairs={{0,8},{4,12},{8,0},{12,4},{1,9},{5,13},{9,1},{13,5},{2,10},{6,14},... | collective-permute-start | bytes 393224 | tf_op jit(solution)/shard_map/ppermute | solution.py:283
  20.0 6.5 %collective-permute-start.6 = (bf16[2,64,512]{2,1,0:T(8,128)(2,1)S(1)}, bf16[2,64,512]{2,1,0:T(8,128)(2,1)S(1)}, u32[]{:S(2)}, u32[]{:S(2)}) collective-permute-start(bf16[2,64,512]{2,1,0:T(8,128)(2,1)S(1)} %get-tuple-element.43), channel_id=1, source_target_pairs={{0,2},{2,0},{1,3},{3,1},{4,6},{6,4},{5,7},{7,5},{8,10},{10,8},{9,1... | collective-permute-start | bytes 393224 | tf_op jit(solution)/shard_map/ppermute | solution.py:358
  21.5 6.8 %collective-permute-start.8 = (bf16[2,64,512]{2,1,0:T(8,128)(2,1)S(1)}, bf16[2,64,512]{2,1,0:T(8,128)(2,1)S(1)}, u32[]{:S(2)}, u32[]{:S(2)}) collective-permute-start(bf16[2,64,512]{2,1,0:T(8,128)(2,1)S(1)} %get-tuple-element.46), channel_id=1, source_target_pairs={{0,2},{2,0},{1,3},{3,1},{4,6},{6,4},{5,7},{7,5},{8,10},{10,8},{9,1... | collective-permute-start | bytes 393224 | tf_op jit(solution)/shard_map/ppermute | solution.py:358
  22.1 11.1 %collective-permute-start.3 = (bf16[1,128,512]{2,1,0:T(8,128)(2,1)S(1)}, bf16[1,128,512]{2,1,0:T(8,128)(2,1)S(1)}, u32[]{:S(2)}, u32[]{:S(2)}) collective-permute-start(bf16[1,128,512]{2,1,0:T(8,128)(2,1)S(1)} %get-tuple-element.35), channel_id=1, source_target_pairs={{0,4},{4,8},{8,12},{12,0},{1,5},{5,9},{9,13},{13,1},{2,6},{6,10},{... | collective-permute-start | bytes 393224 | tf_op jit(solution)/shard_map/ppermute | solution.py:283
  24.7 8.5 %collective-permute-start.5 = (bf16[1,128,512]{2,1,0:T(8,128)(2,1)S(1)}, bf16[1,128,512]{2,1,0:T(8,128)(2,1)S(1)}, u32[]{:S(2)}, u32[]{:S(2)}) collective-permute-start(bf16[1,128,512]{2,1,0:T(8,128)(2,1)S(1)} %get-tuple-element.37), channel_id=1, source_target_pairs={{0,12},{4,0},{8,4},{12,8},{1,13},{5,1},{9,5},{13,9},{2,14},{6,2},{... | collective-permute-start | bytes 393224 | tf_op jit(solution)/shard_map/ppermute | solution.py:283
  26.5 6.8 %copy-start.4 = (bf16[4,256,128]{2,1,0:T(8,128)(2,1)S(1)}, bf16[4,256,128]{2,1,0:T(8,128)(2,1)}, u32[]{:S(2)}) copy-start(bf16[4,256,128]{2,1,0:T(8,128)(2,1)} %constant.2.clone.table_ref) | copy-start | bytes 786436
  26.5 9.0 %collective-permute-start.7 = (bf16[64,512]{1,0:T(8,128)(2,1)S(1)}, bf16[64,512]{1,0:T(8,128)(2,1)S(1)}, u32[]{:S(2)}, u32[]{:S(2)}) collective-permute-start(bf16[64,512]{1,0:T(8,128)(2,1)S(1)} %get-tuple-element.45), channel_id=1, source_target_pairs={{0,4},{4,12},{12,8},{8,0},{1,5},{5,13},{13,9},{9,1},{2,6},{6,14},{... | collective-permute-start | bytes 196616 | tf_op jit(solution)/shard_map/ppermute | solution.py:283
  28.3 7.1 %collective-permute-start.9 = (bf16[64,512]{1,0:T(8,128)(2,1)S(1)}, bf16[64,512]{1,0:T(8,128)(2,1)S(1)}, u32[]{:S(2)}, u32[]{:S(2)}) collective-permute-start(bf16[64,512]{1,0:T(8,128)(2,1)S(1)} %get-tuple-element.47), channel_id=1, source_target_pairs={{0,12},{4,8},{12,0},{8,4},{1,13},{5,9},{13,1},{9,5},{2,14},{6,10},... | collective-permute-start | bytes 196616 | tf_op jit(solution)/shard_map/ppermute | solution.py:283
  31.5 4.6 %collective-permute-start.10 = (bf16[64,512]{1,0:T(8,128)(2,1)S(1)}, bf16[64,512]{1,0:T(8,128)(2,1)S(1)}, u32[]{:S(2)}, u32[]{:S(2)}) collective-permute-start(bf16[64,512]{1,0:T(8,128)(2,1)S(1)} %get-tuple-element.48), channel_id=1, source_target_pairs={{0,8},{4,0},{12,4},{8,12},{1,9},{5,1},{13,5},{9,13},{2,10},{6,2},{... | collective-permute-start | bytes 196616 | tf_op jit(solution)/shard_map/ppermute | solution.py:283

commit v5 on v4

--- a/solution.py
+++ b/solution.py
@@ -92,8 +92,17 @@
 def wave_rows(length, cells, inner, outer):
     row = lax.broadcasted_iota(jnp.int32, (length, cells), 0)
     cell = lax.broadcasted_iota(jnp.int32, (length, cells), 1)
-    angle = lax.rem(row * lax.rem(cell // inner, outer), length).astype(f32) * (2.0 * math.pi / length)
-    return jnp.cos(angle), jnp.sin(angle)
+    turns = lax.rem(row * lax.rem(cell // inner, outer), length)
+    turns = jnp.where(2 * turns > length, turns - length, turns)
+    half = turns.astype(f32) * (math.pi / length)
+    square = half * half
+    sine, cosine = jnp.zeros_like(half), jnp.zeros_like(half)
+    for power in range(7, -1, -1):
+        sign = -1.0 if power % 2 else 1.0
+        cosine = cosine * square + sign / math.factorial(2 * power)
+        sine = sine * square + sign / math.factorial(2 * power + 1)
+    sine = sine * half
+    return 1.0 - 2.0 * sine * sine, 2.0 * sine * cosine
 
 
 def ring(count, folded):

time: 37 us -> 36.9 us (level)
  no operation moved by 1% of the time
where the time goes in v5:
time: 36.9 us; the launch traced here: 36.7 us
  starting transfers between devices  21.9 us (59%)
  waiting for transfers between devices  6.77 us (18%)
  Pallas kernels  4.3 us (12%)
  local copies, waits for them, and re-layouts  2.95 us (8%)
  between operations  0.71 us (2%)
    ppermute x9, starting transfers between devices, spread(): moved.append(lax.ppermute(values[step], 'space', pairs))  19.8 us
    ppermute x9, waiting for transfers between devices, spread(): moved.append(lax.ppermute(values[step], 'space', pairs))  6.22 us
    pallas_call x8, Pallas kernels, call(): pl.pallas_call(kernel, out_shape=tuple(outs), in_specs=[whole] * (len(arg...  4.3 us
    unnamed x12, local copies, waits for them, and re-layouts  2.95 us
    ppermute x2, starting transfers between devices, body(): got = [lax.ppermute(send, 'dp', [(0, 1), (1, 0)]) for send in sends]  2.09 us
  transfers between devices with their start and end apart: 11, of which 4 were waited for; matrix products, arithmetic and copies ran while one was open for 0% of the time, Pallas kernels for 7%

profile of v5, /device:TPU:0, one launch (start us, length us, event | category | flops | bytes accessed | tf_op | source)
XLA Modules:
  0.0 36.7 jit_solution(17564640811436754456)
XLA Ops:
  0.6 0.9 %copy-done.1 = bf16[1,1,16,16,512]{4,3,2,1,0:T(8,128)(2,1)S(1)} copy-done((bf16[1,1,16,16,512]{4,3,2,1,0:T(8,128)(2,1)S(1)}, bf16[1,1,16,16,512]{4,3,2,1,0:T(8,128)(2,1)}, u32[]{:S(2)}) %copy-start.1) | copy-done | bytes 262168
  1.6 0.4 %forward.1 = (bf16[1,128,512]{2,1,0:T(8,128)(2,1)S(1)}, bf16[1,128,512]{2,1,0:T(8,128)(2,1)S(1)}, bf16[1,128,512]{2,1,0:T(8,128)(2,1)S(1)}, bf16[1,128,512]{2,1,0:T(8,128)(2,1)S(1)}) custom-call(bf16[1,256,512]{2,1,0:T(8,128)(2,1)S(1)} %bitcast.4), custom_call_target="tpu_custom_call" | custom-call | tf_op jit(solution)/shard_map/forward/pallas_call | solution.py:276
  2.0 3.1 %collective-permute-start = (bf16[1,128,512]{2,1,0:T(8,128)(2,1)S(1)}, bf16[1,128,512]{2,1,0:T(8,128)(2,1)S(1)}, u32[]{:S(2)}, u32[]{:S(2)}) collective-permute-start(bf16[1,128,512]{2,1,0:T(8,128)(2,1)S(1)} %get-tuple-element.28), channel_id=1, source_target_pairs={{0,4},{4,8},{8,12},{12,0},{1,5},{5,9},{9,13},{13,1},{2,6},{6,10},{... | collective-permute-start | bytes 393224 | tf_op jit(solution)/shard_map/ppermute | solution.py:292
  5.1 2.6 %collective-permute-start.1 = (bf16[1,128,512]{2,1,0:T(8,128)(2,1)S(1)}, bf16[1,128,512]{2,1,0:T(8,128)(2,1)S(1)}, u32[]{:S(2)}, u32[]{:S(2)}) collective-permute-start(bf16[1,128,512]{2,1,0:T(8,128)(2,1)S(1)} %get-tuple-element.29), channel_id=1, source_target_pairs={{0,8},{4,12},{8,0},{12,4},{1,9},{5,13},{9,1},{13,5},{2,10},{6,14},... | collective-permute-start | bytes 393224 | tf_op jit(solution)/shard_map/ppermute | solution.py:292
  7.7 1.3 %collective-permute-start.2 = (bf16[1,128,512]{2,1,0:T(8,128)(2,1)S(1)}, bf16[1,128,512]{2,1,0:T(8,128)(2,1)S(1)}, u32[]{:S(2)}, u32[]{:S(2)}) collective-permute-start(bf16[1,128,512]{2,1,0:T(8,128)(2,1)S(1)} %get-tuple-element.30), channel_id=1, source_target_pairs={{0,12},{4,0},{8,4},{12,8},{1,13},{5,1},{9,5},{13,9},{2,14},{6,2},{... | collective-permute-start | bytes 393224 | tf_op jit(solution)/shard_map/ppermute | solution.py:292
  9.0 1.0 %copy-done = bf16[2,1,4,4,16,512]{5,4,3,2,1,0:T(8,128)(2,1)S(1)} copy-done((bf16[2,1,4,4,16,512]{5,4,3,2,1,0:T(8,128)(2,1)S(1)}, bf16[2,1,4,4,16,512]{5,4,3,2,1,0:T(8,128)(2,1)}, u32[]{:S(2)}) %copy-start) | copy-done | bytes 524312
  10.0 0.9 %copy-done.3 = bf16[4,2,128,128]{3,2,1,0:T(8,128)(2,1)S(1)} copy-done((bf16[4,2,128,128]{3,2,1,0:T(8,128)(2,1)S(1)}, bf16[4,2,128,128]{3,2,1,0:T(8,128)(2,1)}, u32[]{:S(2)}) %copy-start.3) | copy-done | bytes 262168
  11.0 0.8 %activation.1 = (bf16[4,256,256]{2,1,0:T(8,128)(2,1)S(1)}, bf16[4,256,256]{2,1,0:T(8,128)(2,1)S(1)}, f32[4,256,256]{2,1,0:T(8,128)S(1)}, bf16[4,256,256]{2,1,0:T(8,128)(2,1)S(1)}, bf16[4,256,256]{2,1,0:T(8,128)(2,1)S(1)}) custom-call(bf16[2,256,512]{2,1,0:T(8,128)(2,1)S(1)} %bitcast.3, bf16[4,2,128,128]{3,2,1,0:T(8,128)(2,1)S(1)} %copy-done.2, ...), custom_call_target="tpu_custom_call" | custom-call | tf_op jit(solution)/shard_map/activation/pallas_call | solution.py:276
  11.8 4.5 %collective-permute-done.1.refs_2_ = bf16[1,128,512]{2,1,0:T(8,128)(2,1)S(1)} collective-permute-done((bf16[1,128,512]{2,1,0:T(8,128)(2,1)S(1)}, bf16[1,128,512]{2,1,0:T(8,128)(2,1)S(1)}, u32[]{:S(2)}, u32[]{:S(2)}) %collective-permute-start.1) | collective-permute-done | bytes 131104 | tf_op jit(solution)/shard_map/ppermute | solution.py:292
  16.3 0.7 %filter.1 = (bf16[1,128,512]{2,1,0:T(8,128)(2,1)S(1)}, bf16[1,128,512]{2,1,0:T(8,128)(2,1)S(1)}, bf16[1,128,512]{2,1,0:T(8,128)(2,1)S(1)}, bf16[1,128,512]{2,1,0...) custom-call(bf16[1,128,512]{2,1,0:T(8,128)(2,1)S(1)} %get-tuple-element.27.refs_0_, ...), custom_call_target="tpu_custom_call" | custom-call | tf_op jit(solution)/shard_map/filter/pallas_call | solution.py:276
  17.0 2.3 %collective-permute-start.4 = (bf16[1,128,512]{2,1,0:T(8,128)(2,1)S(1)}, bf16[1,128,512]{2,1,0:T(8,128)(2,1)S(1)}, u32[]{:S(2)}, u32[]{:S(2)}) collective-permute-start(bf16[1,128,512]{2,1,0:T(8,128)(2,1)S(1)} %get-tuple-element.36), channel_id=1, source_target_pairs={{0,8},{4,12},{8,0},{12,4},{1,9},{5,13},{9,1},{13,5},{2,10},{6,14},... | collective-permute-start | bytes 393224 | tf_op jit(solution)/shard_map/ppermute | solution.py:292
  19.4 0.5 %weight.1 = (f32[4,64,512]{2,1,0:T(8,128)S(1)}, bf16[2,64,512]{2,1,0:T(8,128)(2,1)S(1)}, bf16[2,64,512]{2,1,0:T(8,128)(2,1)S(1)}) custom-call(bf16[4,256,256]{2,1,0:T(8,128)(2,1)S(1)} %get-tuple-element.38.act_ref, bf16[4,256,256]{2,1,0:T(8,128)(2,1)S(1)} %get-tuple-element.39.flip_ref, bf16[4,256,256]{2,1,0:T(8,128)(2,1)S(1)} %get-tuple-element.40.value_ref, ...), custom_call_target="tpu_custom_call" | custom-call | tf_op jit(solution)/shard_map/weight/pallas_call | solution.py:276
  19.9 1.6 %collective-permute-start.6 = (bf16[2,64,512]{2,1,0:T(8,128)(2,1)S(1)}, bf16[2,64,512]{2,1,0:T(8,128)(2,1)S(1)}, u32[]{:S(2)}, u32[]{:S(2)}) collective-permute-start(bf16[2,64,512]{2,1,0:T(8,128)(2,1)S(1)} %get-tuple-element.43), channel_id=1, source_target_pairs={{0,2},{2,0},{1,3},{3,1},{4,6},{6,4},{5,7},{7,5},{8,10},{10,8},{9,1... | collective-permute-start | bytes 393224 | tf_op jit(solution)/shard_map/ppermute | solution.py:367
  21.4 0.5 %collective-permute-start.8 = (bf16[2,64,512]{2,1,0:T(8,128)(2,1)S(1)}, bf16[2,64,512]{2,1,0:T(8,128)(2,1)S(1)}, u32[]{:S(2)}, u32[]{:S(2)}) collective-permute-start(bf16[2,64,512]{2,1,0:T(8,128)(2,1)S(1)} %get-tuple-element.46), channel_id=1, source_target_pairs={{0,2},{2,0},{1,3},{3,1},{4,6},{6,4},{5,7},{7,5},{8,10},{10,8},{9,1... | collective-permute-start | bytes 393224 | tf_op jit(solution)/shard_map/ppermute | solution.py:367
  22.0 2.6 %collective-permute-start.3 = (bf16[1,128,512]{2,1,0:T(8,128)(2,1)S(1)}, bf16[1,128,512]{2,1,0:T(8,128)(2,1)S(1)}, u32[]{:S(2)}, u32[]{:S(2)}) collective-permute-start(bf16[1,128,512]{2,1,0:T(8,128)(2,1)S(1)} %get-tuple-element.35), channel_id=1, source_target_pairs={{0,4},{4,8},{8,12},{12,0},{1,5},{5,9},{9,13},{13,1},{2,6},{6,10},{... | collective-permute-start | bytes 393224 | tf_op jit(solution)/shard_map/ppermute | solution.py:292
  24.6 1.2 %collective-permute-start.5 = (bf16[1,128,512]{2,1,0:T(8,128)(2,1)S(1)}, bf16[1,128,512]{2,1,0:T(8,128)(2,1)S(1)}, u32[]{:S(2)}, u32[]{:S(2)}) collective-permute-start(bf16[1,128,512]{2,1,0:T(8,128)(2,1)S(1)} %get-tuple-element.37), channel_id=1, source_target_pairs={{0,12},{4,0},{8,4},{12,8},{1,13},{5,1},{9,5},{13,9},{2,14},{6,2},{... | collective-permute-start | bytes 393224 | tf_op jit(solution)/shard_map/ppermute | solution.py:292
  25.8 0.5 %collective-permute-done.6.got_ref = bf16[2,64,512]{2,1,0:T(8,128)(2,1)S(1)} collective-permute-done((bf16[2,64,512]{2,1,0:T(8,128)(2,1)S(1)}, bf16[2,64,512]{2,1,0:T(8,128)(2,1)S(1)}, u32[]{:S(2)}, u32[]{:S(2)}) %collective-permute-start.6) | collective-permute-done | bytes 131104 | tf_op jit(solution)/shard_map/ppermute | solution.py:367
  26.4 1.8 %collective-permute-start.7 = (bf16[64,512]{1,0:T(8,128)(2,1)S(1)}, bf16[64,512]{1,0:T(8,128)(2,1)S(1)}, u32[]{:S(2)}, u32[]{:S(2)}) collective-permute-start(bf16[64,512]{1,0:T(8,128)(2,1)S(1)} %get-tuple-element.45), channel_id=1, source_target_pairs={{0,4},{4,12},{12,8},{8,0},{1,5},{5,13},{13,9},{9,1},{2,6},{6,14},{... | collective-permute-start | bytes 196616 | tf_op jit(solution)/shard_map/ppermute | solution.py:292
  28.2 3.2 %collective-permute-start.9 = (bf16[64,512]{1,0:T(8,128)(2,1)S(1)}, bf16[64,512]{1,0:T(8,128)(2,1)S(1)}, u32[]{:S(2)}, u32[]{:S(2)}) collective-permute-start(bf16[64,512]{1,0:T(8,128)(2,1)S(1)} %get-tuple-element.47), channel_id=1, source_target_pairs={{0,12},{4,8},{12,0},{8,4},{1,13},{5,9},{13,1},{9,5},{2,14},{6,10},... | collective-permute-start | bytes 196616 | tf_op jit(solution)/shard_map/ppermute | solution.py:292
  31.4 1.7 %collective-permute-start.10 = (bf16[64,512]{1,0:T(8,128)(2,1)S(1)}, bf16[64,512]{1,0:T(8,128)(2,1)S(1)}, u32[]{:S(2)}, u32[]{:S(2)}) collective-permute-start(bf16[64,512]{1,0:T(8,128)(2,1)S(1)} %get-tuple-element.48), channel_id=1, source_target_pairs={{0,8},{4,0},{12,4},{8,12},{1,9},{5,1},{13,5},{9,13},{2,10},{6,2},{... | collective-permute-start | bytes 196616 | tf_op jit(solution)/shard_map/ppermute | solution.py:292
  33.1 1.1 %inverse.1 = bf16[1,256,512]{2,1,0:T(8,128)(2,1)} custom-call(bf16[4,256,128]{2,1,0:T(8,128)(2,1)S(1)} %copy-done.4, bf16[1,128,512]{2,1,0:T(8,128)(2,1)S(1)} %get-tuple-element.34.refs_0_, bf16[1,128,512]{2,1,0:T(8,128)(2,1)S(1)} %collective-permute-done.3.refs_1_, bf16[1,128,512]{2,1,0:T(8,128)(2,1)S(1)} %collective-permute-done.4.refs_2_.refs_0_, ...), custom_call_target="tpu_custom_call" | custom-call | tf_op jit(solution)/shard_map/inverse/pallas_call | solution.py:276
  34.2 0.9 %collective-permute-done.9.refs_2_ = bf16[64,512]{1,0:T(8,128)(2,1)S(1)} collective-permute-done((bf16[64,512]{1,0:T(8,128)(2,1)S(1)}, bf16[64,512]{1,0:T(8,128)(2,1)S(1)}, u32[]{:S(2)}, u32[]{:S(2)}) %collective-permute-start.9) | collective-permute-done | bytes 65568 | tf_op jit(solution)/shard_map/ppermute | solution.py:292
  35.2 0.8 %collective-permute-done.10.refs_3_ = bf16[64,512]{1,0:T(8,128)(2,1)S(1)} collective-permute-done((bf16[64,512]{1,0:T(8,128)(2,1)S(1)}, bf16[64,512]{1,0:T(8,128)(2,1)S(1)}, u32[]{:S(2)}, u32[]{:S(2)}) %collective-permute-start.10) | collective-permute-done | bytes 65568 | tf_op jit(solution)/shard_map/ppermute | solution.py:292
  36.0 0.7 %last_sum.1 = (f32[4,2,16,128]{3,2,1,0:T(8,128)}, f32[4,2,16,128]{3,2,1,0:T(8,128)}) custom-call(f32[64,512]{1,0:T(8,128)S(1)} %get-tuple-element.44.refs_0_, bf16[64,512]{1,0:T(8,128)(2,1)S(1)} %collective-permute-done.7.refs_1_, bf16[64,512]{1,0:T(8,128)(2,1)S(1)} %collective-permute-done.9.refs_2_, bf16[64,512]{1,0:T(8,128)(2,1)S(1)} %collective-permute-done.10.refs_3_), custom_call_target="tpu_custom_call" | custom-call | tf_op jit(solution)/shard_map/last_sum/pallas_call | solution.py:276
  (18 shorter events, 0.1 us)
Async XLA Ops:
  0.6 1.0 %copy-start.1 = (bf16[1,1,16,16,512]{4,3,2,1,0:T(8,128)(2,1)S(1)}, bf16[1,1,16,16,512]{4,3,2,1,0:T(8,128)(2,1)}, u32[]{:S(2)}) copy-start(bf16[1,1,16,16,512]{4,3,2,1,0:T(8,128)(2,1)} %param.6) | copy-start | bytes 786436
  1.6 7.4 %copy-start.2 = (bf16[4,2,128,128]{3,2,1,0:T(8,128)(2,1)S(1)}, bf16[4,2,128,128]{3,2,1,0:T(8,128)(2,1)}, u32[]{:S(2)}) copy-start(bf16[4,2,128,128]{3,2,1,0:T(8,128)(2,1)} %first_ref.1) | copy-start | bytes 786436
  2.0 9.8 %collective-permute-start = (bf16[1,128,512]{2,1,0:T(8,128)(2,1)S(1)}, bf16[1,128,512]{2,1,0:T(8,128)(2,1)S(1)}, u32[]{:S(2)}, u32[]{:S(2)}) collective-permute-start(bf16[1,128,512]{2,1,0:T(8,128)(2,1)S(1)} %get-tuple-element.28), channel_id=1, source_target_pairs={{0,4},{4,8},{8,12},{12,0},{1,5},{5,9},{9,13},{13,1},{2,6},{6,10},{... | collective-permute-start | bytes 393224 | tf_op jit(solution)/shard_map/ppermute | solution.py:292
  5.1 3.9 %copy-start.5 = (bf16[2,512]{1,0:T(2,128)(2,1)S(1)}, bf16[2,512]{1,0:T(2,128)(2,1)}, u32[]{:S(2)}) copy-start(bf16[2,512]{1,0:T(2,128)(2,1)} %bias_ref.1) | copy-start | bytes 6148
  5.1 11.2 %collective-permute-start.1 = (bf16[1,128,512]{2,1,0:T(8,128)(2,1)S(1)}, bf16[1,128,512]{2,1,0:T(8,128)(2,1)S(1)}, u32[]{:S(2)}, u32[]{:S(2)}) collective-permute-start(bf16[1,128,512]{2,1,0:T(8,128)(2,1)S(1)} %get-tuple-element.29), channel_id=1, source_target_pairs={{0,8},{4,12},{8,0},{12,4},{1,9},{5,13},{9,1},{13,5},{2,10},{6,14},... | collective-permute-start | bytes 393224 | tf_op jit(solution)/shard_map/ppermute | solution.py:292
  7.7 8.6 %collective-permute-start.2 = (bf16[1,128,512]{2,1,0:T(8,128)(2,1)S(1)}, bf16[1,128,512]{2,1,0:T(8,128)(2,1)S(1)}, u32[]{:S(2)}, u32[]{:S(2)}) collective-permute-start(bf16[1,128,512]{2,1,0:T(8,128)(2,1)S(1)} %get-tuple-element.30), channel_id=1, source_target_pairs={{0,12},{4,0},{8,4},{12,8},{1,13},{5,1},{9,5},{13,9},{2,14},{6,2},{... | collective-permute-start | bytes 393224 | tf_op jit(solution)/shard_map/ppermute | solution.py:292
  9.0 1.0 %copy-start = (bf16[2,1,4,4,16,512]{5,4,3,2,1,0:T(8,128)(2,1)S(1)}, bf16[2,1,4,4,16,512]{5,4,3,2,1,0:T(8,128)(2,1)}, u32[]{:S(2)}) copy-start(bf16[2,1,4,4,16,512]{5,4,3,2,1,0:T(8,128)(2,1)} %param.7) | copy-start | bytes 1572868
  10.0 0.9 %copy-start.3 = (bf16[4,2,128,128]{3,2,1,0:T(8,128)(2,1)S(1)}, bf16[4,2,128,128]{3,2,1,0:T(8,128)(2,1)}, u32[]{:S(2)}) copy-start(bf16[4,2,128,128]{3,2,1,0:T(8,128)(2,1)} %second_ref.1) | copy-start | bytes 786436
  17.0 8.7 %collective-permute-start.4 = (bf16[1,128,512]{2,1,0:T(8,128)(2,1)S(1)}, bf16[1,128,512]{2,1,0:T(8,128)(2,1)S(1)}, u32[]{:S(2)}, u32[]{:S(2)}) collective-permute-start(bf16[1,128,512]{2,1,0:T(8,128)(2,1)S(1)} %get-tuple-element.36), channel_id=1, source_target_pairs={{0,8},{4,12},{8,0},{12,4},{1,9},{5,13},{9,1},{13,5},{2,10},{6,14},... | collective-permute-start | bytes 393224 | tf_op jit(solution)/shard_map/ppermute | solution.py:292
  19.9 6.5 %collective-permute-start.6 = (bf16[2,64,512]{2,1,0:T(8,128)(2,1)S(1)}, bf16[2,64,512]{2,1,0:T(8,128)(2,1)S(1)}, u32[]{:S(2)}, u32[]{:S(2)}) collective-permute-start(bf16[2,64,512]{2,1,0:T(8,128)(2,1)S(1)} %get-tuple-element.43), channel_id=1, source_target_pairs={{0,2},{2,0},{1,3},{3,1},{4,6},{6,4},{5,7},{7,5},{8,10},{10,8},{9,1... | collective-permute-start | bytes 393224 | tf_op jit(solution)/shard_map/ppermute | solution.py:367
  21.4 6.7 %collective-permute-start.8 = (bf16[2,64,512]{2,1,0:T(8,128)(2,1)S(1)}, bf16[2,64,512]{2,1,0:T(8,128)(2,1)S(1)}, u32[]{:S(2)}, u32[]{:S(2)}) collective-permute-start(bf16[2,64,512]{2,1,0:T(8,128)(2,1)S(1)} %get-tuple-element.46), channel_id=1, source_target_pairs={{0,2},{2,0},{1,3},{3,1},{4,6},{6,4},{5,7},{7,5},{8,10},{10,8},{9,1... | collective-permute-start | bytes 393224 | tf_op jit(solution)/shard_map/ppermute | solution.py:367
  22.0 11.1 %collective-permute-start.3 = (bf16[1,128,512]{2,1,0:T(8,128)(2,1)S(1)}, bf16[1,128,512]{2,1,0:T(8,128)(2,1)S(1)}, u32[]{:S(2)}, u32[]{:S(2)}) collective-permute-start(bf16[1,128,512]{2,1,0:T(8,128)(2,1)S(1)} %get-tuple-element.35), channel_id=1, source_target_pairs={{0,4},{4,8},{8,12},{12,0},{1,5},{5,9},{9,13},{13,1},{2,6},{6,10},{... | collective-permute-start | bytes 393224 | tf_op jit(solution)/shard_map/ppermute | solution.py:292
  24.6 8.5 %collective-permute-start.5 = (bf16[1,128,512]{2,1,0:T(8,128)(2,1)S(1)}, bf16[1,128,512]{2,1,0:T(8,128)(2,1)S(1)}, u32[]{:S(2)}, u32[]{:S(2)}) collective-permute-start(bf16[1,128,512]{2,1,0:T(8,128)(2,1)S(1)} %get-tuple-element.37), channel_id=1, source_target_pairs={{0,12},{4,0},{8,4},{12,8},{1,13},{5,1},{9,5},{13,9},{2,14},{6,2},{... | collective-permute-start | bytes 393224 | tf_op jit(solution)/shard_map/ppermute | solution.py:292
  26.4 6.7 %copy-start.4 = (bf16[4,256,128]{2,1,0:T(8,128)(2,1)S(1)}, bf16[4,256,128]{2,1,0:T(8,128)(2,1)}, u32[]{:S(2)}) copy-start(bf16[4,256,128]{2,1,0:T(8,128)(2,1)} %constant.2.clone.table_ref) | copy-start | bytes 786436
  26.4 7.9 %collective-permute-start.7 = (bf16[64,512]{1,0:T(8,128)(2,1)S(1)}, bf16[64,512]{1,0:T(8,128)(2,1)S(1)}, u32[]{:S(2)}, u32[]{:S(2)}) collective-permute-start(bf16[64,512]{1,0:T(8,128)(2,1)S(1)} %get-tuple-element.45), channel_id=1, source_target_pairs={{0,4},{4,12},{12,8},{8,0},{1,5},{5,13},{13,9},{9,1},{2,6},{6,14},{... | collective-permute-start | bytes 196616 | tf_op jit(solution)/shard_map/ppermute | solution.py:292
  28.2 7.0 %collective-permute-start.9 = (bf16[64,512]{1,0:T(8,128)(2,1)S(1)}, bf16[64,512]{1,0:T(8,128)(2,1)S(1)}, u32[]{:S(2)}, u32[]{:S(2)}) collective-permute-start(bf16[64,512]{1,0:T(8,128)(2,1)S(1)} %get-tuple-element.47), channel_id=1, source_target_pairs={{0,12},{4,8},{12,0},{8,4},{1,13},{5,9},{13,1},{9,5},{2,14},{6,10},... | collective-permute-start | bytes 196616 | tf_op jit(solution)/shard_map/ppermute | solution.py:292
  31.4 4.6 %collective-permute-start.10 = (bf16[64,512]{1,0:T(8,128)(2,1)S(1)}, bf16[64,512]{1,0:T(8,128)(2,1)S(1)}, u32[]{:S(2)}, u32[]{:S(2)}) collective-permute-start(bf16[64,512]{1,0:T(8,128)(2,1)S(1)} %get-tuple-element.48), channel_id=1, source_target_pairs={{0,8},{4,0},{12,4},{8,12},{1,9},{5,1},{13,5},{9,13},{2,10},{6,2},{... | collective-permute-start | bytes 196616 | tf_op jit(solution)/shard_map/ppermute | solution.py:292

commit v6 on v5

--- a/solution.py
+++ b/solution.py
@@ -121,7 +121,7 @@
     return home
 
 
-def forward_kernel(count, factor, length_y, length_z, cell_ref, *refs):
+def forward_kernel(count, factor, scale, length_y, length_z, cell_ref, *refs):
     out_refs, table_ref = refs[:-1], refs[-1]
     me = lax.axis_index("space")
     planes, cells, _ = cell_ref.shape
@@ -140,7 +140,7 @@
     for step, out_ref in enumerate(out_refs):
         table = table_ref[neighbour(me, step, count)]
         for plane in range(planes):
-            product = jnp.dot(table, cell_ref[plane], preferred_element_type=f32) * (1.0 / factor)
+            product = jnp.dot(table, cell_ref[plane], preferred_element_type=f32) * scale
             out_ref[plane] = product.astype(bf16)
 
 
@@ -163,7 +163,7 @@
 
 
 def filter_kernel(
-    count, samples, norm_scale, part_refs, slope_ref, first_back_ref, second_back_ref, back_refs,
+    count, samples, part_refs, slope_ref, first_back_ref, second_back_ref, back_refs,
     value_ref, delta_ref, pencil, inner, returned,
 ):
     me = lax.axis_index("space")
@@ -191,8 +191,8 @@
                 ]
                 for x, (real, imag) in enumerate(short_transform(pairs, -1)):
                     base = (sample * length_x + x) * rows + start
-                    value_ref[at, base : base + tile, :block] = (real * norm_scale).astype(bf16)
-                    value_ref[at, base : base + tile, block:] = (imag * norm_scale).astype(bf16)
+                    value_ref[at, base : base + tile, :block] = real.astype(bf16)
+                    value_ref[at, base : base + tile, block:] = imag.astype(bf16)
         back = jnp.dot(value_ref[at], second_back_ref[at], preferred_element_type=f32)
         delta = (back * slope_ref[at]).astype(bf16)
         delta_ref[at] = delta
@@ -218,9 +218,9 @@
     for at in range(act_ref.shape[0]):
         lanes = slice(at * block, (at + 1) * block)
         for which, left, right in ((0, flip_ref, delta_ref), (1, act_ref, value_ref)):
-            square = jnp.dot(left[at], right[at], preferred_element_type=f32) * scale
-            real = square[:block, :block] + square[block:, block:]
-            imag = square[:block, block:] - square[block:, :block]
+            square = jnp.dot(left[at], right[at], preferred_element_type=f32)
+            real = (square[:block, :block] + square[block:, block:]) * scale
+            imag = (square[:block, block:] - square[block:, :block]) * scale
             for part, term in ((0, real), (1, imag)):
                 if exchange:
                     keep_ref, send_ref = term_refs[0], term_refs[-1]
@@ -316,7 +316,7 @@
 
     parts = spread(
         call(
-            functools.partial(forward_kernel, count, factor, length_y, length_z),
+            functools.partial(forward_kernel, count, factor, norm_scale / factor, length_y, length_z),
             [slab] * count,
             [grad_out.reshape(slabs, cells, width)],
             scratch=[pltpu.VMEM((count, 2 * rows, cells), bf16)],
@@ -333,7 +333,7 @@
 
     def filter_body(*refs):
         filter_kernel(
-            count, samples, norm_scale, refs[:count], *refs[count : count + 3], refs[count + 3 : 2 * count + 3],
+            count, samples, refs[:count], *refs[count : count + 3], refs[count + 3 : 2 * count + 3],
             *refs[2 * count + 3 :],
         )
 

time: 36.9 us -> 36.9 us (level)
  no operation moved by 1% of the time
where the time goes in v6:
time: 36.9 us; the launch traced here: 36.7 us
  starting transfers between devices  22 us (60%)
  waiting for transfers between devices  6.75 us (18%)
  Pallas kernels  4.29 us (12%)
  local copies, waits for them, and re-layouts  2.95 us (8%)
  between operations  0.71 us (2%)
    ppermute x9, starting transfers between devices, spread(): moved.append(lax.ppermute(values[step], 'space', pairs))  19.9 us
    ppermute x9, waiting for transfers between devices, spread(): moved.append(lax.ppermute(values[step], 'space', pairs))  6.21 us
    pallas_call x8, Pallas kernels, call(): pl.pallas_call(kernel, out_shape=tuple(outs), in_specs=[whole] * (len(arg...  4.29 us
    unnamed x12, local copies, waits for them, and re-layouts  2.95 us
    ppermute x2, starting transfers between devices, body(): got = [lax.ppermute(send, 'dp', [(0, 1), (1, 0)]) for send in sends]  2.09 us
  transfers between devices with their start and end apart: 11, of which 4 were waited for; matrix products, arithmetic and copies ran while one was open for 0% of the time, Pallas kernels for 7%

profile of v6, /device:TPU:0, one launch (start us, length us, event | category | flops | bytes accessed | tf_op | source)
XLA Modules:
  0.0 36.7 jit_solution(1370028298152560225)
XLA Ops:
  0.6 0.9 %copy-done.1 = bf16[1,1,16,16,512]{4,3,2,1,0:T(8,128)(2,1)S(1)} copy-done((bf16[1,1,16,16,512]{4,3,2,1,0:T(8,128)(2,1)S(1)}, bf16[1,1,16,16,512]{4,3,2,1,0:T(8,128)(2,1)}, u32[]{:S(2)}) %copy-start.1) | copy-done | bytes 262168
  1.6 0.4 %forward.1 = (bf16[1,128,512]{2,1,0:T(8,128)(2,1)S(1)}, bf16[1,128,512]{2,1,0:T(8,128)(2,1)S(1)}, bf16[1,128,512]{2,1,0:T(8,128)(2,1)S(1)}, bf16[1,128,512]{2,1,0:T(8,128)(2,1)S(1)}) custom-call(bf16[1,256,512]{2,1,0:T(8,128)(2,1)S(1)} %bitcast.4), custom_call_target="tpu_custom_call" | custom-call | tf_op jit(solution)/shard_map/forward/pallas_call | solution.py:276
  2.0 3.1 %collective-permute-start = (bf16[1,128,512]{2,1,0:T(8,128)(2,1)S(1)}, bf16[1,128,512]{2,1,0:T(8,128)(2,1)S(1)}, u32[]{:S(2)}, u32[]{:S(2)}) collective-permute-start(bf16[1,128,512]{2,1,0:T(8,128)(2,1)S(1)} %get-tuple-element.28), channel_id=1, source_target_pairs={{0,4},{4,8},{8,12},{12,0},{1,5},{5,9},{9,13},{13,1},{2,6},{6,10},{... | collective-permute-start | bytes 393224 | tf_op jit(solution)/shard_map/ppermute | solution.py:292
  5.1 2.6 %collective-permute-start.1 = (bf16[1,128,512]{2,1,0:T(8,128)(2,1)S(1)}, bf16[1,128,512]{2,1,0:T(8,128)(2,1)S(1)}, u32[]{:S(2)}, u32[]{:S(2)}) collective-permute-start(bf16[1,128,512]{2,1,0:T(8,128)(2,1)S(1)} %get-tuple-element.29), channel_id=1, source_target_pairs={{0,8},{4,12},{8,0},{12,4},{1,9},{5,13},{9,1},{13,5},{2,10},{6,14},... | collective-permute-start | bytes 393224 | tf_op jit(solution)/shard_map/ppermute | solution.py:292
  7.7 1.3 %collective-permute-start.2 = (bf16[1,128,512]{2,1,0:T(8,128)(2,1)S(1)}, bf16[1,128,512]{2,1,0:T(8,128)(2,1)S(1)}, u32[]{:S(2)}, u32[]{:S(2)}) collective-permute-start(bf16[1,128,512]{2,1,0:T(8,128)(2,1)S(1)} %get-tuple-element.30), channel_id=1, source_target_pairs={{0,12},{4,0},{8,4},{12,8},{1,13},{5,1},{9,5},{13,9},{2,14},{6,2},{... | collective-permute-start | bytes 393224 | tf_op jit(solution)/shard_map/ppermute | solution.py:292
  9.0 1.0 %copy-done = bf16[2,1,4,4,16,512]{5,4,3,2,1,0:T(8,128)(2,1)S(1)} copy-done((bf16[2,1,4,4,16,512]{5,4,3,2,1,0:T(8,128)(2,1)S(1)}, bf16[2,1,4,4,16,512]{5,4,3,2,1,0:T(8,128)(2,1)}, u32[]{:S(2)}) %copy-start) | copy-done | bytes 524312
  10.0 0.9 %copy-done.3 = bf16[4,2,128,128]{3,2,1,0:T(8,128)(2,1)S(1)} copy-done((bf16[4,2,128,128]{3,2,1,0:T(8,128)(2,1)S(1)}, bf16[4,2,128,128]{3,2,1,0:T(8,128)(2,1)}, u32[]{:S(2)}) %copy-start.3) | copy-done | bytes 262168
  11.0 0.8 %activation.1 = (bf16[4,256,256]{2,1,0:T(8,128)(2,1)S(1)}, bf16[4,256,256]{2,1,0:T(8,128)(2,1)S(1)}, f32[4,256,256]{2,1,0:T(8,128)S(1)}, bf16[4,256,256]{2,1,0:T(8,128)(2,1)S(1)}, bf16[4,256,256]{2,1,0:T(8,128)(2,1)S(1)}) custom-call(bf16[2,256,512]{2,1,0:T(8,128)(2,1)S(1)} %bitcast.3, bf16[4,2,128,128]{3,2,1,0:T(8,128)(2,1)S(1)} %copy-done.2, ...), custom_call_target="tpu_custom_call" | custom-call | tf_op jit(solution)/shard_map/activation/pallas_call | solution.py:276
  11.8 4.5 %collective-permute-done.1.refs_2_ = bf16[1,128,512]{2,1,0:T(8,128)(2,1)S(1)} collective-permute-done((bf16[1,128,512]{2,1,0:T(8,128)(2,1)S(1)}, bf16[1,128,512]{2,1,0:T(8,128)(2,1)S(1)}, u32[]{:S(2)}, u32[]{:S(2)}) %collective-permute-start.1) | collective-permute-done | bytes 131104 | tf_op jit(solution)/shard_map/ppermute | solution.py:292
  16.3 0.7 %filter.1 = (bf16[1,128,512]{2,1,0:T(8,128)(2,1)S(1)}, bf16[1,128,512]{2,1,0:T(8,128)(2,1)S(1)}, bf16[1,128,512]{2,1,0:T(8,128)(2,1)S(1)}, bf16[1,128,512]{2,1,0...) custom-call(bf16[1,128,512]{2,1,0:T(8,128)(2,1)S(1)} %get-tuple-element.27.refs_0_, ...), custom_call_target="tpu_custom_call" | custom-call | tf_op jit(solution)/shard_map/filter/pallas_call | solution.py:276
  17.1 2.3 %collective-permute-start.4 = (bf16[1,128,512]{2,1,0:T(8,128)(2,1)S(1)}, bf16[1,128,512]{2,1,0:T(8,128)(2,1)S(1)}, u32[]{:S(2)}, u32[]{:S(2)}) collective-permute-start(bf16[1,128,512]{2,1,0:T(8,128)(2,1)S(1)} %get-tuple-element.36), channel_id=1, source_target_pairs={{0,8},{4,12},{8,0},{12,4},{1,9},{5,13},{9,1},{13,5},{2,10},{6,14},... | collective-permute-start | bytes 393224 | tf_op jit(solution)/shard_map/ppermute | solution.py:292
  19.4 0.5 %weight.1 = (f32[4,64,512]{2,1,0:T(8,128)S(1)}, bf16[2,64,512]{2,1,0:T(8,128)(2,1)S(1)}, bf16[2,64,512]{2,1,0:T(8,128)(2,1)S(1)}) custom-call(bf16[4,256,256]{2,1,0:T(8,128)(2,1)S(1)} %get-tuple-element.38.act_ref, bf16[4,256,256]{2,1,0:T(8,128)(2,1)S(1)} %get-tuple-element.39.flip_ref, bf16[4,256,256]{2,1,0:T(8,128)(2,1)S(1)} %get-tuple-element.40.value_ref, ...), custom_call_target="tpu_custom_call" | custom-call | tf_op jit(solution)/shard_map/weight/pallas_call | solution.py:276
  19.9 1.6 %collective-permute-start.6 = (bf16[2,64,512]{2,1,0:T(8,128)(2,1)S(1)}, bf16[2,64,512]{2,1,0:T(8,128)(2,1)S(1)}, u32[]{:S(2)}, u32[]{:S(2)}) collective-permute-start(bf16[2,64,512]{2,1,0:T(8,128)(2,1)S(1)} %get-tuple-element.43), channel_id=1, source_target_pairs={{0,2},{2,0},{1,3},{3,1},{4,6},{6,4},{5,7},{7,5},{8,10},{10,8},{9,1... | collective-permute-start | bytes 393224 | tf_op jit(solution)/shard_map/ppermute | solution.py:367
  21.4 0.5 %collective-permute-start.8 = (bf16[2,64,512]{2,1,0:T(8,128)(2,1)S(1)}, bf16[2,64,512]{2,1,0:T(8,128)(2,1)S(1)}, u32[]{:S(2)}, u32[]{:S(2)}) collective-permute-start(bf16[2,64,512]{2,1,0:T(8,128)(2,1)S(1)} %get-tuple-element.46), channel_id=1, source_target_pairs={{0,2},{2,0},{1,3},{3,1},{4,6},{6,4},{5,7},{7,5},{8,10},{10,8},{9,1... | collective-permute-start | bytes 393224 | tf_op jit(solution)/shard_map/ppermute | solution.py:367
  21.9 2.6 %collective-permute-start.3 = (bf16[1,128,512]{2,1,0:T(8,128)(2,1)S(1)}, bf16[1,128,512]{2,1,0:T(8,128)(2,1)S(1)}, u32[]{:S(2)}, u32[]{:S(2)}) collective-permute-start(bf16[1,128,512]{2,1,0:T(8,128)(2,1)S(1)} %get-tuple-element.35), channel_id=1, source_target_pairs={{0,4},{4,8},{8,12},{12,0},{1,5},{5,9},{9,13},{13,1},{2,6},{6,10},{... | collective-permute-start | bytes 393224 | tf_op jit(solution)/shard_map/ppermute | solution.py:292
  24.6 1.2 %collective-permute-start.5 = (bf16[1,128,512]{2,1,0:T(8,128)(2,1)S(1)}, bf16[1,128,512]{2,1,0:T(8,128)(2,1)S(1)}, u32[]{:S(2)}, u32[]{:S(2)}) collective-permute-start(bf16[1,128,512]{2,1,0:T(8,128)(2,1)S(1)} %get-tuple-element.37), channel_id=1, source_target_pairs={{0,12},{4,0},{8,4},{12,8},{1,13},{5,1},{9,5},{13,9},{2,14},{6,2},{... | collective-permute-start | bytes 393224 | tf_op jit(solution)/shard_map/ppermute | solution.py:292
  25.8 0.5 %collective-permute-done.6.got_ref = bf16[2,64,512]{2,1,0:T(8,128)(2,1)S(1)} collective-permute-done((bf16[2,64,512]{2,1,0:T(8,128)(2,1)S(1)}, bf16[2,64,512]{2,1,0:T(8,128)(2,1)S(1)}, u32[]{:S(2)}, u32[]{:S(2)}) %collective-permute-start.6) | collective-permute-done | bytes 131104 | tf_op jit(solution)/shard_map/ppermute | solution.py:367
  26.4 1.8 %collective-permute-start.7 = (bf16[64,512]{1,0:T(8,128)(2,1)S(1)}, bf16[64,512]{1,0:T(8,128)(2,1)S(1)}, u32[]{:S(2)}, u32[]{:S(2)}) collective-permute-start(bf16[64,512]{1,0:T(8,128)(2,1)S(1)} %get-tuple-element.45), channel_id=1, source_target_pairs={{0,4},{4,12},{12,8},{8,0},{1,5},{5,13},{13,9},{9,1},{2,6},{6,14},{... | collective-permute-start | bytes 196616 | tf_op jit(solution)/shard_map/ppermute | solution.py:292
  28.2 3.2 %collective-permute-start.9 = (bf16[64,512]{1,0:T(8,128)(2,1)S(1)}, bf16[64,512]{1,0:T(8,128)(2,1)S(1)}, u32[]{:S(2)}, u32[]{:S(2)}) collective-permute-start(bf16[64,512]{1,0:T(8,128)(2,1)S(1)} %get-tuple-element.47), channel_id=1, source_target_pairs={{0,12},{4,8},{12,0},{8,4},{1,13},{5,9},{13,1},{9,5},{2,14},{6,10},... | collective-permute-start | bytes 196616 | tf_op jit(solution)/shard_map/ppermute | solution.py:292
  31.3 1.8 %collective-permute-start.10 = (bf16[64,512]{1,0:T(8,128)(2,1)S(1)}, bf16[64,512]{1,0:T(8,128)(2,1)S(1)}, u32[]{:S(2)}, u32[]{:S(2)}) collective-permute-start(bf16[64,512]{1,0:T(8,128)(2,1)S(1)} %get-tuple-element.48), channel_id=1, source_target_pairs={{0,8},{4,0},{12,4},{8,12},{1,9},{5,1},{13,5},{9,13},{2,10},{6,2},{... | collective-permute-start | bytes 196616 | tf_op jit(solution)/shard_map/ppermute | solution.py:292
  33.1 1.1 %inverse.1 = bf16[1,256,512]{2,1,0:T(8,128)(2,1)} custom-call(bf16[4,256,128]{2,1,0:T(8,128)(2,1)S(1)} %copy-done.4, bf16[1,128,512]{2,1,0:T(8,128)(2,1)S(1)} %get-tuple-element.34.refs_0_, bf16[1,128,512]{2,1,0:T(8,128)(2,1)S(1)} %collective-permute-done.3.refs_1_, bf16[1,128,512]{2,1,0:T(8,128)(2,1)S(1)} %collective-permute-done.4.refs_2_.refs_0_, ...), custom_call_target="tpu_custom_call" | custom-call | tf_op jit(solution)/shard_map/inverse/pallas_call | solution.py:276
  34.3 1.1 %collective-permute-done.7.refs_1_ = bf16[64,512]{1,0:T(8,128)(2,1)S(1)} collective-permute-done((bf16[64,512]{1,0:T(8,128)(2,1)S(1)}, bf16[64,512]{1,0:T(8,128)(2,1)S(1)}, u32[]{:S(2)}, u32[]{:S(2)}) %collective-permute-start.7) | collective-permute-done | bytes 65568 | tf_op jit(solution)/shard_map/ppermute | solution.py:292
  35.4 0.6 %collective-permute-done.10.refs_3_ = bf16[64,512]{1,0:T(8,128)(2,1)S(1)} collective-permute-done((bf16[64,512]{1,0:T(8,128)(2,1)S(1)}, bf16[64,512]{1,0:T(8,128)(2,1)S(1)}, u32[]{:S(2)}, u32[]{:S(2)}) %collective-permute-start.10) | collective-permute-done | bytes 65568 | tf_op jit(solution)/shard_map/ppermute | solution.py:292
  36.0 0.7 %last_sum.1 = (f32[4,2,16,128]{3,2,1,0:T(8,128)}, f32[4,2,16,128]{3,2,1,0:T(8,128)}) custom-call(f32[64,512]{1,0:T(8,128)S(1)} %get-tuple-element.44.refs_0_, bf16[64,512]{1,0:T(8,128)(2,1)S(1)} %collective-permute-done.7.refs_1_, bf16[64,512]{1,0:T(8,128)(2,1)S(1)} %collective-permute-done.9.refs_2_, bf16[64,512]{1,0:T(8,128)(2,1)S(1)} %collective-permute-done.10.refs_3_), custom_call_target="tpu_custom_call" | custom-call | tf_op jit(solution)/shard_map/last_sum/pallas_call | solution.py:276
  (18 shorter events, 0.1 us)
Async XLA Ops:
  0.6 1.0 %copy-start.1 = (bf16[1,1,16,16,512]{4,3,2,1,0:T(8,128)(2,1)S(1)}, bf16[1,1,16,16,512]{4,3,2,1,0:T(8,128)(2,1)}, u32[]{:S(2)}) copy-start(bf16[1,1,16,16,512]{4,3,2,1,0:T(8,128)(2,1)} %param.6) | copy-start | bytes 786436
  1.6 7.4 %copy-start.2 = (bf16[4,2,128,128]{3,2,1,0:T(8,128)(2,1)S(1)}, bf16[4,2,128,128]{3,2,1,0:T(8,128)(2,1)}, u32[]{:S(2)}) copy-start(bf16[4,2,128,128]{3,2,1,0:T(8,128)(2,1)} %first_ref.1) | copy-start | bytes 786436
  2.0 9.8 %collective-permute-start = (bf16[1,128,512]{2,1,0:T(8,128)(2,1)S(1)}, bf16[1,128,512]{2,1,0:T(8,128)(2,1)S(1)}, u32[]{:S(2)}, u32[]{:S(2)}) collective-permute-start(bf16[1,128,512]{2,1,0:T(8,128)(2,1)S(1)} %get-tuple-element.28), channel_id=1, source_target_pairs={{0,4},{4,8},{8,12},{12,0},{1,5},{5,9},{9,13},{13,1},{2,6},{6,10},{... | collective-permute-start | bytes 393224 | tf_op jit(solution)/shard_map/ppermute | solution.py:292
  5.1 3.9 %copy-start.5 = (bf16[2,512]{1,0:T(2,128)(2,1)S(1)}, bf16[2,512]{1,0:T(2,128)(2,1)}, u32[]{:S(2)}) copy-start(bf16[2,512]{1,0:T(2,128)(2,1)} %bias_ref.1) | copy-start | bytes 6148
  5.1 11.2 %collective-permute-start.1 = (bf16[1,128,512]{2,1,0:T(8,128)(2,1)S(1)}, bf16[1,128,512]{2,1,0:T(8,128)(2,1)S(1)}, u32[]{:S(2)}, u32[]{:S(2)}) collective-permute-start(bf16[1,128,512]{2,1,0:T(8,128)(2,1)S(1)} %get-tuple-element.29), channel_id=1, source_target_pairs={{0,8},{4,12},{8,0},{12,4},{1,9},{5,13},{9,1},{13,5},{2,10},{6,14},... | collective-permute-start | bytes 393224 | tf_op jit(solution)/shard_map/ppermute | solution.py:292
  7.7 8.6 %collective-permute-start.2 = (bf16[1,128,512]{2,1,0:T(8,128)(2,1)S(1)}, bf16[1,128,512]{2,1,0:T(8,128)(2,1)S(1)}, u32[]{:S(2)}, u32[]{:S(2)}) collective-permute-start(bf16[1,128,512]{2,1,0:T(8,128)(2,1)S(1)} %get-tuple-element.30), channel_id=1, source_target_pairs={{0,12},{4,0},{8,4},{12,8},{1,13},{5,1},{9,5},{13,9},{2,14},{6,2},{... | collective-permute-start | bytes 393224 | tf_op jit(solution)/shard_map/ppermute | solution.py:292
  9.0 1.0 %copy-start = (bf16[2,1,4,4,16,512]{5,4,3,2,1,0:T(8,128)(2,1)S(1)}, bf16[2,1,4,4,16,512]{5,4,3,2,1,0:T(8,128)(2,1)}, u32[]{:S(2)}) copy-start(bf16[2,1,4,4,16,512]{5,4,3,2,1,0:T(8,128)(2,1)} %param.7) | copy-start | bytes 1572868
  10.0 0.9 %copy-start.3 = (bf16[4,2,128,128]{3,2,1,0:T(8,128)(2,1)S(1)}, bf16[4,2,128,128]{3,2,1,0:T(8,128)(2,1)}, u32[]{:S(2)}) copy-start(bf16[4,2,128,128]{3,2,1,0:T(8,128)(2,1)} %second_ref.1) | copy-start | bytes 786436
  17.1 8.7 %collective-permute-start.4 = (bf16[1,128,512]{2,1,0:T(8,128)(2,1)S(1)}, bf16[1,128,512]{2,1,0:T(8,128)(2,1)S(1)}, u32[]{:S(2)}, u32[]{:S(2)}) collective-permute-start(bf16[1,128,512]{2,1,0:T(8,128)(2,1)S(1)} %get-tuple-element.36), channel_id=1, source_target_pairs={{0,8},{4,12},{8,0},{12,4},{1,9},{5,13},{9,1},{13,5},{2,10},{6,14},... | collective-permute-start | bytes 393224 | tf_op jit(solution)/shard_map/ppermute | solution.py:292
  19.9 6.5 %collective-permute-start.6 = (bf16[2,64,512]{2,1,0:T(8,128)(2,1)S(1)}, bf16[2,64,512]{2,1,0:T(8,128)(2,1)S(1)}, u32[]{:S(2)}, u32[]{:S(2)}) collective-permute-start(bf16[2,64,512]{2,1,0:T(8,128)(2,1)S(1)} %get-tuple-element.43), channel_id=1, source_target_pairs={{0,2},{2,0},{1,3},{3,1},{4,6},{6,4},{5,7},{7,5},{8,10},{10,8},{9,1... | collective-permute-start | bytes 393224 | tf_op jit(solution)/shard_map/ppermute | solution.py:367
  21.4 6.7 %collective-permute-start.8 = (bf16[2,64,512]{2,1,0:T(8,128)(2,1)S(1)}, bf16[2,64,512]{2,1,0:T(8,128)(2,1)S(1)}, u32[]{:S(2)}, u32[]{:S(2)}) collective-permute-start(bf16[2,64,512]{2,1,0:T(8,128)(2,1)S(1)} %get-tuple-element.46), channel_id=1, source_target_pairs={{0,2},{2,0},{1,3},{3,1},{4,6},{6,4},{5,7},{7,5},{8,10},{10,8},{9,1... | collective-permute-start | bytes 393224 | tf_op jit(solution)/shard_map/ppermute | solution.py:367
  21.9 11.2 %collective-permute-start.3 = (bf16[1,128,512]{2,1,0:T(8,128)(2,1)S(1)}, bf16[1,128,512]{2,1,0:T(8,128)(2,1)S(1)}, u32[]{:S(2)}, u32[]{:S(2)}) collective-permute-start(bf16[1,128,512]{2,1,0:T(8,128)(2,1)S(1)} %get-tuple-element.35), channel_id=1, source_target_pairs={{0,4},{4,8},{8,12},{12,0},{1,5},{5,9},{9,13},{13,1},{2,6},{6,10},{... | collective-permute-start | bytes 393224 | tf_op jit(solution)/shard_map/ppermute | solution.py:292
  24.6 8.5 %collective-permute-start.5 = (bf16[1,128,512]{2,1,0:T(8,128)(2,1)S(1)}, bf16[1,128,512]{2,1,0:T(8,128)(2,1)S(1)}, u32[]{:S(2)}, u32[]{:S(2)}) collective-permute-start(bf16[1,128,512]{2,1,0:T(8,128)(2,1)S(1)} %get-tuple-element.37), channel_id=1, source_target_pairs={{0,12},{4,0},{8,4},{12,8},{1,13},{5,1},{9,5},{13,9},{2,14},{6,2},{... | collective-permute-start | bytes 393224 | tf_op jit(solution)/shard_map/ppermute | solution.py:292
  26.3 6.8 %copy-start.4 = (bf16[4,256,128]{2,1,0:T(8,128)(2,1)S(1)}, bf16[4,256,128]{2,1,0:T(8,128)(2,1)}, u32[]{:S(2)}) copy-start(bf16[4,256,128]{2,1,0:T(8,128)(2,1)} %constant.2.clone.table_ref) | copy-start | bytes 786436
  26.4 9.0 %collective-permute-start.7 = (bf16[64,512]{1,0:T(8,128)(2,1)S(1)}, bf16[64,512]{1,0:T(8,128)(2,1)S(1)}, u32[]{:S(2)}, u32[]{:S(2)}) collective-permute-start(bf16[64,512]{1,0:T(8,128)(2,1)S(1)} %get-tuple-element.45), channel_id=1, source_target_pairs={{0,4},{4,12},{12,8},{8,0},{1,5},{5,13},{13,9},{9,1},{2,6},{6,14},{... | collective-permute-start | bytes 196616 | tf_op jit(solution)/shard_map/ppermute | solution.py:292
  28.2 7.2 %collective-permute-start.9 = (bf16[64,512]{1,0:T(8,128)(2,1)S(1)}, bf16[64,512]{1,0:T(8,128)(2,1)S(1)}, u32[]{:S(2)}, u32[]{:S(2)}) collective-permute-start(bf16[64,512]{1,0:T(8,128)(2,1)S(1)} %get-tuple-element.47), channel_id=1, source_target_pairs={{0,12},{4,8},{12,0},{8,4},{1,13},{5,9},{13,1},{9,5},{2,14},{6,10},... | collective-permute-start | bytes 196616 | tf_op jit(solution)/shard_map/ppermute | solution.py:292
  31.3 4.6 %collective-permute-start.10 = (bf16[64,512]{1,0:T(8,128)(2,1)S(1)}, bf16[64,512]{1,0:T(8,128)(2,1)S(1)}, u32[]{:S(2)}, u32[]{:S(2)}) collective-permute-start(bf16[64,512]{1,0:T(8,128)(2,1)S(1)} %get-tuple-element.48), channel_id=1, source_target_pairs={{0,8},{4,0},{12,4},{8,12},{1,9},{5,1},{13,5},{9,13},{2,10},{6,2},{... | collective-permute-start | bytes 196616 | tf_op jit(solution)/shard_map/ppermute | solution.py:292
